TPU v7x, 32 devices: a whole 2x2x4 slice. The times are simulated.
32 devices in a mesh: ctx: 4 (over y, x), exp: 4 (over z), fsdp: 2 (over core).
Axes of the slice: x: 2, y: 2, z: 4, core: 2. Of those that a mesh axis runs over, the one named last changes fastest.
Arguments:
- hidden_in: bfloat16 [16, 2, 128, 768], P(('exp', 'fsdp'), None, 'ctx'), may hold values from -6 to 6
- seq_lengths: int32 [16], P(('exp', 'fsdp')), may hold values from 64 to 256, as said below
- expert_ids: int32 [16, 2, 128, 2], P(('exp', 'fsdp'), None, 'ctx'), may hold values from 0 to 15, all different within a row
- route_rank: int32 [8, 4, 128], P(('exp', 'fsdp'), 'ctx'), may hold values from 0 to 127, each once within a row
- gain_attn: bfloat16 [768], P(('ctx', 'exp', 'fsdp')), may hold values from 0.5 to 1.5
- w_qkv: bfloat16 [768, 2304], P(('ctx', 'exp', 'fsdp')), may hold values from -0.21875 to 0.21875
- w_out: bfloat16 [768, 768], P(('ctx', 'exp', 'fsdp')), may hold values from -3.5 to 3.5
- w_router: bfloat16 [768, 16], P(('ctx', 'exp', 'fsdp')), may hold values from -0.125 to 0.125
- gain_ffn: bfloat16 [768], P(('ctx', 'exp', 'fsdp')), may hold values from 0.5 to 1.5
- w_gate_up: bfloat16 [768, 4096], P(('ctx', 'exp', 'fsdp')), may hold values from -0.21875 to 0.21875
- w_shared_down: bfloat16 [2048, 768], P(('ctx', 'exp', 'fsdp')), may hold values from -0.125 to 0.125
- w_experts_in: bfloat16 [16, 768, 4096], P('exp', ('ctx', 'fsdp')), may hold values from -0.21875 to 0.21875
- w_experts_out: bfloat16 [16, 2048, 768], P('exp', ('ctx', 'fsdp')), may hold values from -0.125 to 0.125
- grad_output: bfloat16 [16, 2, 128, 768], P(('exp', 'fsdp'), None, 'ctx'), may hold values from -6 to 6
Outputs:
- layer_out: bfloat16 [16, 2, 128, 768], P(('exp', 'fsdp'), None, 'ctx')
- grad_input: float32 [16, 2, 128, 768], P(('exp', 'fsdp'), None, 'ctx')
- grad_gain_attn: float32 [768], P(('ctx', 'exp', 'fsdp'))
- grad_w_qkv: float32 [768, 2304], P(('ctx', 'exp', 'fsdp'))
- grad_w_out: float32 [768, 768], P(('ctx', 'exp', 'fsdp'))
- grad_w_router: float32 [768, 16], P(('ctx', 'exp', 'fsdp'))
- grad_gain_ffn: float32 [768], P(('ctx', 'exp', 'fsdp'))
- grad_w_gate_up: float32 [768, 4096], P(('ctx', 'exp', 'fsdp'))
- grad_w_shared_down: float32 [2048, 768], P(('ctx', 'exp', 'fsdp'))
- grad_w_experts_in: float32 [16, 768, 4096], P('exp', ('ctx', 'fsdp'))
- grad_w_experts_out: float32 [16, 2048, 768], P('exp', ('ctx', 'fsdp'))
Inputs may be any that keep to these rules, and one draw needn't show every extreme that they name: `seq_lengths`: of each 2 consecutive sequences, one has length exactly 256. `expert_ids`: the 2 experts of a slot differ. `route_rank`: each row of 128 entries holds every rank once.
All inputs are finite; a program needn't handle non-finite values.
Results may differ from a plain program's by a relative error of at most 0.015.
Values may be sent and summed in bfloat16 or wider, within the bound.
A program may use at most 256 MiB of HBM per device.

v0:
```python
import jax
import jax.numpy as jnp
from jax import lax
from jax.sharding import PartitionSpec as P

HS = 64
CAP = 18


epsilon = 1e-06
masked_out = -1e30
highest = lax.Precision.HIGHEST


def rms_norm(values_in, gain_row):
    return (
        values_in
        * lax.rsqrt(jnp.mean(values_in * values_in, axis=-1, keepdims=True) + epsilon)
        * gain_row
    )


def rope_tables(places):
    half_size = HS // 2
    frequency = 10000.0 ** (-jnp.arange(half_size, dtype=jnp.float32) * 2.0 / HS)
    angles = places.astype(jnp.float32)[:, None] * frequency[None, :]
    return (jnp.cos(angles), jnp.sin(angles))


def rotate(values_in, cosines, sine_rows):
    half_size = values_in.shape[-1] // 2
    leading = values_in[..., :half_size]
    trailing = values_in[..., half_size:]
    cos_rows = cosines[:, None, :]
    sin_rows = sine_rows[:, None, :]
    return jnp.concatenate(
        [leading * cos_rows - trailing * sin_rows, leading * sin_rows + trailing * cos_rows],
        axis=-1,
    )


def swiglu(merged_rows):
    gate_part, up_part = jnp.split(merged_rows, 2, axis=-1)
    return jax.nn.silu(gate_part) * up_part


def first_t(left_side, right_side, precision=None):
    return lax.dot_general(
        left_side,
        right_side,
        (((0,), (0,)), ((), ())),
        precision=precision,
        preferred_element_type=jnp.float32,
    )


def second_t(left_side, right_side, precision=None):
    return lax.dot_general(
        left_side,
        right_side,
        (((1,), (1,)), ((), ())),
        precision=precision,
        preferred_element_type=jnp.float32,
    )


def per_device(
    hidden_in,
    seq_lengths,
    expert_ids,
    route_rank,
    gain_attn,
    w_qkv,
    w_out,
    w_router,
    gain_ffn,
    w_gate_up,
    w_shared_down,
    w_experts_in,
    w_experts_out,
    grad_output,
):
    num_seqs, two_ends, half_len, model_width = hidden_in.shape
    shard_len = 2 * half_len
    tok_count = num_seqs * shard_len
    num_heads = model_width // HS
    score_scale = HS ** (-0.5)
    ctx_size = lax.axis_size("ctx")
    full_len = shard_len * ctx_size
    whole_half = half_len * ctx_size
    gain_one, wqkv_all, wout_all, router_all, gain_two, shared_in, shared_down = (
        lax.all_gather(gain_attn, ("ctx", "exp", "fsdp"), axis=0, tiled=True),
        lax.all_gather(w_qkv, ("ctx", "exp", "fsdp"), axis=0, tiled=True),
        lax.all_gather(w_out, ("ctx", "exp", "fsdp"), axis=0, tiled=True),
        lax.all_gather(w_router, ("ctx", "exp", "fsdp"), axis=0, tiled=True),
        lax.all_gather(gain_ffn, ("ctx", "exp", "fsdp"), axis=0, tiled=True),
        lax.all_gather(w_gate_up, ("ctx", "exp", "fsdp"), axis=0, tiled=True),
        lax.all_gather(w_shared_down, ("ctx", "exp", "fsdp"), axis=0, tiled=True),
    )
    experts_in, experts_out = (
        lax.all_gather(w_experts_in, ("ctx", "fsdp"), axis=1, tiled=True),
        lax.all_gather(w_experts_out, ("ctx", "fsdp"), axis=1, tiled=True),
    )
    lower_places = lax.axis_index("ctx") * half_len + jnp.arange(half_len, dtype=jnp.int32)
    places = jnp.concatenate([lower_places, full_len - 1 - lower_places])
    whole_range = jnp.arange(whole_half, dtype=jnp.int32)
    full_places = jnp.concatenate([whole_range, full_len - 1 - whole_range])
    live_mask = (places[None, :] < seq_lengths[:, None]).astype(jnp.float32)
    live_rows = live_mask.reshape(tok_count, 1)
    inputs_f = hidden_in.astype(jnp.float32).reshape(tok_count, model_width)
    gain_attn_f = gain_one.astype(jnp.float32)
    normed_b = rms_norm(inputs_f, gain_attn_f).astype(jnp.bfloat16)
    qkv_merged = jnp.dot(normed_b, wqkv_all, preferred_element_type=jnp.float32).reshape(
        num_seqs, shard_len, 3, num_heads, HS
    )
    cosines, sine_rows = rope_tables(places)
    queries = rotate(qkv_merged[:, :, 0], cosines, sine_rows).astype(jnp.bfloat16)
    keys_local = rotate(qkv_merged[:, :, 1], cosines, sine_rows).astype(jnp.bfloat16)
    values_local = qkv_merged[:, :, 2].astype(jnp.bfloat16)
    end_shape = (num_seqs, 2, half_len, model_width)
    keys_full, values_full = (
        lax.all_gather(keys_local.reshape(end_shape), "ctx", axis=2, tiled=True),
        lax.all_gather(values_local.reshape(end_shape), "ctx", axis=2, tiled=True),
    )
    keys_full = keys_full.reshape(num_seqs, full_len, num_heads, HS)
    values_full = values_full.reshape(num_seqs, full_len, num_heads, HS)
    stat_shape = (num_seqs, num_heads, shard_len)
    block_range = jnp.arange(ctx_size, dtype=jnp.int32)

    def block_scores(query_rows, query_places, key_rows, key_places):
        scores = (
            jnp.einsum("bqhd,bkhd->bhqk", query_rows, key_rows, preferred_element_type=jnp.float32)
            * score_scale
        )
        allowed = (key_places[None, None, :] <= query_places[None, :, None]) & (
            key_places[None, None, :] < seq_lengths[:, None, None]
        )
        return jnp.where(allowed[:, None], scores, masked_out)

    def key_block(block_idx):
        offset = block_idx * shard_len
        return (
            lax.dynamic_slice_in_dim(keys_full, offset, shard_len, 1),
            lax.dynamic_slice_in_dim(values_full, offset, shard_len, 1),
            lax.dynamic_slice_in_dim(full_places, offset, shard_len, 0),
        )

    def lse_step(state_in, block_idx):
        run_max, run_sum = state_in
        key_rows, value_rows, key_places = key_block(block_idx)
        scores = block_scores(queries, places, key_rows, key_places)
        new_max = jnp.maximum(run_max, jnp.max(scores, axis=-1))
        run_sum = run_sum * jnp.exp(run_max - new_max) + jnp.sum(
            jnp.exp(scores - new_max[..., None]), axis=-1
        )
        return ((new_max, run_sum), None)

    (row_max, row_sum), unused = lax.scan(
        lse_step,
        (jnp.full(stat_shape, masked_out, jnp.float32), jnp.zeros(stat_shape, jnp.float32)),
        block_range,
    )
    log_total = row_max + jnp.log(row_sum)

    def context_step(running, block_idx):
        key_rows, value_rows, key_places = key_block(block_idx)
        prob_rows = jnp.exp(
            block_scores(queries, places, key_rows, key_places) - log_total[..., None]
        ).astype(jnp.bfloat16)
        return (
            running
            + jnp.einsum(
                "bhqk,bkhd->bqhd", prob_rows, value_rows, preferred_element_type=jnp.float32
            ),
            None,
        )

    context, unused = lax.scan(
        context_step, jnp.zeros((num_seqs, shard_len, num_heads, HS), jnp.float32), block_range
    )
    context_b = context.reshape(tok_count, model_width).astype(jnp.bfloat16)
    attended = inputs_f + jnp.dot(context_b, wout_all, preferred_element_type=jnp.float32)
    gain_ffn_f = gain_two.astype(jnp.float32)
    normed_two = rms_norm(attended, gain_ffn_f).astype(jnp.bfloat16)
    logits = jnp.dot(normed_two, router_all, preferred_element_type=jnp.float32)
    num_experts = router_all.shape[1]
    expert_range = jnp.arange(num_experts, dtype=jnp.int32)
    picked_ids = expert_ids.reshape(tok_count, 2)
    pick_hot = (picked_ids[:, :, None] == expert_range).astype(jnp.float32)
    chosen = jnp.sum(pick_hot * logits[:, None, :], axis=-1)
    gate_probs = jax.nn.softmax(chosen, axis=-1)
    expert_load = (jnp.sum(pick_hot, axis=1) * live_rows).astype(jnp.bfloat16)
    rank_rows = route_rank.reshape(tok_count)
    earlier = (rank_rows[None, :] < rank_rows[:, None]).astype(jnp.bfloat16)
    position = jnp.dot(earlier, expert_load, preferred_element_type=jnp.float32)
    chosen_pos = jnp.sum(pick_hot * position[:, None, :], axis=-1)
    kept_mask = live_rows * (chosen_pos < CAP).astype(jnp.float32)
    slot_hot = (chosen_pos[:, :, None] == jnp.arange(CAP, dtype=jnp.float32)).astype(jnp.float32)
    dispatch = (
        (pick_hot[:, :, :, None] * slot_hot[:, :, None, :] * kept_mask[:, :, None, None])
        .reshape(tok_count, 2, num_experts * CAP)
        .astype(jnp.bfloat16)
    )
    dispatch_any = dispatch[:, 0] + dispatch[:, 1]
    exp_size = lax.axis_size("exp")
    per_owner = num_experts // exp_size
    send_rows = (
        first_t(dispatch_any, normed_two)
        .astype(jnp.bfloat16)
        .reshape(exp_size, per_owner, CAP, model_width)
    )
    arrived = lax.all_to_all(send_rows, "exp", split_axis=0, concat_axis=0, tiled=True)
    expert_merged = jnp.einsum(
        "secd,edf->secf", arrived, experts_in, preferred_element_type=jnp.float32
    )
    expert_hidden = swiglu(expert_merged).astype(jnp.bfloat16)
    expert_result = jnp.einsum(
        "secf,efd->secd", expert_hidden, experts_out, preferred_element_type=jnp.float32
    ).astype(jnp.bfloat16)
    returned = lax.all_to_all(
        expert_result, "exp", split_axis=0, concat_axis=0, tiled=True
    ).reshape(num_experts * CAP, model_width)
    routed = jnp.einsum("tks,sd->tkd", dispatch, returned, preferred_element_type=jnp.float32)
    mixture = jnp.sum(gate_probs[:, :, None] * routed, axis=1)
    shared_merged = jnp.dot(normed_two, shared_in, preferred_element_type=jnp.float32)
    shared_hidden = swiglu(shared_merged).astype(jnp.bfloat16)
    shared_result = jnp.dot(shared_hidden, shared_down, preferred_element_type=jnp.float32)
    layer_out = (
        (live_rows * (attended + mixture + shared_result)).reshape(end_shape).astype(jnp.bfloat16)
    )
    upstream = grad_output.astype(jnp.float32).reshape(tok_count, model_width) * live_rows
    upstream_b = upstream.astype(jnp.bfloat16)
    upstream_f = upstream_b.astype(jnp.float32)
    d_shared_down = first_t(shared_hidden, upstream_b)
    d_shared_hidden = second_t(upstream_b, shared_down)
    unused, swiglu_pull = jax.vjp(swiglu, shared_merged)
    d_shared_merged = swiglu_pull(d_shared_hidden)[0].astype(jnp.bfloat16)
    d_shared_in = first_t(normed_two, d_shared_merged)
    d_normed_two = second_t(d_shared_merged, shared_in)
    gate_grads = jnp.sum(routed * upstream_f[:, None, :], axis=-1)
    weighted = (gate_probs[:, :, None] * upstream_f[:, None, :]).astype(jnp.bfloat16)
    d_returned = (
        jnp.einsum("tks,tkd->sd", dispatch, weighted, preferred_element_type=jnp.float32)
        .astype(jnp.bfloat16)
        .reshape(exp_size, per_owner, CAP, model_width)
    )
    d_result = lax.all_to_all(d_returned, "exp", split_axis=0, concat_axis=0, tiled=True)
    d_experts_out = jnp.einsum(
        "secf,secd->efd", expert_hidden, d_result, preferred_element_type=jnp.float32
    )
    d_expert_hidden = jnp.einsum(
        "secd,efd->secf", d_result, experts_out, preferred_element_type=jnp.float32
    )
    unused, expert_pull = jax.vjp(swiglu, expert_merged)
    d_expert_merged = expert_pull(d_expert_hidden)[0].astype(jnp.bfloat16)
    d_experts_in = jnp.einsum(
        "secd,secf->edf", arrived, d_expert_merged, preferred_element_type=jnp.float32
    )
    d_arrived = jnp.einsum(
        "secf,edf->secd", d_expert_merged, experts_in, preferred_element_type=jnp.float32
    ).astype(jnp.bfloat16)
    d_sent = lax.all_to_all(d_arrived, "exp", split_axis=0, concat_axis=0, tiled=True).reshape(
        num_experts * CAP, model_width
    )
    d_normed_two = d_normed_two + jnp.dot(dispatch_any, d_sent, preferred_element_type=jnp.float32)
    unused, gate_pull = jax.vjp(lambda chosen_in: jax.nn.softmax(chosen_in, axis=-1), chosen)
    d_chosen = gate_pull(gate_grads)[0]
    d_logits = jnp.sum(pick_hot * d_chosen[:, :, None], axis=1)
    d_router = first_t(normed_two.astype(jnp.float32), d_logits, highest)
    d_normed_two = d_normed_two + second_t(d_logits, router_all.astype(jnp.float32), highest)
    unused, second_pull = jax.vjp(rms_norm, attended, gain_ffn_f)
    d_attended, d_gain_ffn = second_pull(d_normed_two)
    d_attended = d_attended + upstream
    d_attended_b = d_attended.astype(jnp.bfloat16)
    d_out_proj = first_t(context_b, d_attended_b)
    d_context = (
        second_t(d_attended_b, wout_all)
        .astype(jnp.bfloat16)
        .reshape(num_seqs, shard_len, num_heads, HS)
    )

    def score_grads(
        query_rows, query_places, key_rows, value_rows, key_places, d_rows, lse_rows, delta_rows
    ):
        prob_rows = jnp.exp(
            block_scores(query_rows, query_places, key_rows, key_places) - lse_rows[..., None]
        )
        d_probs = jnp.einsum(
            "bqhd,bkhd->bhqk", d_rows, value_rows, preferred_element_type=jnp.float32
        )
        d_scores = (prob_rows * (d_probs - delta_rows[..., None])).astype(jnp.bfloat16)
        return (prob_rows.astype(jnp.bfloat16), d_scores)

    def delta_step(running, block_idx):
        key_rows, value_rows, key_places = key_block(block_idx)
        prob_rows = jnp.exp(
            block_scores(queries, places, key_rows, key_places) - log_total[..., None]
        )
        d_probs = jnp.einsum(
            "bqhd,bkhd->bhqk", d_context, value_rows, preferred_element_type=jnp.float32
        )
        return (running + jnp.sum(prob_rows * d_probs, axis=-1), None)

    row_delta, unused = lax.scan(delta_step, jnp.zeros(stat_shape, jnp.float32), block_range)
    head_shape = (num_seqs, shard_len, num_heads, HS)

    def query_step(d_query, block_idx):
        key_rows, value_rows, key_places = key_block(block_idx)
        prob_b, d_scores = score_grads(
            queries, places, key_rows, value_rows, key_places, d_context, log_total, row_delta
        )
        return (
            d_query
            + jnp.einsum("bhqk,bkhd->bqhd", d_scores, key_rows, preferred_element_type=jnp.float32)
            * score_scale,
            None,
        )

    d_query, unused = lax.scan(query_step, jnp.zeros(head_shape, jnp.float32), block_range)
    query_all, d_context_all = (
        lax.all_gather(queries.reshape(end_shape), "ctx", axis=2, tiled=True),
        lax.all_gather(d_context.reshape(end_shape), "ctx", axis=2, tiled=True),
    )
    stat_ends = (num_seqs, num_heads, 2, half_len)
    lse_all, delta_all = (
        lax.all_gather(log_total.reshape(stat_ends), "ctx", axis=3, tiled=True),
        lax.all_gather(row_delta.reshape(stat_ends), "ctx", axis=3, tiled=True),
    )
    query_all = query_all.reshape(num_seqs, full_len, num_heads, HS)
    d_context_all = d_context_all.reshape(num_seqs, full_len, num_heads, HS)
    lse_all = lse_all.reshape(num_seqs, num_heads, full_len)
    delta_all = delta_all.reshape(num_seqs, num_heads, full_len)

    def owner_step(state_in, block_idx):
        d_keys, d_values = state_in
        offset = block_idx * shard_len
        query_rows = lax.dynamic_slice_in_dim(query_all, offset, shard_len, 1)
        d_rows = lax.dynamic_slice_in_dim(d_context_all, offset, shard_len, 1)
        lse_rows = lax.dynamic_slice_in_dim(lse_all, offset, shard_len, 2)
        delta_rows = lax.dynamic_slice_in_dim(delta_all, offset, shard_len, 2)
        query_places = lax.dynamic_slice_in_dim(full_places, offset, shard_len, 0)
        prob_b, d_scores = score_grads(
            query_rows, query_places, keys_local, values_local, places, d_rows, lse_rows, delta_rows
        )
        d_keys = (
            d_keys
            + jnp.einsum(
                "bhqk,bqhd->bkhd", d_scores, query_rows, preferred_element_type=jnp.float32
            )
            * score_scale
        )
        d_values = d_values + jnp.einsum(
            "bhqk,bqhd->bkhd", prob_b, d_rows, preferred_element_type=jnp.float32
        )
        return ((d_keys, d_values), None)

    (d_keys_local, d_values_local), unused = lax.scan(
        owner_step,
        (jnp.zeros(head_shape, jnp.float32), jnp.zeros(head_shape, jnp.float32)),
        block_range,
    )
    unused, rope_pull = jax.vjp(
        lambda rows_in: rotate(rows_in, cosines, sine_rows), qkv_merged[:, :, 0]
    )
    d_query_pre = rope_pull(d_query)[0]
    d_key_pre = rope_pull(d_keys_local)[0]
    d_qkv_merged = (
        jnp.stack([d_query_pre, d_key_pre, d_values_local], axis=2)
        .reshape(tok_count, 3 * model_width)
        .astype(jnp.bfloat16)
    )
    d_qkv = first_t(normed_b, d_qkv_merged)
    d_normed = second_t(d_qkv_merged, wqkv_all)
    unused, first_pull = jax.vjp(rms_norm, inputs_f, gain_attn_f)
    d_inputs, d_gain_attn = first_pull(d_normed)
    grad_input = (d_attended + d_inputs).reshape(end_shape)
    dense_sums = (
        lax.psum_scatter(d_gain_attn, ("ctx", "exp", "fsdp"), scatter_dimension=0, tiled=True),
        lax.psum_scatter(d_qkv, ("ctx", "exp", "fsdp"), scatter_dimension=0, tiled=True),
        lax.psum_scatter(d_out_proj, ("ctx", "exp", "fsdp"), scatter_dimension=0, tiled=True),
        lax.psum_scatter(d_router, ("ctx", "exp", "fsdp"), scatter_dimension=0, tiled=True),
        lax.psum_scatter(d_gain_ffn, ("ctx", "exp", "fsdp"), scatter_dimension=0, tiled=True),
        lax.psum_scatter(d_shared_in, ("ctx", "exp", "fsdp"), scatter_dimension=0, tiled=True),
        lax.psum_scatter(d_shared_down, ("ctx", "exp", "fsdp"), scatter_dimension=0, tiled=True),
    )
    expert_sums = (
        lax.psum_scatter(
            d_experts_in.astype(jnp.bfloat16), ("ctx", "fsdp"), scatter_dimension=1, tiled=True
        ).astype(jnp.float32),
        lax.psum_scatter(
            d_experts_out.astype(jnp.bfloat16), ("ctx", "fsdp"), scatter_dimension=1, tiled=True
        ).astype(jnp.float32),
    )
    return (
        layer_out,
        grad_input,
        dense_sums[0],
        dense_sums[1],
        dense_sums[2],
        dense_sums[3],
        dense_sums[4],
        dense_sums[5],
        dense_sums[6],
        expert_sums[0],
        expert_sums[1],
    )


def solution(mesh):
    return jax.shard_map(
        per_device,
        mesh=mesh,
        in_specs=(
            P(("exp", "fsdp"), None, "ctx", None),
            P(("exp", "fsdp")),
            P(("exp", "fsdp"), None, "ctx", None),
            P(("exp", "fsdp"), "ctx", None),
            P(("ctx", "exp", "fsdp")),
            P(("ctx", "exp", "fsdp"), None),
            P(("ctx", "exp", "fsdp"), None),
            P(("ctx", "exp", "fsdp"), None),
            P(("ctx", "exp", "fsdp")),
            P(("ctx", "exp", "fsdp"), None),
            P(("ctx", "exp", "fsdp"), None),
            P("exp", ("ctx", "fsdp"), None),
            P("exp", ("ctx", "fsdp"), None),
            P(("exp", "fsdp"), None, "ctx", None),
        ),
        out_specs=(
            P(("exp", "fsdp"), None, "ctx", None),
            P(("exp", "fsdp"), None, "ctx", None),
            P(("ctx", "exp", "fsdp")),
            P(("ctx", "exp", "fsdp"), None),
            P(("ctx", "exp", "fsdp"), None),
            P(("ctx", "exp", "fsdp"), None),
            P(("ctx", "exp", "fsdp")),
            P(("ctx", "exp", "fsdp"), None),
            P(("ctx", "exp", "fsdp"), None),
            P("exp", ("ctx", "fsdp"), None),
            P("exp", ("ctx", "fsdp"), None),
        ),
        check_vma=False,
    )
```

profile of v0, /device:TPU:31, one launch (start us, length us, event | category | flops | bytes accessed | tf_op | source)
XLA Modules:
  0.0 1241.0 jit_solution(10594759753018058192)
XLA Ops:
  13.9 38.3 %all-reduce.10 = (bf16[768]{0:T(1024)(128)(2,1)S(1)}, bf16[768]{0:T(1024)(128)(2,1)S(1)}) all-reduce(bf16[768]{0:T(1024)(128)(2,1)S(1)} %dynamic-update-slice, bf16[768]{0:T(1024)(128)(2,1)S(1)} %dynamic-update-slice.1), channel_id=1, replica_groups=mesh['ctx'=4,'exp'=4,'fsdp'=2] {'ctx','exp','fsdp'}, use_global_device_ids=true, to_apply=%add.4 | all-reduce | flops 1536 | bytes 6144
  54.1 37.3 %all-gather = bf16[32,24,16]{1,2,0:T(8,128)(2,1)S(1)} all-gather(bf16[1,24,16]{1,2,0:T(8,128)(2,1)S(1)} %bitcast.284), channel_id=1, replica_groups=mesh['ctx'=4,'exp'=4,'fsdp'=2] {'ctx','exp','fsdp'}, dimensions={0}, use_global_device_ids=true | all-gather | bytes 25344 | tf_op jit(solution)/shard_map/all_gather | solution.py:95
  93.1 5.8 copy.177
  98.9 3.1 fusion.151
  106.5 11.4 all_gather.48
  119.9 10.7 all_gather.47
  134.0 23.5 %while.59 = (s32[]{:T(128)}, f32[2,12,64]{2,1,0:T(8,128)S(1)}, f32[2,12,64]{2,1,0:T(8,128)}, s32[4]{0:T(128)}, s32[256]{0:T(256)}, /*index=5*/s32[64]{0:T(128)},...) while((s32[]{:T(128)}, f32[2,12,64]{2,1,0:T(8,128)S(1)}, ...), condition=%wide.region_4.5_spmd.clone, body=%wide.region_1.4_spmd.clone.sunk | while | flops 13094535 | bytes 1687258 | solution.py:158
  159.3 24.3 %while.60 = (s32[]{:T(128)}, f32[2,64,12,64]{1,3,2,0:T(8,128)S(1)}, s32[4]{0:T(128)}, bf16[2,256,12,64]{1,3,2,0:T(8,128)(2,1)S(1)}, s32[256]{0:T(256)}, /*index=...) while((s32[]{:T(128)}, f32[2,64,12,64]{1,3,2,0:T(8,128)S(1)}, ...), condition=%wide.region_6.7_spmd.clone, body=%wide.region_5.6_spmd.clone.sunk | while | flops 25768072 | bytes 2403548 | solution.py:178
  184.4 2.2 multiply_reduce_fusion.4
  193.2 2.0 copy.190
  195.2 10.2 all-to-all-start
  211.6 2.1 fusion.94
  217.7 4.5 all-to-all-start.2
  222.4 32.9 %all-gather.12.cloned.1.call-done = bf16[4,768,4096]{2,1,0:T(8,128)(2,1)} async-done(((bf16[4,96,4096]{2,1,0:T(8,128)(2,1)}), bf16[4,768,4096]{2,1,0:T(8,128)(2,1)}) %all-gather.12.cloned.1.call-update) | async-done | bytes 25165840 | tf_op jit(solution)/shard_map/all_gather | solution.py:101
  255.3 15.0 %fusion.80 = f32[4,4,18,4096]{3,2,0,1:T(8,128)} fusion(bf16[4,768,4096]{2,1,0:T(8,128)(2,1)} %all-gather.12.cloned.1.call-done, bf16[4,4,18,768]{3,1,2,0:T(4,128)(2,1)S(1)} %all-to-all-done), kind=kOutput, calls=%fused_computation.109 | convolution fusion | flops 1811939328 | bytes 30326784 | tf_op jit(solution)/shard_map/secd,edf->secf/dot_general | solution.py:213
  270.3 58.9 %all-gather.14.cloned.1.call-done = bf16[4,2048,768]{2,1,0:T(8,128)(2,1)} async-done(((bf16[4,256,768]{2,1,0:T(8,128)(2,1)}), bf16[4,2048,768]{2,1,0:T(8,128)(2,1)}) %all-gather.14.cloned.1.call-update) | async-done | bytes 12582928 | tf_op jit(solution)/shard_map/all_gather | solution.py:102
  329.2 12.8 %fusion.85 = (bf16[4,4,18,2048]{3,2,0,1:T(8,128)(2,1)}, bf16[4,4,18,2048]{3,2,0,1:T(8,128)(2,1)}, bf16[4,4,18,2048]{3,2,0,1:T(8,128)(2,1)}) fusion(f32[4,4,18,4096]{3,2,0,1:T(8,128)} %fusion.80, bf16[4,2048,768]{2,1,0:T(8,128)(2,1)} %all-gather.14.cloned.1.call-done, bf16[4,4,18,768]{3,1,2,0:T(4,128)(2,1)} %all-to-all-done.2), kind=kOutput, calls=%fused_computation.113 | convolution fusion | flops 915406848 | bytes 21282816 | tf_op jit(solution)/shard_map/secd,efd->secf/dot_general | solution.py:251
  342.0 9.8 bitcast_convert_fusion.1
  352.1 13.8 %bitcast_convert_fusion = bf16[4,768,4096]{2,1,0:T(8,128)(2,1)} fusion(bf16[4,4,18,2048]{3,2,0,1:T(8,128)(2,1)} %get-tuple-element.890, bf16[4,4,18,2048]{3,2,0,1:T(8,128)(2,1)} %get-tuple-element.889, bf16[4,4,18,768]{3,1,2,0:T(4,128)(2,1)S(1)} %all-to-all-done), kind=kOutput, calls=%fused_computation.99 | convolution fusion | flops 1829240832 | bytes 27967488 | tf_op jit(solution)/shard_map/secd,secf->edf/dot_general | solution.py:256
  365.9 34.1 %all-gather.16.cloned.1.call-done = bf16[768,4096]{1,0:T(8,128)(2,1)} async-done(((bf16[24,4096]{1,0:T(8,128)(2,1)}), bf16[768,4096]{1,0:T(8,128)(2,1)}) %all-gather.16.cloned.1.call-update) | async-done | bytes 6291472 | tf_op jit(solution)/shard_map/all_gather | solution.py:97
  400.0 5.1 fusion.153
  405.1 55.8 %all-gather.18.cloned.1.call-done = bf16[2048,768]{1,0:T(8,128)(2,1)} async-done(((bf16[64,768]{1,0:T(8,128)(2,1)}), bf16[2048,768]{1,0:T(8,128)(2,1)}) %all-gather.18.cloned.1.call-update) | async-done | bytes 3145744 | tf_op jit(solution)/shard_map/all_gather | solution.py:98
  460.9 4.7 fusion.105
  466.4 3.6 fusion.156
  479.6 11.8 all_gather.56
  491.5 2.3 copy.210
  495.2 10.2 all_gather.57
  506.3 7.6 fusion.107
  513.9 7.6 fusion.98
  522.6 5.6 all-to-all-start.1
  528.3 13.2 %fusion.95 = bf16[4,4,18,768]{3,2,0,1:T(8,128)(2,1)S(1)} fusion(bf16[4,768,4096]{2,1,0:T(8,128)(2,1)} %all-gather.12.cloned.1.call-done, bf16[4,4,18,2048]{3,2,0,1:T(8,128)(2,1)} %get-tuple-element.890, bf16[4,4,18,2048]{3,2,0,1:T(8,128)(2,1)} %get-tuple-element.889), kind=kOutput, calls=%fused_computation.128 | convolution fusion | flops 1816879104 | bytes 27967488 | tf_op jit(solution)/shard_map/secf,edf->secd/dot_general | solution.py:259
  542.6 4.5 all-to-all-start.3
  547.6 6.1 fusion.108
  555.7 2.4 multiply_reduce_fusion
  569.6 21.5 %while.61 = (s32[]{:T(128)}, f32[2,12,64]{2,1,0:T(8,128)S(1)}, s32[4]{0:T(128)S(1)}, s32[256]{0:T(256)}, s32[64]{0:T(128)}, /*index=5*/s32[2]{0:T(128)}, bf16[2,...) while((s32[]{:T(128)}, f32[2,12,64]{2,1,0:T(8,128)S(1)}, ...), condition=%wide.region_20.21_spmd.clone, body=%wide.region_18.20_spmd.clone.sunk | while | flops 25671300 | bytes 2238189 | solution.py:304
  591.3 5.8 all_gather.59
  598.0 15.3 %all_gather.58 = bf16[2,2,128,768]{3,1,0,2:T(2,128)(2,1)} all-gather(bf16[2,2,32,768]{3,1,0,2:T(2,128)(2,1)S(1)} %copy-done.25), channel_id=1, replica_groups=mesh['ctx'=4,'exp'=4,'fsdp'=2] {'ctx'}, dimensions={2}, use_global_device_ids=true | all-gather | bytes 983040 | tf_op jit(solution)/shard_map/all_gather | solution.py:322
  613.2 3.8 copy.215
  617.0 3.1 reshape.754
  620.2 2.0 fusion.128
  622.7 52.2 %while.63 = (s32[]{:T(128)}, f32[2,64,12,64]{1,3,2,0:T(8,128)}, f32[2,64,12,64]{1,3,2,0:T(8,128)}, s32[4]{0:T(128)}, bf16[2,256,12,64]{1,3,2,0:T(8,128)(2,1)}, /...) while((s32[]{:T(128)}, f32[2,64,12,64]{1,3,2,0:T(8,128)}, ...), condition=%wide.region_24.25_spmd.clone, body=%wide.region_23.24_spmd.clone.sunk | while | flops 51523720 | bytes 5776641 | solution.py:357
  629.9 3.2 fusion.254
  633.2 2.2 fusion.255
  642.6 3.5 fusion.254
  646.1 2.5 fusion.255
  655.8 3.3 fusion.254
  659.2 2.7 fusion.255
  669.1 3.3 fusion.254
  672.4 2.5 fusion.255
  675.1 28.6 %while.62 = (s32[]{:T(128)}, f32[2,64,12,64]{1,3,2,0:T(8,128)}, s32[4]{0:T(128)S(1)}, bf16[2,256,12,64]{3,1,2,0:T(8,128)(2,1)S(1)}, s32[256]{0:T(256)}, /*index=...) while((s32[]{:T(128)}, f32[2,64,12,64]{1,3,2,0:T(8,128)}, ...), condition=%wide.region_22.23_spmd.clone, body=%wide.region_21.22_spmd.clone.sunk | while | flops 38645896 | bytes 3804400 | solution.py:319
  686.3 2.5 fusion.245
  693.7 2.7 fusion.245
  701.2 2.5 fusion.245
  707.7 4.0 fusion.154
  716.3 3.7 fusion.121
  720.0 47.9 %all-reduce.9 = (f32[768]{0:T(1024)S(1)}, f32[768,16]{0,1:T(8,128)S(1)}, f32[768]{0:T(1024)S(1)}) all-reduce(f32[768]{0:T(1024)S(1)} %get-tuple-element.764, f32[768,16]{0,1:T(8,128)} %fusion.155, f32[768]{0:T(1024)S(1)} %copy-done.42), channel_id=2, replica_groups=mesh['ctx'=4,'exp'=4,'fsdp'=2] {'ctx','exp','fsdp'}, use_global_device_ids=true, to_apply=%region_27.28.clone | all-reduce | flops 13824 | bytes 110592
  770.5 2.2 fusion.114
  772.6 3.5 fusion.102
  776.1 3.3 convert_element_type.242
  779.4 5.4 convert_element_type.240
  784.8 57.7 %reduce-scatter.14.cloned.1.call-done = f32[64,768]{1,0:T(8,128)} async-done(((f32[2048,768]{1,0:T(8,128)}), f32[64,768]{1,0:T(8,128)}) %reduce-scatter.14.cloned.1.call-update) | async-done | bytes 196624 | tf_op jit(solution)/shard_map/reduce_scatter | solution.py:384
  842.5 162.2 %reduce-scatter.12.cloned.1.call-done = f32[24,4096]{1,0:T(8,128)} async-done(((f32[768,4096]{1,0:T(8,128)}), f32[24,4096]{1,0:T(8,128)}) %reduce-scatter.12.cloned.1.call-update) | async-done | bytes 393232 | tf_op jit(solution)/shard_map/reduce_scatter | solution.py:383
  1004.8 103.7 %reduce-scatter.10.cloned.1.call-done = f32[24,768]{1,0:T(8,128)} async-done(((f32[768,768]{1,0:T(8,128)}), f32[24,768]{1,0:T(8,128)}) %reduce-scatter.10.cloned.1.call-update) | async-done | bytes 73744 | tf_op jit(solution)/shard_map/reduce_scatter | solution.py:380
  1108.5 125.4 %reduce-scatter.8.cloned.1.call-done = f32[24,2304]{1,0:T(8,128)} async-done(((f32[768,2304]{1,0:T(8,128)}), f32[24,2304]{1,0:T(8,128)}) %reduce-scatter.8.cloned.1.call-update) | async-done | bytes 221200 | tf_op jit(solution)/shard_map/reduce_scatter | solution.py:379
  (418 shorter events, 186.2 us)
Async XLA Ops:
  7.2 6.1 copy-start.9
  7.2 6.2 copy-start.55
  7.2 6.5 copy-start.56
  7.2 46.2 %copy-start.53 = (s32[2,2,32,2]{2,3,1,0:T(2,128)S(1)}, s32[2,2,32,2]{2,3,1,0:T(2,128)}, u32[]{:S(2)}) copy-start(s32[2,2,32,2]{2,3,1,0:T(2,128)} %param.26) | copy-start | bytes 3076
  7.2 46.9 %copy-start.52 = (bf16[24,16]{0,1:T(8,128)(2,1)S(1)}, bf16[24,16]{0,1:T(8,128)(2,1)}, u32[]{:S(2)}) copy-start(bf16[24,16]{0,1:T(8,128)(2,1)} %param.31) | copy-start | bytes 2308
  7.2 85.9 %all-gather.8.cloned.1.call-start = ((), (), s32[]{:S(2)}) async-start(), calls=%async_computation.10 | async-start | bytes 3649536 | tf_op jit(solution)/shard_map/all_gather | solution.py:93
  8.0 176.4 %all-gather.10.cloned.1.call-start = ((), (), s32[]{:S(2)}) async-start(), calls=%async_computation.11 | async-start | bytes 1216512 | tf_op jit(solution)/shard_map/all_gather | solution.py:94
  8.7 246.5 %all-gather.12.cloned.1.call-start = ((), (), s32[]{:S(2)}) async-start(), calls=%async_computation.12 | async-start | bytes 28311552 | tf_op jit(solution)/shard_map/all_gather | solution.py:101
  9.4 319.7 %all-gather.14.cloned.1.call-start = ((), (), s32[]{:S(2)}) async-start(), calls=%async_computation.13 | async-start | bytes 14155776 | tf_op jit(solution)/shard_map/all_gather | solution.py:102
  10.0 390.0 %all-gather.16.cloned.1.call-start = ((), (), s32[]{:S(2)}) async-start(), calls=%async_computation.14 | async-start | bytes 6488064 | tf_op jit(solution)/shard_map/all_gather | solution.py:97
  10.6 450.2 %all-gather.18.cloned.1.call-start = ((), (), s32[]{:S(2)}) async-start(), calls=%async_computation.15 | async-start | bytes 3244032 | tf_op jit(solution)/shard_map/all_gather | solution.py:98
  52.3 46.7 %copy-start.37 = (f32[768]{0:T(1024)}, f32[768]{0:T(1024)S(1)}, u32[]{:S(2)}) copy-start(f32[768]{0:T(1024)S(1)} %convert_element_type.200) | copy-start | bytes 9220
  53.5 45.4 %copy-start.40 = (s32[128,2]{0,1:T(2,128)}, s32[128,2]{0,1:T(2,128)S(1)}, u32[]{:S(2)}) copy-start(s32[128,2]{0,1:T(2,128)S(1)} %eq.36) | copy-start | bytes 3076
  93.0 12.1 copy-start.29
  93.0 12.1 copy-start.31
  93.1 5.8 copy-start.15
  105.3 14.5 %copy-start.11 = (bf16[2,64,12,64]{1,3,2,0:T(8,128)(2,1)}, bf16[2,64,12,64]{1,3,2,0:T(8,128)(2,1)S(1)}, u32[]{:S(2)}) copy-start(bf16[2,64,12,64]{1,3,2,0:T(8,128)(2,1)S(1)} %maximum_convert_fusion.2) | copy-start | bytes 589828
  105.7 24.8 %copy-start.13 = (bf16[2,64,12,64]{1,3,2,0:T(8,128)(2,1)}, bf16[2,64,12,64]{1,3,2,0:T(8,128)(2,1)S(1)}, u32[]{:S(2)}) copy-start(bf16[2,64,12,64]{1,3,2,0:T(8,128)(2,1)S(1)} %maximum_convert_fusion.1) | copy-start | bytes 589828
  183.7 3.5 copy-start.35
  183.7 3.6 copy-start.28
  183.7 3.7 copy-start.41
  183.7 4.3 copy-start.47
  183.7 4.3 copy-start.57
  183.7 4.6 copy-start.36
  184.4 2.3 copy-start.21
  186.6 8.6 copy-start.3
  187.1 2.0 copy-start.51
  187.3 319.0 %copy-start.6 = (bf16[128,768]{1,0:T(8,128)(2,1)}, bf16[128,768]{1,0:T(8,128)(2,1)S(1)}, u32[]{:S(2)}) copy-start(bf16[128,768]{1,0:T(8,128)(2,1)S(1)} %multiply_convert_fusion.5) | copy-start | bytes 589828
  195.2 22.4 %all-to-all-start = ((bf16[4,4,18,768]{3,1,2,0:T(4,128)(2,1)}), bf16[4,4,18,768]{3,1,2,0:T(4,128)(2,1)S(1)}, u32[]{:S(2)}, u32[]{:S(2)}) async-start(bf16[4,4,18,768]{3,1,2,0:T(4,128)(2,1)} %copy.190), calls=%async_computation | async-start | bytes 884736 | tf_op jit(solution)/shard_map/all_to_all | solution.py:212
  217.7 52.6 %all-to-all-start.2 = ((bf16[4,4,18,768]{3,1,2,0:T(4,128)(2,1)}), bf16[4,4,18,768]{3,1,2,0:T(4,128)(2,1)}, u32[]{:S(2)}, u32[]{:S(2)}) async-start(bf16[4,4,18,768]{3,1,2,0:T(4,128)(2,1)} %copy.196), calls=%async_computation.2 | async-start | bytes 884736 | tf_op jit(solution)/shard_map/all_to_all | solution.py:247
  222.2 553.9 %reduce-scatter.18.cloned.1.call-start = ((), (), s32[]{:S(2)}) async-start(), calls=%async_computation.21 | async-start | bytes 14155776 | tf_op jit(solution)/shard_map/reduce_scatter | solution.py:390
  351.8 427.7 %reduce-scatter.16.cloned.1.call-start = ((), (), s32[]{:S(2)}) async-start(), calls=%async_computation.20 | async-start | bytes 28311552 | tf_op jit(solution)/shard_map/reduce_scatter | solution.py:387
  365.8 95.0 %copy-start.24 = (bf16[128,768]{1,0:T(8,128)(2,1)S(1)}, bf16[128,768]{1,0:T(8,128)(2,1)}, u32[]{:S(2)}) copy-start(bf16[128,768]{1,0:T(8,128)(2,1)} %copy-done.23) | copy-start | bytes 589828
  365.8 476.7 %reduce-scatter.14.cloned.1.call-start = ((), (), s32[]{:S(2)}) async-start(), calls=%async_computation.19 | async-start | bytes 6488064 | tf_op jit(solution)/shard_map/reduce_scatter | solution.py:384
  470.0 534.7 %reduce-scatter.12.cloned.1.call-start = ((), (), s32[]{:S(2)}) async-start(), calls=%async_computation.18 | async-start | bytes 12976128 | tf_op jit(solution)/shard_map/reduce_scatter | solution.py:383
  477.2 29.1 %copy-start.50 = (f32[128]{0:T(128)S(1)}, f32[128]{0:T(128)}, u32[]{:S(2)}) copy-start(f32[128]{0:T(128)} %copy-done.49) | copy-start | bytes 1540
  522.6 20.0 %all-to-all-start.1 = ((bf16[4,4,18,768]{3,1,2,0:T(4,128)(2,1)}), bf16[4,4,18,768]{3,1,2,0:T(4,128)(2,1)}, u32[]{:S(2)}, u32[]{:S(2)}) async-start(bf16[4,4,18,768]{3,1,2,0:T(4,128)(2,1)} %copy.192), calls=%async_computation.1 | async-start | bytes 884736 | tf_op jit(solution)/shard_map/all_to_all | solution.py:220
  528.3 19.4 %copy-start.17 = (bf16[128,2048]{1,0:T(8,128)(2,1)S(1)}, bf16[128,2048]{1,0:T(8,128)(2,1)}, u32[]{:S(2)}) copy-start(bf16[128,2048]{1,0:T(8,128)(2,1)} %get-tuple-element.892) | copy-start | bytes 1572868
  542.6 16.1 %all-to-all-start.3 = ((bf16[4,4,18,768]{3,1,2,0:T(4,128)(2,1)}), bf16[4,4,18,768]{3,1,2,0:T(4,128)(2,1)}, u32[]{:S(2)}, u32[]{:S(2)}) async-start(bf16[4,4,18,768]{3,1,2,0:T(4,128)(2,1)} %copy.198), calls=%async_computation.3 | async-start | bytes 884736 | tf_op jit(solution)/shard_map/all_to_all | solution.py:262
  547.1 8.6 copy-start.14
  547.1 8.6 copy-start.45
  547.1 561.3 %reduce-scatter.10.cloned.1.call-start = ((), (), s32[]{:S(2)}) async-start(), calls=%async_computation.17 | async-start | bytes 2433024 | tf_op jit(solution)/shard_map/reduce_scatter | solution.py:380
  553.7 4.4 copy-start.39
  553.7 4.4 copy-start.43
  553.7 7.7 copy-start.27
  554.8 7.8 copy-start.4
  561.3 3.8 copy-start.33
  562.7 6.9 copy-start.18
  566.3 53.9 %copy-start.7 = (f32[128,768]{1,0:T(8,128)}, f32[128,768]{1,0:T(8,128)S(1)}, u32[]{:S(2)}) copy-start(f32[128,768]{1,0:T(8,128)S(1)} %fusion.113) | copy-start | bytes 1179652
  569.6 28.4 %copy-start.25 = (bf16[2,2,32,768]{3,1,0,2:T(2,128)(2,1)S(1)}, bf16[2,2,32,768]{3,1,0,2:T(2,128)(2,1)}, u32[]{:S(2)}) copy-start(bf16[2,2,32,768]{3,1,0,2:T(2,128)(2,1)} %copy.214) | copy-start | bytes 589828
  591.1 6.8 copy-start.19
  591.1 29.1 %copy-start.22 = (bf16[128,768]{0,1:T(8,128)(2,1)S(1)}, bf16[128,768]{0,1:T(8,128)(2,1)}, u32[]{:S(2)}) copy-start(bf16[128,768]{0,1:T(8,128)(2,1)} %copy-done.21) | copy-start | bytes 589828
  613.2 9.5 copy-start.2
  674.9 559.0 %reduce-scatter.8.cloned.1.call-start = ((), (), s32[]{:S(2)}) async-start(), calls=%async_computation.16 | async-start | bytes 7299072 | tf_op jit(solution)/shard_map/reduce_scatter | solution.py:379
  675.1 28.6 %copy-start.30 = (f32[64,32]{0,1:T(8,128)S(1)}, f32[64,32]{0,1:T(8,128)}, u32[]{:S(2)}) copy-start(f32[64,32]{0,1:T(8,128)} %copy-done.29) | copy-start | bytes 24580
  675.1 28.6 %copy-start.32 = (f32[64,32]{0,1:T(8,128)S(1)}, f32[64,32]{0,1:T(8,128)}, u32[]{:S(2)}) copy-start(f32[64,32]{0,1:T(8,128)} %copy-done.31) | copy-start | bytes 24580
  703.7 1.9 copy-start
  705.6 2.1 copy-start.16
  707.7 4.0 copy-start.8
  711.7 2.8 copy-start.34
  711.7 4.6 copy-start.1
  711.7 4.6 copy-start.38
  711.7 8.3 copy-start.42
  716.3 56.3 %copy-start.48 = (f32[128]{0:T(128)S(1)}, f32[128]{0:T(128)}, u32[]{:S(2)}) copy-start(f32[128]{0:T(128)} %reshape.758) | copy-start | bytes 1540
  (10 other events, 7.5 us)
Sparse Core Ops, SparseCore 0:
  11.1 59.7 all-gather.7
  73.9 54.0 all-gather.9
  129.9 125.2 all-gather.11
  257.0 72.1 all-gather.13
  332.0 67.9 all-gather.15
  402.9 57.9 all-gather.17
  464.4 94.0 reduce-scatter.17
  562.1 161.7 reduce-scatter.15
  730.1 112.3 reduce-scatter.13
  850.0 154.7 reduce-scatter.11
  1010.6 97.8 reduce-scatter.9
  1115.5 118.3 reduce-scatter.7
where the time goes:
time: 1260 us; the launch traced here: 1240 us
  waiting for transfers between devices  635 us (50%)
  blocking collectives  189 us (15%)
  matrix products  189 us (15%)
  local copies, waits for them, and re-layouts  106 us (8%)
  other arithmetic  67.8 us (5%)
  starting transfers between devices  26.3 us (2%)
  between operations  15.4 us (1%)
  loops' own time  13.9 us (1%)
    reduce_scatter x1, waiting for transfers between devices, per_device(): lax.psum_scatter(d_shared_in, ('ctx', 'exp', 'fsdp'), scatter_dimension=0...  162 us
    reduce_scatter x1, waiting for transfers between devices, per_device(): lax.psum_scatter(d_qkv, ('ctx', 'exp', 'fsdp'), scatter_dimension=0, tile...  125 us
    reduce_scatter x1, waiting for transfers between devices, per_device(): lax.psum_scatter(d_out_proj, ('ctx', 'exp', 'fsdp'), scatter_dimension=0,...  104 us
    unnamed x2, blocking collectives  86.2 us
    all_gather x1, waiting for transfers between devices, per_device(): lax.all_gather(w_experts_out, ('ctx', 'fsdp'), axis=1, tiled=True)  58.9 us
    reduce_scatter x1, waiting for transfers between devices, per_device(): lax.psum_scatter(d_shared_down, ('ctx', 'exp', 'fsdp'), scatter_dimension...  57.7 us
    all_gather x1, waiting for transfers between devices, per_device(): lax.all_gather(w_shared_down, ('ctx', 'exp', 'fsdp'), axis=0, tiled=True)  55.8 us
    all_gather x1, blocking collectives, per_device(): lax.all_gather(w_router, ('ctx', 'exp', 'fsdp'), axis=0, tiled=True)  37.3 us
  transfers between devices with their start and end apart: 16, of which 8 were waited for; matrix products, arithmetic and copies ran while one was open for 29% of the time, Pallas kernels for 0%

commit v1 on v0

--- a/solution.py
+++ b/solution.py
@@ -1,6 +1,10 @@
+import functools
+
 import jax
 import jax.numpy as jnp
 from jax import lax
+from jax.experimental import pallas as pl
+from jax.experimental.pallas import tpu as pltpu
 from jax.sharding import PartitionSpec as P
 
 HS = 64
@@ -406,9 +410,994 @@
     )
 
 
+F32 = jnp.float32
+BF = jnp.bfloat16
+MESH = pl.DeviceIdType.MESH
+ROWS = 24
+VMEM_BYTES = 60 * 1024 * 1024
+
+
+def place():
+    return lax.axis_index("ctx"), lax.axis_index("exp"), lax.axis_index("fsdp")
+
+
+def wrap(value, size):
+    return lax.rem(value, size)
+
+
+def mm(left, right):
+    return lax.dot_general(
+        left, right, (((1,), (0,)), ((), ())), preferred_element_type=F32
+    )
+
+
+def mm_nt(left, right):
+    return lax.dot_general(
+        left, right, (((1,), (1,)), ((), ())), preferred_element_type=F32
+    )
+
+
+def mm_tn(left, right):
+    return lax.dot_general(
+        left, right, (((0,), (0,)), ((), ())), preferred_element_type=F32
+    )
+
+
+def greet(peers):
+    barrier = pltpu.get_barrier_semaphore()
+    for peer in peers:
+        pl.semaphore_signal(barrier, inc=1, device_id=peer, device_id_type=MESH)
+    pl.semaphore_wait(barrier, len(peers))
+
+
+class Courier:
+    def __init__(self, send, recv):
+        self.send, self.recv, self.count, self.sent = send, recv, 0, []
+
+    def push(self, src, dst, device):
+        index = self.count
+        self.count += 1
+        copy = pltpu.make_async_remote_copy(
+            src_ref=src,
+            dst_ref=dst,
+            send_sem=self.send.at[index],
+            recv_sem=self.recv.at[index],
+            device_id=device,
+            device_id_type=MESH,
+        )
+        copy.start()
+        self.sent.append(copy)
+        return copy
+
+    def finish(self):
+        for copy in self.sent:
+            copy.wait_send()
+
+
+def swap_halves(rows):
+    width = rows.shape[1]
+    lane = lax.broadcasted_iota(jnp.int32, rows.shape, 1)
+    ahead = pltpu.roll(rows, width - HS // 2, 1)
+    behind = pltpu.roll(rows, HS // 2, 1)
+    return jnp.where((lane & (HS - 1)) < HS // 2, -ahead, behind)
+
+
+def wide(table, times):
+    return jnp.concatenate([table] * times, axis=1)
+
+
+def position_of(index, half_len, full_len):
+    block = index // (2 * half_len)
+    inside = index & (2 * half_len - 1)
+    low = block * half_len + (inside & (half_len - 1))
+    return jnp.where(inside >= half_len, full_len - 1 - low, low)
+
+
+def allowed_keys(length, half_len, full_len):
+    shape = (full_len, full_len)
+    query_at = position_of(lax.broadcasted_iota(jnp.int32, shape, 0), half_len, full_len)
+    key_at = position_of(lax.broadcasted_iota(jnp.int32, shape, 1), half_len, full_len)
+    return (key_at <= query_at) & (key_at < length)
+
+
+def head_probs(query, key, allowed):
+    scores = jnp.where(allowed, mm_nt(query, key) * (HS**-0.5), masked_out)
+    weights = jnp.exp(scores - jnp.max(scores, axis=1, keepdims=True))
+    return weights * (1.0 / jnp.sum(weights, axis=1, keepdims=True))
+
+
+def column_row(tail, lane):
+    pick = (lax.broadcasted_iota(jnp.int32, (8, 128), 1) == lane).astype(BF)
+    return mm_nt(pick, tail)[0:1]
+
+
+def local_copy(src, dst, sem):
+    return pltpu.make_async_copy(src, dst, sem)
+
+
+def plane_peers(c, z, f, nc):
+    return [(wrap(c + s, nc), z, f) for s in range(1, nc)]
+
+
+def column_peers(c, z, f, nz):
+    return [(c, wrap(z + s, nz), f) for s in range(1, nz)]
+
+
+def attention_forward(
+    nc, nz, len_ref, hid_ref, wq_ref, gu_ref, wo_ref, sd_ref, win_ref, wout_ref, cos_ref, sin_ref,
+    att_ref, normed_ref, qkv_ref, ctx_ref, w_ref, wo_all, gu_all, sd_all, wie_ref, woe_ref,
+    hid_all, wq_st, wq_buf, gu_st, gu_buf, wo_buf, part, part_own, rs_in,
+    send, recv, esend, erecv, lsem,
+):
+    c, z, f = place()
+    in_plane = plane_peers(c, z, f, nc)
+    in_column = column_peers(c, z, f, nz)
+    sibling = (c, z, 1 - f)
+    across = [(wrap(c + s, nc), z, 1 - f) for s in range(1, nc)]
+    greet(in_plane + in_column + [sibling] + across)
+    mail = Courier(send, recv)
+    num_seqs, shard_len, width = hid_ref.shape
+    full_len = nc * shard_len
+    half_len = shard_len // 2
+    down_rows = sd_ref.shape[0]
+
+    staged_wq = [
+        mail.push(wq_ref.at[wrap(c + s, nc)], wq_st.at[c], in_plane[s - 1]) for s in range(1, nc)
+    ]
+    arriving = [
+        [mail.push(hid_ref.at[q], hid_all.at[q, c], peer) for peer in in_plane]
+        for q in range(num_seqs)
+    ]
+    staged_gu = [
+        mail.push(gu_ref.at[wrap(c + s, nc)], gu_st.at[c], in_plane[s - 1]) for s in range(1, nc)
+    ]
+    wq_st[c] = wq_ref[c]
+    gu_st[c] = gu_ref[c]
+    wo_buf[z, f] = wo_ref[...]
+    own_down = pl.ds(pl.multiple_of((z * 2 + f) * down_rows, down_rows), down_rows)
+    sd_all[own_down] = sd_ref[...]
+    for q in range(num_seqs):
+        hid_all[q, c] = hid_ref[q]
+
+    for copy in staged_wq:
+        copy.wait_recv()
+    column_wq = [mail.push(wq_st, wq_buf.at[:, z, f], peer) for peer in in_column]
+    column_wo = [mail.push(wo_ref, wo_buf.at[z, f], peer) for peer in in_column]
+    sibling_wq = [mail.push(wq_st, wq_buf.at[:, z, f], sibling)]
+    sibling_wo = [mail.push(wo_ref, wo_buf.at[z, f], sibling)]
+    for i in range(nc):
+        wq_buf[i, z, f] = wq_st[i]
+
+    for copy in staged_gu:
+        copy.wait_recv()
+    column_gu = [mail.push(gu_st, gu_buf.at[:, z, f], peer) for peer in in_column]
+    column_sd = [mail.push(sd_ref, sd_all.at[own_down], peer) for peer in in_column]
+    sibling_late = [
+        mail.push(gu_st, gu_buf.at[:, z, f], sibling),
+        mail.push(sd_ref, sd_all.at[own_down], sibling),
+    ]
+    for i in range(nc):
+        gu_buf[i, z, f] = gu_st[i]
+
+    block = 2 * c + f
+    shard_rows, units = win_ref.shape[1], win_ref.shape[2] // 2
+    half_units = units // 2
+    lands = pl.ds(pl.multiple_of(block * shard_rows, shard_rows), shard_rows)
+    expert_in = []
+    own_in = []
+    for s in range(nc):
+        owner = wrap(c + s, nc)
+        for g in range(2):
+            core = f if g == 0 else 1 - f
+            for side in range(2):
+                from_lane = pl.multiple_of(side * units + core * half_units, half_units)
+                src = win_ref.at[owner, :, pl.ds(from_lane, half_units)]
+                dst = wie_ref.at[lands, pl.ds(side * half_units, half_units)]
+                if s == 0 and g == 0:
+                    own_in.append(local_copy(src, dst, lsem.at[side]))
+                    own_in[-1].start()
+                else:
+                    expert_in.append(mail.push(src, dst, (owner, z, core)))
+    out_rows = wout_ref.shape[1]
+    to_core = block // nc
+    slot = wrap(block, nc)
+    out_lands = pl.ds(pl.multiple_of(slot * out_rows, out_rows), out_rows)
+
+    def out_copy(s, device, to_slot, lands_at):
+        return pltpu.make_async_remote_copy(
+            src_ref=wout_ref.at[wrap(c + s, nc)],
+            dst_ref=woe_ref.at[lands_at],
+            send_sem=esend.at[s],
+            recv_sem=erecv.at[to_slot],
+            device_id=device,
+            device_id_type=MESH,
+        )
+
+    for s in range(1, nc):
+        out_copy(s, (wrap(c + s, nc), z, to_core), slot, out_lands).start()
+    own_out = local_copy(wout_ref.at[c], woe_ref.at[out_lands], lsem.at[2])
+
+    @pl.when(to_core == f)
+    def _():
+        own_out.start()
+
+    @pl.when(to_core != f)
+    def _():
+        out_copy(0, sibling, slot, out_lands).start()
+
+    for s in range(1, nz):
+        origin = wrap(z + nz - s, nz)
+        column_wq[s - 1].wait_recv()
+        sibling_wq.append(mail.push(wq_buf.at[:, origin, f], wq_buf.at[:, origin, f], sibling))
+    for s in range(1, nz):
+        origin = wrap(z + nz - s, nz)
+        column_wo[s - 1].wait_recv()
+        sibling_wo.append(mail.push(wo_buf.at[origin, f], wo_buf.at[origin, f], sibling))
+    for copy in sibling_wq:
+        copy.wait_recv()
+    for i in range(nc):
+        rows = nz * 2 * wq_ref.shape[1]
+        w_ref[i * rows : (i + 1) * rows, :] = (
+            wq_buf[i].astype(F32).reshape(rows, wq_ref.shape[2]).astype(BF)
+        )
+    for copy in sibling_wo:
+        copy.wait_recv()
+    wo_all[...] = wo_buf[...].astype(F32).reshape(wo_all.shape).astype(BF)
+
+    head_width = wo_all.shape[0]
+    cosines = wide(cos_ref[...], 2 * head_width // 128)
+    sines = wide(sin_ref[...], 2 * head_width // 128)
+    gain_row = column_row(w_ref[:, 512:640], 80)
+    parting = []
+    for q in range(num_seqs):
+        for copy in arriving[q]:
+            copy.wait_recv()
+        rows = hid_all[q].reshape(full_len, width).astype(F32)
+        normed = (
+            rows * lax.rsqrt(jnp.mean(rows * rows, axis=1, keepdims=True) + epsilon) * gain_row
+        ).astype(BF)
+        normed_ref[q] = normed
+        merged = mm(normed, w_ref[:, : 3 * head_width])
+        both = merged[:, : 2 * head_width]
+        both = (both * cosines + swap_halves(both) * sines).astype(BF)
+        values = merged[:, 2 * head_width :].astype(BF)
+        qkv_ref[q, :, : 2 * head_width] = both
+        qkv_ref[q, :, 2 * head_width :] = values
+        allowed = allowed_keys(len_ref[q], half_len, full_len)
+        heads = []
+        for h in range(head_width // HS):
+            probs = head_probs(
+                both[:, h * HS : (h + 1) * HS],
+                both[:, head_width + h * HS : head_width + (h + 1) * HS],
+                allowed,
+            ).astype(BF)
+            heads.append(mm(probs, values[:, h * HS : (h + 1) * HS]))
+        context = jnp.concatenate(heads, axis=1).astype(BF)
+        ctx_ref[q] = context
+        product = mm(context, wo_all[...]).reshape(nc, shard_len, width)
+        part_own[q] = product
+        part[q] = product.astype(BF)
+        parting.append(
+            [
+                mail.push(part.at[q, wrap(c + s, nc)], rs_in.at[s - 1, q], in_plane[s - 1])
+                for s in range(1, nc)
+            ]
+        )
+    for s in range(1, nz):
+        origin = wrap(z + nz - s, nz)
+        column_gu[s - 1].wait_recv()
+        column_sd[s - 1].wait_recv()
+        from_rows = pl.ds(pl.multiple_of((origin * 2 + f) * down_rows, down_rows), down_rows)
+        sibling_late.append(mail.push(gu_buf.at[:, origin, f], gu_buf.at[:, origin, f], sibling))
+        sibling_late.append(mail.push(sd_all.at[from_rows], sd_all.at[from_rows], sibling))
+    for q in range(num_seqs):
+        total = hid_ref[q].astype(F32) + part_own[q, c]
+        for s in range(1, nc):
+            parting[q][s - 1].wait_recv()
+            total = total + rs_in[s - 1, q].astype(F32)
+        att_ref[q] = total
+    for copy in sibling_late:
+        copy.wait_recv()
+    for i in range(nc):
+        rows = nz * 2 * gu_ref.shape[1]
+        gu_all[i * rows : (i + 1) * rows, :] = (
+            gu_buf[i].astype(F32).reshape(rows, gu_ref.shape[2]).astype(BF)
+        )
+    for copy in own_in:
+        copy.wait()
+    for copy in expert_in:
+        copy.wait_recv()
+    for at in range(nc):
+        origin_block = f * nc + at
+
+        @pl.when(origin_block != block)
+        def _(at=at):
+            out_copy(0, sibling, at, pl.ds(at * out_rows, out_rows)).wait_recv()
+
+    @pl.when(to_core == f)
+    def _():
+        own_out.wait()
+
+    @pl.when(to_core != f)
+    def _():
+        out_copy(0, sibling, slot, out_lands).wait_send()
+
+    for s in range(1, nc):
+        out_copy(s, (wrap(c + s, nc), z, to_core), slot, out_lands).wait_send()
+    mail.finish()
+
+
+def ffn_pass(rows_ref, grads_ref, in_ref, out_ref, hidden_ref, dm_ref, result, back, units, step):
+    result[...] = jnp.zeros_like(result)
+    back[...] = jnp.zeros_like(back)
+
+    def body(j, carry):
+        low = pl.multiple_of(j * step, step)
+        gate_at, up_at = pl.ds(low, step), pl.ds(pl.multiple_of(units + low, step), step)
+        rows, grads = rows_ref[...], grads_ref[...]
+        gate, up = mm(rows, in_ref[:, gate_at]), mm(rows, in_ref[:, up_at])
+        down = out_ref[gate_at, :]
+        d_hidden = mm_nt(grads, down)
+        share = 1.0 / (1.0 + jnp.exp(-gate))
+        lit = gate * share
+        hidden = (lit * up).astype(BF)
+        d_gate = (d_hidden * up * (share * (1.0 + gate * (1.0 - share)))).astype(BF)
+        d_up = (d_hidden * lit).astype(BF)
+        hidden_ref[:, gate_at] = hidden
+        dm_ref[:, gate_at] = d_gate
+        dm_ref[:, up_at] = d_up
+        result[...] += mm(hidden, down)
+        back[...] += mm_nt(d_gate, in_ref[:, gate_at]) + mm_nt(d_up, in_ref[:, up_at])
+        return carry
+
+    lax.fori_loop(0, units // step, body, 0)
+
+
+def split_dot(dot, left, right, left_wide=True):
+    whole = left if left_wide else right
+    high = whole.astype(BF)
+    low = (whole - high.astype(F32)).astype(BF)
+    if left_wide:
+        return dot(high, right) + dot(low, right)
+    return dot(left, high) + dot(left, low)
+
+
+def middle(
+    nc, nz, att_ref, go_ref, rt_ref, w_ref, gu_ref, sd_ref, wie_ref, woe_ref,
+    out_ref, datt_ref, ggu_ref, gsd_ref, gex_ref, gwi_ref, gwo_ref,
+    up_own, up_all, nt_all, sb, ar, xs, ds, rs_shared, sh_hidden, sh_dm, sh_out, sh_back, sh_send,
+    ex_hidden, ex_dm, ex_out, ex_back, pr, pin, fb, rb, send, recv,
+):
+    c, z, f = place()
+    in_plane = plane_peers(c, z, f, nc)
+    sibling = (c, z, 1 - f)
+    ring = [(dz, dc) for dz in range(nz) for dc in range(nc) if dz or dc]
+
+    def peer(dz, dc):
+        return (wrap(c + dc, nc), wrap(z + dz, nz), f)
+
+    greet([peer(*step) for step in ring] + [sibling])
+    mail = Courier(send, recv)
+    tok, width = att_ref.shape
+
+    table = rt_ref[...]
+    live = table[:, 4:5]
+    upstream = go_ref[...].astype(F32) * live
+    up_b = upstream.astype(BF)
+    up_f = up_b.astype(F32)
+    up_own[...] = up_b
+    up_all[c] = up_b
+    up_copies = [mail.push(up_own, up_all.at[c], p) for p in in_plane]
+    tail = w_ref[:, 512:640]
+    gain_row = column_row(tail, 81)
+    attended = att_ref[...]
+    inverse = lax.rsqrt(jnp.mean(attended * attended, axis=1, keepdims=True) + epsilon)
+    normed = (attended * inverse * gain_row).astype(BF)
+    nt_all[c] = normed
+
+    lane = lax.broadcasted_iota(jnp.int32, (tok, 128), 1).astype(F32)
+    logits = mm(normed, tail)
+    hots = [(lane == 64.0 + table[:, 2 + k : 3 + k]).astype(F32) for k in range(2)]
+    chosen = [jnp.sum(hot * logits, axis=1, keepdims=True) for hot in hots]
+    top = jnp.maximum(chosen[0], chosen[1])
+    raised = [jnp.exp(value - top) for value in chosen]
+    total = raised[0] + raised[1]
+    gates = [value / total for value in raised]
+    num_slots = nz * nc * ROWS
+    slot_lane = lax.broadcasted_iota(jnp.int32, (tok, num_slots), 1).astype(F32)
+    dispatch = [(slot_lane == table[:, k : k + 1]).astype(BF) for k in range(2)]
+    anyone = dispatch[0] + dispatch[1]
+    weighted = [(gates[k] * up_f).astype(BF) for k in range(2)]
+    rows_out = mm_tn(anyone, normed).astype(BF)
+    grads_out = (mm_tn(dispatch[0], weighted[0]) + mm_tn(dispatch[1], weighted[1])).astype(BF)
+    num_experts = nz * nc
+    sb[:, 0] = rows_out.astype(F32).reshape(num_experts, ROWS, width).astype(BF)
+    sb[:, 1] = grads_out.astype(F32).reshape(num_experts, ROWS, width).astype(BF)
+    row_copies = []
+    for dz, dc in ring:
+        to = peer(dz, dc)
+        row_copies.append(mail.push(sb.at[to[1] * nc + to[0]], ar.at[f, z, c], to))
+    nt_copies = [mail.push(nt_all.at[c], nt_all.at[c], p) for p in in_plane]
+    ar[f, z, c] = sb[z * nc + c]
+    forwards = [mail.push(sb.at[z * nc + c], ar.at[f, z, c], sibling)]
+    for copy, (dz, dc) in zip(row_copies, ring):
+        copy.wait_recv()
+        oz, oc = wrap(z + nz - dz, nz), wrap(c + nc - dc, nc)
+        forwards.append(mail.push(ar.at[f, oz, oc], ar.at[f, oz, oc], sibling))
+
+    for copy in up_copies + nt_copies:
+        copy.wait_recv()
+    rows_ref = nt_all.reshape(nc * tok, width)
+    grads_ref = up_all.reshape(nc * tok, width)
+    units = sd_ref.shape[0]
+    ffn_pass(rows_ref, grads_ref, gu_ref, sd_ref, sh_hidden, sh_dm, sh_out, sh_back, units, 256)
+    sh_send[0] = sh_out[...].astype(BF).reshape(nc, tok, width)
+    sh_send[1] = sh_back[...].astype(BF).reshape(nc, tok, width)
+    shared_copies = [
+        mail.push(sh_send.at[:, wrap(c + s, nc)], rs_shared.at[s - 1], in_plane[s - 1])
+        for s in range(1, nc)
+    ]
+
+    for copy in forwards:
+        copy.wait_recv()
+    half = nz * nc * ROWS
+    for core in range(2):
+        xs[core * half : (core + 1) * half] = (
+            ar[core, :, :, 0].astype(F32).reshape(half, width).astype(BF)
+        )
+        ds[core * half : (core + 1) * half] = (
+            ar[core, :, :, 1].astype(F32).reshape(half, width).astype(BF)
+        )
+    half_units = woe_ref.shape[0]
+    ffn_pass(xs, ds, wie_ref, woe_ref, ex_hidden, ex_dm, ex_out, ex_back, half_units, 256)
+    theirs = pl.ds(pl.multiple_of((1 - f) * half, half), half)
+    ours = pl.ds(pl.multiple_of(f * half, half), half)
+    pr[:, 0] = ex_out[theirs].reshape(num_experts, ROWS, width).astype(BF)
+    pr[:, 1] = ex_back[theirs].reshape(num_experts, ROWS, width).astype(BF)
+    swap = mail.push(pr, pin, sibling)
+    swap.wait_recv()
+    fb[:, 0] = (
+        ex_out[ours].reshape(num_experts, ROWS, width) + pin[:, 0].astype(F32)
+    ).astype(BF)
+    fb[:, 1] = (
+        ex_back[ours].reshape(num_experts, ROWS, width) + pin[:, 1].astype(F32)
+    ).astype(BF)
+    returns = []
+    for dz, dc in ring:
+        to = peer(dz, dc)
+        returns.append(mail.push(fb.at[to[1] * nc + to[0]], rb.at[z * nc + c], to))
+    rb[z * nc + c] = fb[z * nc + c]
+
+    def shared_grads(j, carry):
+        at = pl.ds(pl.multiple_of(j * 256, 256), 256)
+        piece = mm_tn(rows_ref[...], sh_dm[:, at])
+        ggu_ref[:, :, :, :, at] = piece.reshape(ggu_ref.shape[:4] + (256,)).astype(BF)
+        return carry
+
+    lax.fori_loop(0, 2 * units // 256, shared_grads, 0)
+    gsd_ref[...] = mm_tn(sh_hidden[...], grads_ref[...]).reshape(gsd_ref.shape).astype(BF)
+
+    def expert_grads(j, carry):
+        at = pl.ds(pl.multiple_of(j * 256, 256), 256)
+        gwi_ref[:, at] = mm_tn(xs[...], ex_dm[:, at]).astype(BF)
+        return carry
+
+    lax.fori_loop(0, 2 * half_units // 256, expert_grads, 0)
+
+    def down_grads(j, carry):
+        at = pl.ds(pl.multiple_of(j * 256, 256), 256)
+        gwo_ref[at, :] = mm_tn(ex_hidden[:, at], ds[...]).astype(BF)
+        return carry
+
+    lax.fori_loop(0, half_units // 256, down_grads, 0)
+
+    mine = pl.ds(pl.multiple_of(c * tok, tok), tok)
+    shared = sh_out[mine]
+    d_normed = sh_back[mine]
+    for s in range(1, nc):
+        shared_copies[s - 1].wait_recv()
+        shared = shared + rs_shared[s - 1, 0].astype(F32)
+        d_normed = d_normed + rs_shared[s - 1, 1].astype(F32)
+    for copy in returns:
+        copy.wait_recv()
+    results = rb[:, 0].astype(F32).reshape(num_slots, width).astype(BF)
+    d_rows = rb[:, 1].astype(F32).reshape(num_slots, width).astype(BF)
+    routed = [mm(dispatch[k], results) for k in range(2)]
+    mixture = gates[0] * routed[0] + gates[1] * routed[1]
+    out_ref[...] = (live * (attended + mixture + shared)).astype(BF)
+    d_gates = [jnp.sum(routed[k] * up_f, axis=1, keepdims=True) for k in range(2)]
+    mean_gate = gates[0] * d_gates[0] + gates[1] * d_gates[1]
+    d_logits = hots[0] * (gates[0] * (d_gates[0] - mean_gate)) + hots[1] * (
+        gates[1] * (d_gates[1] - mean_gate)
+    )
+    d_normed = d_normed + mm(anyone, d_rows) + split_dot(mm_nt, d_logits, tail)
+    d_router = split_dot(mm_tn, normed, d_logits, left_wide=False)
+    scaled = d_normed * gain_row
+    d_attended = (
+        upstream
+        + inverse * scaled
+        - attended * (inverse * inverse * inverse)
+        * jnp.mean(attended * scaled, axis=1, keepdims=True)
+    )
+    datt_ref[...] = d_attended
+    d_gain = jnp.sum(d_normed * attended * inverse, axis=0, keepdims=True)
+    turned = jnp.transpose(jnp.broadcast_to(d_gain, (128, width)), (1, 0))
+    extra_lane = lax.broadcasted_iota(jnp.int32, (width, 128), 1)
+    gex_ref[...] = jnp.where(extra_lane == 80, turned, d_router).reshape(gex_ref.shape)
+    mail.finish()
+
+
+def attention_backward(
+    nc, nz, len_ref, datt_ref, hid_ref, normed_ref, qkv_ref, w_ref, wo_ref, ctx_ref, cos_ref,
+    sin_ref, gex_ref, ggu_ref, gsd_ref, gwi_ref, gwo_ref,
+    gin_ref, fq_ref, fgu_ref, fsd_ref, fwo_ref, fex_ref, ein_ref, eout_ref,
+    da_own, da_all, part, part_own, rs_in, gq, gwo_at,
+    sib_gu, zb_gu, zi_gu, pb_gu, sib_q, zb_q, zi_q, pb_q, sib_ex, zb_ex, zi_ex, pb_ex, in_ex,
+    sib_sd, zb_sd, zi_sd, sib_wo, zb_wo, zi_wo,
+    send, recv, esend, erecv, lsem,
+):
+    c, z, f = place()
+    in_plane = plane_peers(c, z, f, nc)
+    in_column = column_peers(c, z, f, nz)
+    sibling = (c, z, 1 - f)
+    across = [(wrap(c + s, nc), z, 1 - f) for s in range(1, nc)]
+    greet(in_plane + in_column + [sibling] + across)
+    mail = Courier(send, recv)
+    num_seqs, shard_len, width = datt_ref.shape
+    full_len = nc * shard_len
+    half_len = shard_len // 2
+    head_width = wo_ref.shape[0]
+
+    da_own[...] = datt_ref[...].astype(BF)
+    arriving = []
+    for q in range(num_seqs):
+        arriving.append([mail.push(da_own.at[q], da_all.at[q, c], p) for p in in_plane])
+        da_all[q, c] = da_own[q]
+    sibling_gu = mail.push(ggu_ref.at[:, :, 1 - f], sib_gu, sibling)
+    sibling_ex = mail.push(gex_ref.at[:, :, 1 - f], sib_ex, sibling)
+    sibling_sd = mail.push(gsd_ref.at[:, 1 - f], sib_sd, sibling)
+
+    block = 2 * c + f
+    shard_rows, units = ein_ref.shape[1], ein_ref.shape[2] // 2
+    half_units = units // 2
+    expert_in, own_in = [], []
+    for s in range(nc):
+        owner = wrap(c + s, nc)
+        for g in range(2):
+            core = f if g == 0 else 1 - f
+            from_rows = pl.ds(
+                pl.multiple_of((2 * owner + core) * shard_rows, shard_rows), shard_rows
+            )
+            for side in range(2):
+                to_lane = pl.multiple_of(side * units + f * half_units, half_units)
+                src = gwi_ref.at[from_rows, pl.ds(side * half_units, half_units)]
+                dst = ein_ref.at[c, :, pl.ds(to_lane, half_units)]
+                if s == 0 and g == 0:
+                    own_in.append(local_copy(src, dst, lsem.at[side]))
+                    own_in[-1].start()
+                else:
+                    expert_in.append(mail.push(src, dst, (owner, z, core)))
+    out_rows = eout_ref.shape[1]
+    from_core = block // nc
+
+    def out_copy(j, arrives):
+        to_block = f * nc + j
+        return pltpu.make_async_remote_copy(
+            src_ref=gwo_ref.at[pl.ds(j * out_rows, out_rows)],
+            dst_ref=eout_ref.at[arrives],
+            send_sem=esend.at[j],
+            recv_sem=erecv.at[arrives],
+            device_id=(to_block // 2, z, wrap(to_block, 2)),
+            device_id_type=MESH,
+        )
+
+    def own_out(j):
+        return local_copy(
+            gwo_ref.at[pl.ds(j * out_rows, out_rows)], eout_ref.at[c], lsem.at[2]
+        )
+
+    for j in range(nc):
+
+        @pl.when(f * nc + j == block)
+        def _(j=j):
+            own_out(j).start()
+
+        @pl.when(f * nc + j != block)
+        def _(j=j):
+            out_copy(j, c).start()
+
+    sibling_gu.wait_recv()
+    for i in range(nc):
+        zb_gu[i] = (ggu_ref[i, :, f].astype(F32) + sib_gu[i].astype(F32)).astype(BF)
+    gu_copies = [
+        mail.push(zb_gu.at[:, wrap(z + s, nz)], zi_gu.at[s - 1], in_column[s - 1])
+        for s in range(1, nz)
+    ]
+    sibling_ex.wait_recv()
+    for i in range(nc):
+        zb_ex[i] = gex_ref[i, :, f] + sib_ex[i]
+    ex_copies = [
+        mail.push(zb_ex.at[:, wrap(z + s, nz)], zi_ex.at[s - 1], in_column[s - 1])
+        for s in range(1, nz)
+    ]
+    sibling_sd.wait_recv()
+    zb_sd[...] = (gsd_ref[:, f].astype(F32) + sib_sd[...].astype(F32)).astype(BF)
+    sd_copies = [
+        mail.push(zb_sd.at[wrap(z + s, nz)], zi_sd.at[s - 1], in_column[s - 1])
+        for s in range(1, nz)
+    ]
+
+    cosines = wide(cos_ref[...], 2 * head_width // 128)
+    sines = wide(sin_ref[...], 2 * head_width // 128)
+    grad_qkv = jnp.zeros((width, 3 * head_width), F32)
+    grad_out = jnp.zeros((head_width, width), F32)
+    parting = []
+    for q in range(num_seqs):
+        for copy in arriving[q]:
+            copy.wait_recv()
+        d_rows = da_all[q].reshape(full_len, width)
+        d_context = mm_nt(d_rows, wo_ref[...]).astype(BF)
+        grad_out = grad_out + mm_tn(ctx_ref[q], d_rows)
+        allowed = allowed_keys(len_ref[q], half_len, full_len)
+        merged = qkv_ref[q]
+        d_query, d_key, d_value = [], [], []
+        for h in range(head_width // HS):
+            query = merged[:, h * HS : (h + 1) * HS]
+            key = merged[:, head_width + h * HS : head_width + (h + 1) * HS]
+            value = merged[:, 2 * head_width + h * HS : 2 * head_width + (h + 1) * HS]
+            d_head = d_context[:, h * HS : (h + 1) * HS]
+            probs = head_probs(query, key, allowed)
+            d_probs = mm_nt(d_head, value)
+            delta = jnp.sum(probs * d_probs, axis=1, keepdims=True)
+            d_scores = (probs * (d_probs - delta)).astype(BF)
+            d_query.append(mm(d_scores, key) * (HS**-0.5))
+            d_key.append(mm_tn(d_scores, query) * (HS**-0.5))
+            d_value.append(mm_tn(probs.astype(BF), d_head))
+        both = jnp.concatenate(d_query + d_key, axis=1)
+        both = both * cosines - swap_halves(both) * sines
+        d_merged = jnp.concatenate([both] + d_value, axis=1).astype(BF)
+        product = mm_nt(d_merged, w_ref[:, : 3 * head_width]).reshape(nc, shard_len, width)
+        part_own[q] = product
+        part[q] = product.astype(BF)
+        parting.append(
+            [
+                mail.push(part.at[q, wrap(c + s, nc)], rs_in.at[s - 1, q], in_plane[s - 1])
+                for s in range(1, nc)
+            ]
+        )
+        grad_qkv = grad_qkv + mm_tn(normed_ref[q], d_merged)
+    gq[...] = grad_qkv.reshape(gq.shape).astype(BF)
+    sibling_q = mail.push(gq.at[:, :, 1 - f], sib_q, sibling)
+    gwo_at[...] = grad_out.reshape(gwo_at.shape).astype(BF)
+    sibling_wo = mail.push(gwo_at.at[:, 1 - f], sib_wo, sibling)
+
+    sibling_q.wait_recv()
+    for i in range(nc):
+        zb_q[i] = (gq[i, :, f].astype(F32) + sib_q[i].astype(F32)).astype(BF)
+    q_copies = [
+        mail.push(zb_q.at[:, wrap(z + s, nz)], zi_q.at[s - 1], in_column[s - 1])
+        for s in range(1, nz)
+    ]
+    sibling_wo.wait_recv()
+    zb_wo[...] = (gwo_at[:, f].astype(F32) + sib_wo[...].astype(F32)).astype(BF)
+    wo_copies = [
+        mail.push(zb_wo.at[wrap(z + s, nz)], zi_wo.at[s - 1], in_column[s - 1])
+        for s in range(1, nz)
+    ]
+
+    def column_sum(own, copies, inbox):
+        total = own.astype(F32)
+        for s in range(1, nz):
+            copies[s - 1].wait_recv()
+            total = total + inbox[s - 1].astype(F32)
+        return total
+
+    def hand_out(box, final):
+        final[c] = box[c]
+        return [
+            mail.push(box.at[wrap(c + s, nc)], final.at[c], in_plane[s - 1])
+            for s in range(1, nc)
+        ]
+
+    pb_gu[...] = column_sum(zb_gu[:, z], gu_copies, zi_gu).astype(BF)
+    final_gu = hand_out(pb_gu, fgu_ref)
+    pb_ex[...] = column_sum(zb_ex[:, z], ex_copies, zi_ex)
+    final_ex = hand_out(pb_ex, in_ex)
+    fsd_ref[...] = column_sum(zb_sd[z], sd_copies, zi_sd)
+    for q in range(num_seqs):
+        d_normed = part_own[q, c]
+        for s in range(1, nc):
+            parting[q][s - 1].wait_recv()
+            d_normed = d_normed + rs_in[s - 1, q].astype(F32)
+        gain_row = column_row(w_ref[:, 512:640], 80)
+        rows = hid_ref[q].astype(F32)
+        inverse = lax.rsqrt(jnp.mean(rows * rows, axis=1, keepdims=True) + epsilon)
+        scaled = d_normed * gain_row
+        gin_ref[q] = (
+            datt_ref[q]
+            + inverse * scaled
+            - rows * (inverse * inverse * inverse)
+            * jnp.mean(rows * scaled, axis=1, keepdims=True)
+        )
+    fwo_ref[...] = column_sum(zb_wo[z], wo_copies, zi_wo)
+    pb_q[...] = column_sum(zb_q[:, z], q_copies, zi_q).astype(BF)
+    final_q = hand_out(pb_q, fq_ref)
+    for copy in final_ex:
+        copy.wait_recv()
+    fex_ref[...] = jnp.sum(in_ex[...], axis=0)
+    for copy in final_gu + final_q:
+        copy.wait_recv()
+
+    for copy in own_in:
+        copy.wait()
+    for copy in expert_in:
+        copy.wait_recv()
+    for arrives in range(nc):
+
+        @pl.when((arrives != c) | (from_core != f))
+        def _(arrives=arrives):
+            out_copy(0, arrives).wait_recv()
+
+    for j in range(nc):
+
+        @pl.when(f * nc + j == block)
+        def _(j=j):
+            own_out(j).wait()
+
+        @pl.when(f * nc + j != block)
+        def _(j=j):
+            out_copy(j, c).wait_send()
+
+    mail.finish()
+
+
+def vmem(*shape, dtype=jnp.bfloat16):
+    return pltpu.VMEM(shape, dtype)
+
+
+def run(kernel, args, outs, scratch, copies, collective, spaces_in, spaces_out, flops, name):
+    dma = pltpu.SemaphoreType.DMA
+    return pl.pallas_call(
+        kernel,
+        out_shape=[jax.ShapeDtypeStruct(shape, dtype) for shape, dtype in outs],
+        in_specs=[pl.BlockSpec(memory_space=space) for space in spaces_in],
+        out_specs=[pl.BlockSpec(memory_space=space) for space in spaces_out],
+        scratch_shapes=list(scratch) + copies,
+        compiler_params=pltpu.CompilerParams(
+            collective_id=collective, has_side_effects=True, vmem_limit_bytes=VMEM_BYTES
+        ),
+        cost_estimate=pl.CostEstimate(flops=flops, bytes_accessed=20_000_000, transcendentals=0),
+        name=name,
+    )(*args)
+
+
+def fast_device(
+    hidden_in, seq_lengths, expert_ids, route_rank, gain_attn, w_qkv, w_out, w_router, gain_ffn,
+    w_gate_up, w_shared_down, w_experts_in, w_experts_out, grad_output,
+):
+    nc, nz = lax.axis_size("ctx"), lax.axis_size("exp")
+    num_seqs, two_ends, half_len, width = hidden_in.shape
+    shard_len = 2 * half_len
+    full_len = nc * shard_len
+    tok = num_seqs * shard_len
+    rows_w = w_qkv.shape[0]
+    head_width = w_qkv.shape[1] // 3 // nc
+    num_experts = w_router.shape[1]
+    down_rows = w_shared_down.shape[0]
+    units = w_gate_up.shape[1] // 2
+    own_units = units // nc
+    half_units = w_experts_in.shape[2] // 4
+    in_rows, out_rows = w_experts_in.shape[1], w_experts_out.shape[1]
+    hbm, vm, sm = pl.ANY, pltpu.VMEM, pltpu.SMEM
+    dma = pltpu.SemaphoreType.DMA
+
+    wq = w_qkv.reshape(rows_w, 3, nc, head_width).transpose(2, 0, 1, 3)
+    wq = wq.reshape(nc, rows_w, 3 * head_width)
+    small = jnp.concatenate([w_router, gain_attn[:, None], gain_ffn[:, None]], axis=1)
+    small = jnp.pad(small, ((0, 0), (0, 640 - 3 * head_width - small.shape[1])))
+    wq = jnp.concatenate([wq, jnp.broadcast_to(small, (nc,) + small.shape)], axis=2)
+    gu = w_gate_up.reshape(rows_w, 2, nc, own_units).transpose(2, 0, 1, 3)
+    gu = gu.reshape(nc, rows_w, 2 * own_units)
+
+    every = jnp.arange(full_len, dtype=jnp.int32)
+    inside = every % shard_len
+    low = every // shard_len * half_len + inside % half_len
+    cosines, sines = rope_tables(jnp.where(inside >= half_len, full_len - 1 - low, low))
+    cosines = jnp.tile(cosines, (1, 4))
+    sines = jnp.tile(sines, (1, 4))
+
+    mine = lax.axis_index("ctx") * half_len + jnp.arange(half_len, dtype=jnp.int32)
+    places = jnp.concatenate([mine, full_len - 1 - mine])
+    live = (places[None, :] < seq_lengths[:, None]).astype(F32).reshape(tok, 1)
+    picked = expert_ids.reshape(tok, 2)
+    hot = (picked[:, :, None] == jnp.arange(num_experts, dtype=jnp.int32)).astype(F32)
+    load = (jnp.sum(hot, axis=1) * live).astype(BF)
+    rank = route_rank.reshape(tok)
+    earlier = (rank[None, :] < rank[:, None]).astype(BF)
+    position = jnp.dot(earlier, load, preferred_element_type=F32)
+    at = jnp.sum(hot * position[:, None, :], axis=-1)
+    kept = (live > 0) & (at < CAP)
+    slots = jnp.where(kept, picked.astype(F32) * ROWS + at, -1.0)
+    table = jnp.concatenate([slots, picked.astype(F32), live], axis=1)
+    table = jnp.pad(table, ((0, 0), (0, 128 - table.shape[1])))
+
+    hidden = hidden_in.reshape(num_seqs, shard_len, width)
+    grads = grad_output.reshape(tok, width)
+    blocks = (nc, nz, 2, rows_w)
+    wqkv_width = wq.shape[2]
+    att, normed, qkv, context, w_all, wo_all, gu_all, sd_all, wie, woe = run(
+        functools.partial(attention_forward, nc, nz),
+        (seq_lengths, hidden, wq, gu, w_out, w_shared_down, w_experts_in, w_experts_out, cosines, sines),
+        [
+            ((num_seqs, shard_len, width), F32),
+            ((num_seqs, full_len, width), BF),
+            ((num_seqs, full_len, 3 * head_width), BF),
+            ((num_seqs, full_len, head_width), BF),
+            ((width, wqkv_width), BF),
+            ((head_width, width), BF),
+            ((width, 2 * own_units), BF),
+            ((own_units, width), BF),
+            ((width, 2 * half_units), BF),
+            ((half_units, width), BF),
+        ],
+        [
+            vmem(num_seqs, nc, shard_len, width),
+            vmem(nc, rows_w, wqkv_width),
+            vmem(*blocks, wqkv_width),
+            vmem(nc, rows_w, 2 * own_units),
+            vmem(*blocks, 2 * own_units),
+            vmem(nz, 2, rows_w, width),
+            vmem(num_seqs, nc, shard_len, width),
+            vmem(num_seqs, nc, shard_len, width, dtype=F32),
+            vmem(nc - 1, num_seqs, shard_len, width),
+        ],
+        [dma((80,)), dma((80,)), dma((nc,)), dma((nc,)), dma((3,))],
+        0,
+        [sm] + [vm] * 5 + [hbm, hbm, vm, vm],
+        [vm] * 8 + [hbm, hbm],
+        1_000_000_000,
+        "attention_forward",
+    )
+    slots_all = num_experts * ROWS
+    out, d_att, ggu, gsd, gex, gwi, gwo = run(
+        functools.partial(middle, nc, nz),
+        (att.reshape(tok, width), grads, table, w_all, gu_all, sd_all, wie, woe),
+        [
+            ((tok, width), BF),
+            ((tok, width), F32),
+            ((*blocks, 2 * own_units), BF),
+            ((nz, 2, down_rows, width), BF),
+            ((*blocks, 128), F32),
+            ((width, 2 * half_units), BF),
+            ((half_units, width), BF),
+        ],
+        [
+            vmem(tok, width),
+            vmem(nc, tok, width),
+            vmem(nc, tok, width),
+            vmem(num_experts, 2, ROWS, width),
+            vmem(2, nz, nc, 2, ROWS, width),
+            vmem(2 * slots_all, width),
+            vmem(2 * slots_all, width),
+            vmem(nc - 1, 2, tok, width),
+            vmem(nc * tok, own_units),
+            vmem(nc * tok, 2 * own_units),
+            vmem(nc * tok, width, dtype=F32),
+            vmem(nc * tok, width, dtype=F32),
+            vmem(2, nc, tok, width),
+            vmem(2 * slots_all, half_units),
+            vmem(2 * slots_all, 2 * half_units),
+            vmem(2 * slots_all, width, dtype=F32),
+            vmem(2 * slots_all, width, dtype=F32),
+            vmem(num_experts, 2, ROWS, width),
+            vmem(num_experts, 2, ROWS, width),
+            vmem(num_experts, 2, ROWS, width),
+            vmem(num_experts, 2, ROWS, width),
+        ],
+        [dma((64,)), dma((64,))],
+        1,
+        [vm] * 8,
+        [vm] * 7,
+        13_000_000_000,
+        "routed_and_shared",
+    )
+    grad_in, fq, fgu, fsd, fwo, fex, e_in, e_out = run(
+        functools.partial(attention_backward, nc, nz),
+        (seq_lengths, d_att.reshape(num_seqs, shard_len, width), hidden, normed, qkv, w_all, wo_all,
+         context, cosines, sines, gex, ggu, gsd, gwi, gwo),
+        [
+            ((num_seqs, shard_len, width), F32),
+            ((nc, rows_w, 3 * head_width), BF),
+            ((nc, rows_w, 2 * own_units), BF),
+            ((down_rows, width), F32),
+            ((rows_w, width), F32),
+            ((rows_w, 128), F32),
+            (w_experts_in.shape, BF),
+            (w_experts_out.shape, BF),
+        ],
+        [
+            vmem(num_seqs, shard_len, width),
+            vmem(num_seqs, nc, shard_len, width),
+            vmem(num_seqs, nc, shard_len, width),
+            vmem(num_seqs, nc, shard_len, width, dtype=F32),
+            vmem(nc - 1, num_seqs, shard_len, width),
+            vmem(*blocks, 3 * head_width),
+            vmem(nz, 2, rows_w, width),
+            vmem(nc, nz, rows_w, 2 * own_units),
+            vmem(nc, nz, rows_w, 2 * own_units),
+            vmem(nz - 1, nc, rows_w, 2 * own_units),
+            vmem(nc, rows_w, 2 * own_units),
+            vmem(nc, nz, rows_w, 3 * head_width),
+            vmem(nc, nz, rows_w, 3 * head_width),
+            vmem(nz - 1, nc, rows_w, 3 * head_width),
+            vmem(nc, rows_w, 3 * head_width),
+            vmem(nc, nz, rows_w, 128, dtype=F32),
+            vmem(nc, nz, rows_w, 128, dtype=F32),
+            vmem(nz - 1, nc, rows_w, 128, dtype=F32),
+            vmem(nc, rows_w, 128, dtype=F32),
+            vmem(nc, rows_w, 128, dtype=F32),
+            vmem(nz, down_rows, width),
+            vmem(nz, down_rows, width),
+            vmem(nz - 1, down_rows, width),
+            vmem(nz, rows_w, width),
+            vmem(nz, rows_w, width),
+            vmem(nz - 1, rows_w, width),
+        ],
+        [dma((80,)), dma((80,)), dma((nc,)), dma((nc,)), dma((3,))],
+        2,
+        [sm] + [vm] * 12 + [hbm, hbm],
+        [vm] * 6 + [hbm, hbm],
+        2_000_000_000,
+        "attention_backward",
+    )
+    grad_qkv = fq.astype(F32).reshape(nc, rows_w, 3, head_width).transpose(1, 2, 0, 3)
+    grad_qkv = grad_qkv.reshape(w_qkv.shape)
+    grad_gu = fgu.astype(F32).reshape(nc, rows_w, 2, own_units).transpose(1, 2, 0, 3)
+    grad_gain = jnp.sum(w_qkv.astype(F32) * grad_qkv, axis=1) / gain_attn.astype(F32)
+    return (
+        out.reshape(hidden_in.shape),
+        grad_in.reshape(hidden_in.shape),
+        grad_gain,
+        grad_qkv,
+        fwo,
+        fex[:, 64 : 64 + num_experts],
+        fex[:, 80],
+        grad_gu.reshape(w_gate_up.shape),
+        fsd,
+        e_in.astype(F32),
+        e_out.astype(F32),
+    )
+
+
+def fits(mesh, hidden_in, w_qkv, w_router, w_gate_up, w_experts_in):
+    nc, nz, nf = mesh.shape["ctx"], mesh.shape["exp"], mesh.shape["fsdp"]
+    heads = w_qkv.shape[1] // 3 // HS
+    return (
+        nf == 2
+        and nc % 2 == 0
+        and heads % nc == 0
+        and w_router.shape[1] == nc * nz
+        and (heads // nc * HS * 2) % 128 == 0
+        and 3 * heads // nc * HS == 576
+        and w_router.shape[1] == 16
+        and hidden_in.shape[2] // nc == 32
+        and hidden_in.shape[0] == 2 * nz * nf
+        and hidden_in.shape[3] == 768
+        and CAP <= ROWS
+    )
+
+
 def solution(mesh):
+    def whole(*args):
+        chosen = fast_device if fits(mesh, args[0], args[5], args[7], args[9], args[11]) else per_device
+        return placed(mesh, chosen)(*args)
+
+    return whole
+
+
+def placed(mesh, chosen):
     return jax.shard_map(
-        per_device,
+        chosen,
         mesh=mesh,
         in_specs=(
             P(("exp", "fsdp"), None, "ctx", None),

time: 1260 us -> 286 us (0.23); the launches traced: 1240 us -> 280 us
  waiting for transfers between devices: 635 us -> 0 us
  Pallas kernels: 0 us -> 250 us
  blocking collectives: 189 us -> 0 us
  matrix products: 189 us -> 0.93 us
  local copies, waits for them, and re-layouts: 106 us -> 18.1 us
  other arithmetic: 67.8 us -> 10 us
  starting transfers between devices: 26.3 us -> 0 us
  between operations: 15.4 us -> 0.86 us
  loops' own time: 13.9 us -> 0 us
    reduce_scatter x6 -> x0, waiting for transfers between devices: 449 us -> none  [the longest x1 162 us: per_device(): lax.psum_scatter(d_shared_in, ('ctx', 'exp', 'fsdp'), scatter_dimension=0...]
    pallas_call x0 -> x3, Pallas kernels: none -> 250 us  [run(): pl.pallas_call(kernel, out_shape=[jax.ShapeDtypeStruct(shape, dtype) for...]
    dot_general x62 -> x1, matrix products: 189 us -> 0.93 us  [fast_device(): position = jnp.dot(earlier, load, preferred_element_type=F32)]
    all_gather x6 -> x0, waiting for transfers between devices: 182 us -> none  [the longest x1 58.9 us: per_device(): lax.all_gather(w_experts_out, ('ctx', 'fsdp'), axis=1, tiled=True)]
    all_gather x7 -> x0, blocking collectives: 103 us -> none  [the longest x1 37.3 us: per_device(): lax.all_gather(w_router, ('ctx', 'exp', 'fsdp'), axis=0, tiled=True)]
    unnamed x2 -> x0, blocking collectives: 86.2 us -> none
    dynamic_slice x44 -> x0, local copies, waits for them, and re-layouts: 39.4 us -> none  [the longest x20 19.6 us: per_device(): lax.scan(lse_step, (jnp.full(stat_shape, masked_out, jnp.float32), jnp.ze...]
    all_to_all x4 -> x0, starting transfers between devices: 24.8 us -> none  [the longest x1 10.2 us: per_device(): lax.all_to_all(send_rows, 'exp', split_axis=0, concat_axis=0, tiled=True)]
  transfers between devices with their start and end apart: 16 -> 0, of which waited for: 8 -> 0; matrix products, arithmetic and copies ran while one was open for 29% -> 0% of each run, Pallas kernels for 0% -> 0%
where the time goes in v1:
time: 286 us; the launch traced here: 280 us
  Pallas kernels  250 us (87%)
  local copies, waits for them, and re-layouts  18.1 us (6%)
  other arithmetic  10 us (3%)
    pallas_call x3, Pallas kernels, run(): pl.pallas_call(kernel, out_shape=[jax.ShapeDtypeStruct(shape, dtype) for...  250 us

profile of v1, /device:TPU:31, one launch (start us, length us, event | category | flops | bytes accessed | tf_op | source)
XLA Modules:
  0.0 280.3 jit_solution(4075562510857425963)
XLA Ops:
  0.7 0.1 pad_add_fusion
  0.8 0.7 compare_convert_fusion
  1.5 0.1 reshape.241
  1.6 0.1 reshape.242
  1.7 0.7 copy.78
  2.3 0.1 eq.18
  2.4 0.7 pad_maximum_fusion.1
  3.2 0.1 copy.85
  3.3 0.9 fusion
  4.3 0.1 copy.79
  4.4 0.6 pad.9.rt_ref
  5.0 0.2 multiply_sine_fusion
  5.3 0.8 copy.77.sin_ref
  6.0 0.8 copy.76.cos_ref
  6.8 1.1 reshape.226
  7.9 0.1 copy.89
  7.9 0.2 reshape.227
  8.1 0.7 pad_maximum_fusion.wq_ref
  8.8 1.1 reshape.228
  9.9 0.2 copy.88
  10.1 0.8 reshape.229.gu_ref
  10.9 81.5 %attention_forward.1 = (f32[2,64,768]{2,1,0:T(8,128)}, bf16[2,256,768]{2,1,0:T(8,128)(2,1)}, bf16[2,256,576]{2,1,0:T(8,128)(2,1)}, bf16[2,256,192]{2,1,0:T(8,128...) custom-call(s32[2]{0:T(128)} %len_ref.3, ...), custom_call_target="tpu_custom_call" | custom-call | flops 1000000000 | bytes 20000000 | tf_op jit(solution)/shard_map/attention_forward/pallas_call | solution.py:1160
  92.3 87.8 %routed_and_shared.1 = (bf16[128,768]{1,0:T(8,128)(2,1)}, f32[128,768]{1,0:T(8,128)}, bf16[4,4,2,24,1024]{4,3,2,1,0:T(8,128)(2,1)}, bf16[4,2,64,768]{3,2,1,0:T(8...) custom-call(f32[128,768]{1,0:T(8,128)} %bitcast.34, ...), custom_call_target="tpu_custom_call" | custom-call | flops 12999999488 | bytes 20000000 | tf_op jit(solution)/shard_map/routed_and_shared/pallas_call | solution.py:1160
  180.1 0.0 copy-start.2
  180.1 0.0 copy-start.7
  180.1 81.1 %attention_backward.1 = (f32[2,64,768]{2,1,0:T(8,128)}, bf16[4,24,576]{2,1,0:T(8,128)(2,1)}, bf16[4,24,1024]{2,1,0:T(8,128)(2,1)}, f32[64,768]{1,0:T(8,128)}, f3...) custom-call(s32[2]{0:T(128)} %len_ref.3, ...), custom_call_target="tpu_custom_call" | custom-call | flops 2000000000 | bytes 20000000 | tf_op jit(solution)/shard_map/attention_backward/pallas_call | solution.py:1160
  261.3 1.4 slice_reduce_fusion
  262.7 0.8 slice.6
  263.4 0.7 copy.84
  264.1 1.1 reshape.250
  265.2 0.2 copy.82
  265.4 0.2 reshape.244
  265.6 0.0 copy-done.2
  265.6 0.0 copy-start.1
  265.6 0.1 multiply_reduce_fusion
  265.8 0.0 copy-done.7
  265.8 0.5 convert_divide_fusion
  266.3 1.3 reshape.252
  267.6 0.0 copy-done.1
  267.6 0.0 copy-start
  267.6 1.0 copy.83
  268.6 2.1 reshape.246
  270.7 3.3 %convert_element_type.76 = f32[4,256,768]{2,1,0:T(8,128)} convert(bf16[4,256,768]{2,1,0:T(8,128)(2,1)} %get-tuple-element.60) | non-fusion elementwise | flops 786432 | bytes 4718592 | tf_op jit(solution)/shard_map/convert_element_type | solution.py:1368
  274.1 0.0 copy-done
  274.1 0.0 copy-start.4
  274.1 0.0 copy-start.3
  274.1 0.0 copy-start.6
  274.1 0.0 copy-start.5
  274.1 3.5 %convert_element_type.75 = f32[4,96,4096]{2,1,0:T(8,128)} convert(bf16[4,96,4096]{2,1,0:T(8,128)(2,1)S(1)} %copy-done) | non-fusion elementwise | flops 1572864 | bytes 9437184 | tf_op jit(solution)/shard_map/convert_element_type | solution.py:1367
  277.6 0.0 copy-done.4
  277.6 0.7 copy.94
  278.2 0.0 copy-done.3
  278.2 0.7 copy.95
  279.0 0.0 copy-done.6
  279.0 0.6 copy.96
  279.6 0.0 copy-done.5
  279.6 0.7 copy.97
  (13 shorter events, 0.1 us)
Async XLA Ops:
  180.1 85.5 %copy-start.2 = (bf16[24,2304]{1,0:T(8,128)(2,1)S(1)}, bf16[24,2304]{1,0:T(8,128)(2,1)}, u32[]{:S(2)}) copy-start(bf16[24,2304]{1,0:T(8,128)(2,1)} %param.19) | copy-start | bytes 331780
  180.1 85.6 %copy-start.7 = (bf16[24]{0:T(256)(128)(2,1)S(1)}, bf16[24]{0:T(256)(128)(2,1)}, u32[]{:S(2)}) copy-start(bf16[24]{0:T(256)(128)(2,1)} %param.18) | copy-start | bytes 148
  265.6 2.0 copy-start.1
  267.6 6.4 %copy-start = (bf16[4,96,4096]{2,1,0:T(8,128)(2,1)S(1)}, bf16[4,96,4096]{2,1,0:T(8,128)(2,1)}, u32[]{:S(2)}) copy-start(bf16[4,96,4096]{2,1,0:T(8,128)(2,1)} %get-tuple-element.59) | copy-start | bytes 9437188
  274.1 3.5 %copy-start.4 = (bf16[128,768]{1,0:T(8,128)(2,1)S(1)}, bf16[128,768]{1,0:T(8,128)(2,1)}, u32[]{:S(2)}) copy-start(bf16[128,768]{1,0:T(8,128)(2,1)} %get-tuple-element.42) | copy-start | bytes 589828
  274.1 4.2 %copy-start.3 = (f32[2,64,768]{2,1,0:T(8,128)S(1)}, f32[2,64,768]{2,1,0:T(8,128)}, u32[]{:S(2)}) copy-start(f32[2,64,768]{2,1,0:T(8,128)} %get-tuple-element.53) | copy-start | bytes 1179652
  274.1 4.9 %copy-start.6 = (f32[24,768]{1,0:T(8,128)S(1)}, f32[24,768]{1,0:T(8,128)}, u32[]{:S(2)}) copy-start(f32[24,768]{1,0:T(8,128)} %get-tuple-element.135) | copy-start | bytes 221188
  274.1 5.5 %copy-start.5 = (f32[64,768]{1,0:T(8,128)S(1)}, f32[64,768]{1,0:T(8,128)}, u32[]{:S(2)}) copy-start(f32[64,768]{1,0:T(8,128)} %get-tuple-element.139) | copy-start | bytes 589828

commit v2 on v0

--- a/solution.py
+++ b/solution.py
@@ -1,6 +1,10 @@
+import functools
+
 import jax
 import jax.numpy as jnp
 from jax import lax
+from jax.experimental import pallas as pl
+from jax.experimental.pallas import tpu as pltpu
 from jax.sharding import PartitionSpec as P
 
 HS = 64
@@ -406,9 +410,1048 @@
     )
 
 
+F32 = jnp.float32
+BF = jnp.bfloat16
+MESH = pl.DeviceIdType.MESH
+ROWS = 24
+SMALL = 64
+VMEM_BYTES = 63 * 1024 * 1024
+
+
+def place():
+    return lax.axis_index("ctx"), lax.axis_index("exp"), lax.axis_index("fsdp")
+
+
+def wrap(value, size):
+    return lax.rem(value, size)
+
+
+def mm(left, right):
+    return lax.dot_general(
+        left, right, (((1,), (0,)), ((), ())), preferred_element_type=F32
+    )
+
+
+def mm_nt(left, right):
+    return lax.dot_general(
+        left, right, (((1,), (1,)), ((), ())), preferred_element_type=F32
+    )
+
+
+def mm_tn(left, right):
+    return lax.dot_general(
+        left, right, (((0,), (0,)), ((), ())), preferred_element_type=F32
+    )
+
+
+def greet(peers):
+    barrier = pltpu.get_barrier_semaphore()
+    for peer in peers:
+        pl.semaphore_signal(barrier, inc=1, device_id=peer, device_id_type=MESH)
+
+
+def met(peers):
+    pl.semaphore_wait(pltpu.get_barrier_semaphore(), len(peers))
+
+
+class Courier:
+    def __init__(self, send, recv):
+        self.send, self.recv, self.count, self.sent = send, recv, 0, []
+
+    def push(self, src, dst, device):
+        index = self.count
+        self.count += 1
+        copy = pltpu.make_async_remote_copy(
+            src_ref=src,
+            dst_ref=dst,
+            send_sem=self.send.at[index],
+            recv_sem=self.recv.at[index],
+            device_id=device,
+            device_id_type=MESH,
+        )
+        copy.start()
+        self.sent.append(copy)
+        return copy
+
+    def settle(self, copies):
+        for copy in copies:
+            copy.wait_send()
+        done = {id(copy) for copy in copies}
+        self.sent = [copy for copy in self.sent if id(copy) not in done]
+
+    def finish(self):
+        self.settle(list(self.sent))
+
+
+def swap_halves(rows):
+    width = rows.shape[1]
+    lane = lax.broadcasted_iota(jnp.int32, rows.shape, 1)
+    ahead = pltpu.roll(rows, width - HS // 2, 1)
+    behind = pltpu.roll(rows, HS // 2, 1)
+    return jnp.where((lane & (HS - 1)) < HS // 2, -ahead, behind)
+
+
+def wide(table, times):
+    return jnp.concatenate([table] * times, axis=1)
+
+
+def position_of(index, half_len, full_len):
+    block = index // (2 * half_len)
+    inside = index & (2 * half_len - 1)
+    low = block * half_len + (inside & (half_len - 1))
+    return jnp.where(inside >= half_len, full_len - 1 - low, low)
+
+
+def allowed_keys(length, half_len, full_len):
+    shape = (full_len, full_len)
+    query_at = position_of(lax.broadcasted_iota(jnp.int32, shape, 0), half_len, full_len)
+    key_at = position_of(lax.broadcasted_iota(jnp.int32, shape, 1), half_len, full_len)
+    return (key_at <= query_at) & (key_at < length)
+
+
+def head_probs(query, key, allowed):
+    scores = jnp.where(allowed, mm_nt(query, key) * (HS**-0.5), masked_out)
+    weights = jnp.exp(scores - jnp.max(scores, axis=1, keepdims=True))
+    return weights * (1.0 / jnp.sum(weights, axis=1, keepdims=True))
+
+
+def column_row(tail, lane):
+    pick = (lax.broadcasted_iota(jnp.int32, (8, 128), 1) == lane).astype(BF)
+    return mm_nt(pick, tail)[0:1]
+
+
+def split_dot(dot, left, right, left_wide=True):
+    whole = left if left_wide else right
+    high = whole.astype(BF)
+    low = (whole - high.astype(F32)).astype(BF)
+    if left_wide:
+        return dot(high, right) + dot(low, right)
+    return dot(left, high) + dot(left, low)
+
+
+def inverse_rms(rows):
+    return lax.rsqrt(jnp.mean(rows * rows, axis=1, keepdims=True) + epsilon)
+
+
+def norm_back(rows, inverse, scaled):
+    return inverse * scaled - rows * (inverse * inverse * inverse) * jnp.mean(
+        rows * scaled, axis=1, keepdims=True
+    )
+
+
+def join(blocks, shape):
+    return blocks.astype(F32).reshape(shape).astype(BF)
+
+
+def ffn_pass(rows_ref, grads_ref, in_ref, out_ref, hidden_ref, dm_ref, result, back, units, step):
+    result[...] = jnp.zeros(result.shape, F32)
+    back[...] = jnp.zeros(back.shape, F32)
+
+    def body(j, carry):
+        low = pl.multiple_of(j * step, step)
+        gate_at, up_at = pl.ds(low, step), pl.ds(pl.multiple_of(units + low, step), step)
+        rows, grads = rows_ref[...], grads_ref[...]
+        gate, up = mm(rows, in_ref[:, gate_at]), mm(rows, in_ref[:, up_at])
+        down = out_ref[gate_at, :]
+        d_hidden = mm_nt(grads, down)
+        share = 1.0 / (1.0 + jnp.exp(-gate))
+        lit = gate * share
+        hidden = (lit * up).astype(BF)
+        d_gate = (d_hidden * up * (share * (1.0 + gate * (1.0 - share)))).astype(BF)
+        d_up = (d_hidden * lit).astype(BF)
+        hidden_ref[:, gate_at] = hidden
+        dm_ref[:, gate_at] = d_gate
+        dm_ref[:, up_at] = d_up
+        result[...] += mm(hidden, down)
+        back[...] += mm_nt(d_gate, in_ref[:, gate_at]) + mm_nt(d_up, in_ref[:, up_at])
+        return carry
+
+    lax.fori_loop(0, units // step, body, 0)
+
+
+def block_kernel(
+    nc, nz,
+    len_ref, hid_ref, go_ref, ids_ref, rank_ref, wqkv_ref, small_ref, gu_ref, wo_ref, sd_ref,
+    win_ref, wout_ref, turn_ref,
+    out_ref, gin_ref, fq_ref, fgu_ref, fsd_ref, fwo_ref, ein_ref, eout_ref,
+    hid_all, up_own, up_all, wq_own, wq_st, wq_buf, w_ref, gu_st, gu_buf, gu_all, wo_st, wo_buf,
+    wo_all, sd_all, wie, woe, normed_ref, qkv_ref, ctx_all, att_own, nt_all,
+    sb, ar, xs, ds, acc_a, acc_b, sh_own, sh_hidden, sh_dm, sh_send, rs_shared,
+    ex_hidden, ex_dm, pin, fb, rb, gsd, da_own, dctx_send, dctx_all, part, part_own, rs_in,
+    sib_gu, zi_gu, pb_gu, sib_q, zi_q, pb_q, sib_sd, zi_sd, sib_wo, zi_wo, pb_wo, in_wo,
+    send, recv, esend, erecv, gsend, grecv, lsem,
+):
+    c, z, f = place()
+    in_plane = [(wrap(c + s, nc), z, f) for s in range(1, nc)]
+    in_column = [(c, wrap(z + s, nz), f) for s in range(1, nz)]
+    sibling = (c, z, 1 - f)
+    across = [(wrap(c + s, nc), z, 1 - f) for s in range(1, nc)]
+    ring = [(dz, dc) for dz in range(nz) for dc in range(nc) if dz or dc]
+    everyone = [(wrap(c + dc, nc), wrap(z + dz, nz), f) for dz, dc in ring]
+    greet(everyone + [sibling] + across)
+
+    num_seqs, shard_len, width = hid_ref.shape
+    full_len = nc * shard_len
+    half_len = shard_len // 2
+    tok = num_seqs * shard_len
+    rows_w = wqkv_ref.shape[0]
+    head_width = wqkv_ref.shape[1] // 3 // nc
+    heads_here = head_width // HS
+    wide_cols = wq_own.shape[2]
+    units = gu_ref.shape[1] // 2
+    own_units = units // nc
+    down_rows = sd_ref.shape[0]
+    num_experts = nz * nc
+    num_slots = num_experts * ROWS
+    block_rows = nz * 2 * rows_w
+    mail = Courier(send, recv)
+
+    for owner in range(nc):
+        wq_own[owner] = jnp.concatenate(
+            [
+                wqkv_ref[:, side * width + owner * head_width : side * width + (owner + 1) * head_width]
+                for side in range(3)
+            ]
+            + [small_ref[...]],
+            axis=1,
+        )
+    met(everyone + [sibling] + across)
+
+    staged_wq = [
+        mail.push(wq_own.at[wrap(c + s, nc)], wq_st.at[c], in_plane[s - 1]) for s in range(1, nc)
+    ]
+    arriving = [
+        [mail.push(hid_ref.at[q], hid_all.at[q, c], peer) for peer in in_plane]
+        for q in range(num_seqs)
+    ]
+    staged_wo = [mail.push(wo_ref, wo_st.at[c], peer) for peer in in_plane]
+    staged_gu = []
+    for s in range(1, nc):
+        owner = wrap(c + s, nc)
+        for side in range(2):
+            at = pl.ds(pl.multiple_of(side * units + owner * own_units, own_units), own_units)
+            staged_gu.append(
+                mail.push(
+                    gu_ref.at[:, at],
+                    gu_st.at[c, :, pl.ds(side * own_units, own_units)],
+                    in_plane[s - 1],
+                )
+            )
+
+    block = 2 * c + f
+    shard_rows = win_ref.shape[1]
+    half_units = units // 2
+    lands = pl.ds(pl.multiple_of(block * shard_rows, shard_rows), shard_rows)
+    expert_in, own_in = [], []
+    for s in range(nc):
+        owner = wrap(c + s, nc)
+        for g in range(2):
+            core = f if g == 0 else 1 - f
+            for side in range(2):
+                from_lane = pl.multiple_of(side * units + core * half_units, half_units)
+                src = win_ref.at[owner, :, pl.ds(from_lane, half_units)]
+                dst = wie.at[lands, pl.ds(side * half_units, half_units)]
+                if s == 0 and g == 0:
+                    own_in.append(pltpu.make_async_copy(src, dst, lsem.at[side]))
+                    own_in[-1].start()
+                else:
+                    expert_in.append(mail.push(src, dst, (owner, z, core)))
+    out_rows = wout_ref.shape[1]
+    to_core = block // nc
+    slot = wrap(block, nc)
+    out_lands = pl.ds(pl.multiple_of(slot * out_rows, out_rows), out_rows)
+
+    def out_copy(s, device, to_slot, lands_at):
+        return pltpu.make_async_remote_copy(
+            src_ref=wout_ref.at[wrap(c + s, nc)],
+            dst_ref=woe.at[lands_at],
+            send_sem=esend.at[s],
+            recv_sem=erecv.at[to_slot],
+            device_id=device,
+            device_id_type=MESH,
+        )
+
+    for s in range(1, nc):
+        out_copy(s, (wrap(c + s, nc), z, to_core), slot, out_lands).start()
+    own_out = pltpu.make_async_copy(wout_ref.at[c], woe.at[out_lands], lsem.at[2])
+
+    @pl.when(to_core == f)
+    def _():
+        own_out.start()
+
+    @pl.when(to_core != f)
+    def _():
+        out_copy(0, sibling, slot, out_lands).start()
+
+    row_at = lax.broadcasted_iota(jnp.int32, (tok, 1), 0)
+    inside = row_at & (shard_len - 1)
+    low = c * half_len + (inside & (half_len - 1))
+    places = jnp.where(inside >= half_len, full_len - 1 - low, low)
+    lengths = jnp.zeros((tok, 1), jnp.int32)
+    for q in range(num_seqs):
+        lengths = jnp.where(row_at // shard_len == q, len_ref[q], lengths)
+    live = (places < lengths).astype(F32)
+    lane = lax.broadcasted_iota(jnp.int32, (tok, 128), 1).astype(F32)
+    picked = ids_ref[...].astype(F32)
+    hots = [(lane == SMALL + picked[:, k : k + 1]).astype(F32) for k in range(2)]
+    rank_row = jnp.broadcast_to(rank_ref[...].astype(F32), (tok, tok))
+    earlier = (rank_row < jnp.transpose(rank_row, (1, 0))).astype(BF)
+    position = mm(earlier, ((hots[0] + hots[1]) * live).astype(BF))
+    slot_lane = lax.broadcasted_iota(jnp.int32, (tok, num_slots), 1).astype(F32)
+    dispatch = []
+    for k in range(2):
+        at = jnp.sum(hots[k] * position, axis=1, keepdims=True)
+        slot_at = jnp.where((live > 0) & (at < CAP), picked[:, k : k + 1] * ROWS + at, -1.0)
+        dispatch.append((slot_lane == slot_at).astype(BF))
+    anyone = dispatch[0] + dispatch[1]
+    upstream = go_ref[...].reshape(tok, width).astype(F32) * live
+    up_b = upstream.astype(BF)
+    up_f = up_b.astype(F32)
+    up_own[...] = up_b.reshape(num_seqs, shard_len, width)
+    up_copies = [mail.push(up_own, up_all.at[:, c], peer) for peer in in_plane]
+    for q in range(num_seqs):
+        hid_all[q, c] = hid_ref[q]
+        up_all[q, c] = up_own[q]
+
+    own_down = pl.ds(pl.multiple_of((z * 2 + f) * down_rows, down_rows), down_rows)
+    sd_all[own_down] = sd_ref[...]
+
+    def spread(stage, staged, buffer):
+        for copy in staged:
+            copy.wait_recv()
+        copies = [mail.push(stage, buffer.at[:, z, f], peer) for peer in in_column]
+        copies.append(mail.push(stage, buffer.at[:, z, f], sibling))
+        for i in range(nc):
+            buffer[i, z, f] = stage[i]
+        return copies
+
+    def forward(copies, buffer):
+        passed = []
+        for s in range(1, nz):
+            origin = wrap(z + nz - s, nz)
+            copies[s - 1].wait_recv()
+            passed.append(
+                mail.push(buffer.at[:, origin, f], buffer.at[:, origin, f], sibling)
+            )
+        return passed
+
+    with jax.named_scope("a_stage_wq"):
+        wq_st[c] = wq_own[c]
+        spread_wq = spread(wq_st, staged_wq, wq_buf)
+    with jax.named_scope("a_stage_wo"):
+        wo_st[c] = wo_ref[...]
+        spread_wo = spread(wo_st, staged_wo, wo_buf)
+    with jax.named_scope("a_stage_gu"):
+        for side in range(2):
+            at = pl.ds(pl.multiple_of(side * units + c * own_units, own_units), own_units)
+            gu_st[c, :, side * own_units : (side + 1) * own_units] = gu_ref[:, at]
+        spread_gu = spread(gu_st, staged_gu, gu_buf)
+    spread_sd = [mail.push(sd_ref, sd_all.at[own_down], peer) for peer in in_column]
+    spread_sd.append(mail.push(sd_ref, sd_all.at[own_down], sibling))
+    with jax.named_scope("a_forward_wq"):
+        passed_wq = forward(spread_wq, wq_buf)
+        for copy in passed_wq + spread_wq[-1:]:
+            copy.wait_recv()
+        for i in range(nc):
+            w_ref[i * block_rows : (i + 1) * block_rows, :] = join(
+                wq_buf[i], (block_rows, wide_cols)
+            )
+
+    cosines = wide(turn_ref[:, :128], 2 * head_width // 128)
+    sines = wide(turn_ref[:, 128:], 2 * head_width // 128)
+    tail_at = wide_cols - 128
+    attn_gain = column_row(w_ref[:, tail_at:], SMALL + num_experts)
+    ctx_copies = []
+    for q in range(num_seqs):
+        with jax.named_scope("a_wait_hidden"):
+            for copy in arriving[q]:
+                copy.wait_recv()
+        with jax.named_scope("a_attention"):
+            rows = hid_all[q].reshape(full_len, width).astype(F32)
+            normed = (rows * inverse_rms(rows) * attn_gain).astype(BF)
+            normed_ref[q] = normed
+            merged = mm(normed, w_ref[:, : 3 * head_width])
+            both = merged[:, : 2 * head_width]
+            both = (both * cosines + swap_halves(both) * sines).astype(BF)
+            values = merged[:, 2 * head_width :].astype(BF)
+            qkv_ref[q, :, : 2 * head_width] = both
+            qkv_ref[q, :, 2 * head_width :] = values
+            allowed = allowed_keys(len_ref[q], half_len, full_len)
+            heads = []
+            for h in range(heads_here):
+                probs = head_probs(
+                    both[:, h * HS : (h + 1) * HS],
+                    both[:, head_width + h * HS : head_width + (h + 1) * HS],
+                    allowed,
+                ).astype(BF)
+                heads.append(mm(probs, values[:, h * HS : (h + 1) * HS]))
+            context = jnp.concatenate(heads, axis=1).astype(BF)
+            ctx_all[c, q] = context.reshape(nc, shard_len, head_width)
+        ctx_copies.append(
+            [mail.push(ctx_all.at[c, q], ctx_all.at[c, q], peer) for peer in in_plane]
+        )
+    with jax.named_scope("a_forward_wo"):
+        passed_wo = forward(spread_wo, wo_buf)
+        for copy in passed_wo + spread_wo[-1:]:
+            copy.wait_recv()
+        for i in range(nc):
+            wo_all[i * block_rows : (i + 1) * block_rows, :] = join(
+                wo_buf[i], (block_rows, width)
+            )
+    ffn_gain = column_row(w_ref[:, tail_at:], SMALL + num_experts + 1)
+    for q in range(num_seqs):
+        with jax.named_scope("a_wait_context"):
+            for copy in ctx_copies[q]:
+                copy.wait_recv()
+        with jax.named_scope("a_project"):
+            total = hid_all[q].reshape(full_len, width).astype(F32)
+            for i in range(nc):
+                total = total + mm(
+                    ctx_all[i, q].reshape(full_len, head_width),
+                    wo_all[i * head_width : (i + 1) * head_width, :],
+                )
+            acc_a[q * full_len : (q + 1) * full_len] = total
+            nt_all[q] = (
+                (total * inverse_rms(total) * ffn_gain).astype(BF).reshape(nc, shard_len, width)
+            )
+    by_block = acc_a.reshape(num_seqs, nc, shard_len, width)
+    for q in range(num_seqs):
+        att_own[q] = by_block[q, c]
+
+    with jax.named_scope("b_dispatch"):
+        normed = jnp.concatenate([nt_all[q, c] for q in range(num_seqs)], axis=0)
+        tail = w_ref[:, tail_at:]
+        logits = mm(normed, tail)
+        chosen = [jnp.sum(hot * logits, axis=1, keepdims=True) for hot in hots]
+        top = jnp.maximum(chosen[0], chosen[1])
+        raised = [jnp.exp(value - top) for value in chosen]
+        gates = [value / (raised[0] + raised[1]) for value in raised]
+        weighted = [(gates[k] * up_f).astype(BF) for k in range(2)]
+        rows_out = mm_tn(anyone, normed)
+        grads_out = mm_tn(dispatch[0], weighted[0]) + mm_tn(dispatch[1], weighted[1])
+        sb[:, 0] = rows_out.reshape(num_experts, ROWS, width).astype(BF)
+        sb[:, 1] = grads_out.reshape(num_experts, ROWS, width).astype(BF)
+        row_copies = [
+            mail.push(sb.at[to[1] * nc + to[0]], ar.at[f, z, c], to) for to in everyone
+        ]
+        ar[f, z, c] = sb[z * nc + c]
+        forwards = [mail.push(sb.at[z * nc + c], ar.at[f, z, c], sibling)]
+
+    with jax.named_scope("b_forward_gu"):
+        passed_gu = forward(spread_gu, gu_buf)
+        passed_sd = []
+        for s in range(1, nz):
+            origin = wrap(z + nz - s, nz)
+            spread_sd[s - 1].wait_recv()
+            at = pl.ds(pl.multiple_of((origin * 2 + f) * down_rows, down_rows), down_rows)
+            passed_sd.append(mail.push(sd_all.at[at], sd_all.at[at], sibling))
+        for copy in passed_gu + spread_gu[-1:] + passed_sd + spread_sd[-1:]:
+            copy.wait_recv()
+        for i in range(nc):
+            gu_all[i * block_rows : (i + 1) * block_rows, :] = join(
+                gu_buf[i], (block_rows, 2 * own_units)
+            )
+    with jax.named_scope("b_wait_upstream"):
+        for copy in up_copies:
+            copy.wait_recv()
+    plane_tok = nc * tok
+    shared_rows = nt_all.reshape(plane_tok, width)
+    shared_grads = up_all.reshape(plane_tok, width)
+    with jax.named_scope("b_shared"):
+        first = pl.ds(0, plane_tok)
+        ffn_pass(
+            shared_rows, shared_grads, gu_all, sd_all, sh_hidden, sh_dm,
+            acc_a.at[first], acc_b.at[first], own_units, 256,
+        )
+        for k, acc in enumerate((acc_a, acc_b)):
+            cut = acc.reshape(num_seqs, nc, shard_len, width)
+            for q in range(num_seqs):
+                sh_own[k, q] = cut[q, c]
+            sh_send[k] = cut[...].astype(BF)
+    shared_copies = [
+        mail.push(sh_send.at[:, :, wrap(c + s, nc)], rs_shared.at[s - 1], in_plane[s - 1])
+        for s in range(1, nc)
+    ]
+
+    with jax.named_scope("b_forward_rows"):
+        for copy, (dz, dc) in zip(row_copies, ring):
+            copy.wait_recv()
+            oz, oc = wrap(z + nz - dz, nz), wrap(c + nc - dc, nc)
+            forwards.append(mail.push(ar.at[f, oz, oc], ar.at[f, oz, oc], sibling))
+        for copy in forwards:
+            copy.wait_recv()
+        for core in range(2):
+            at = slice(core * num_slots, (core + 1) * num_slots)
+            xs[at] = join(ar[core, :, :, 0], (num_slots, width))
+            ds[at] = join(ar[core, :, :, 1], (num_slots, width))
+    with jax.named_scope("b_wait_experts"):
+        for copy in own_in:
+            copy.wait()
+        for copy in expert_in:
+            copy.wait_recv()
+        for at in range(nc):
+
+            @pl.when(f * nc + at != block)
+            def _(at=at):
+                out_copy(0, sibling, at, pl.ds(at * out_rows, out_rows)).wait_recv()
+
+        @pl.when(to_core == f)
+        def _():
+            own_out.wait()
+
+    mail.settle(row_copies + forwards[:1])
+    pr = sb
+    acc = [ref.at[pl.ds(0, num_slots)] for ref in (acc_a, acc_b)]
+    for turn in range(2):
+        core = 1 - f if turn == 0 else f
+        at = pl.ds(pl.multiple_of(core * num_slots, num_slots), num_slots)
+        with jax.named_scope("b_experts"):
+            ffn_pass(
+                xs.at[at], ds.at[at], wie, woe, ex_hidden.at[at], ex_dm.at[at],
+                acc[0], acc[1], half_units, 256,
+            )
+        if turn == 0:
+            for k in range(2):
+                pr[:, k] = acc[k][...].reshape(num_experts, ROWS, width).astype(BF)
+            swap = mail.push(pr, pin, sibling)
+    with jax.named_scope("b_sibling_sum"):
+        swap.wait_recv()
+        for k in range(2):
+            fb[:, k] = (
+                acc[k][...].reshape(num_experts, ROWS, width) + pin[:, k].astype(F32)
+            ).astype(BF)
+        returns = [
+            mail.push(fb.at[to[1] * nc + to[0]], rb.at[z * nc + c], to) for to in everyone
+        ]
+        rb[z * nc + c] = fb[z * nc + c]
+
+    gwi, gwo = wie, woe
+
+    def expert_grads(j, carry):
+        at = pl.ds(pl.multiple_of(j * 256, 256), 256)
+        gwi[:, at] = mm_tn(xs[...], ex_dm[:, at]).astype(BF)
+        return carry
+
+    home_in, home_own = [], []
+    for side in range(2):
+        steps = half_units // 256
+        with jax.named_scope("b_gwi"):
+            lax.fori_loop(side * steps, (side + 1) * steps, expert_grads, 0)
+        for s in range(nc):
+            owner = wrap(c + s, nc)
+            for g in range(2):
+                core = f if g == 0 else 1 - f
+                from_rows = pl.ds(
+                    pl.multiple_of((2 * owner + core) * shard_rows, shard_rows), shard_rows
+                )
+                to_lane = pl.multiple_of(side * units + f * half_units, half_units)
+                src = gwi.at[from_rows, pl.ds(side * half_units, half_units)]
+                dst = ein_ref.at[c, :, pl.ds(to_lane, half_units)]
+                if s == 0 and g == 0:
+                    home_own.append(pltpu.make_async_copy(src, dst, lsem.at[3 + side]))
+                    home_own[-1].start()
+                else:
+                    home_in.append(mail.push(src, dst, (owner, z, core)))
+
+    def home_out(j, arrives):
+        to_block = f * nc + j
+        return pltpu.make_async_remote_copy(
+            src_ref=gwo.at[pl.ds(j * out_rows, out_rows)],
+            dst_ref=eout_ref.at[arrives],
+            send_sem=gsend.at[j],
+            recv_sem=grecv.at[arrives],
+            device_id=(to_block // 2, z, wrap(to_block, 2)),
+            device_id_type=MESH,
+        )
+
+    def home_out_own(j):
+        return pltpu.make_async_copy(
+            gwo.at[pl.ds(j * out_rows, out_rows)], eout_ref.at[c], lsem.at[5]
+        )
+
+    with jax.named_scope("b_gwo"):
+        for j in range(nc):
+            gwo[j * out_rows : (j + 1) * out_rows, :] = mm_tn(
+                ex_hidden[:, j * out_rows : (j + 1) * out_rows], ds[...]
+            ).astype(BF)
+
+            @pl.when(f * nc + j == block)
+            def _(j=j):
+                home_out_own(j).start()
+
+            @pl.when(f * nc + j != block)
+            def _(j=j):
+                home_out(j, c).start()
+
+    mail.settle(spread_gu + passed_gu)
+    ggu = gu_buf
+    with jax.named_scope("b_shared_grads"):
+
+        def gate_up_grads(j, carry):
+            at = pl.ds(pl.multiple_of(j * 256, 256), 256)
+            piece = mm_tn(shared_rows[...], sh_dm[:, at])
+            ggu[:, :, :, :, at] = piece.reshape(ggu.shape[:4] + (256,)).astype(BF)
+            return carry
+
+        lax.fori_loop(0, 2 * own_units // 256, gate_up_grads, 0)
+        gsd[...] = mm_tn(sh_hidden[...], shared_grads[...]).reshape(gsd.shape).astype(BF)
+        sibling_gu = mail.push(ggu.at[:, :, 1 - f], sib_gu, sibling)
+        sibling_sd = mail.push(gsd.at[:, 1 - f], sib_sd, sibling)
+
+    with jax.named_scope("c_wait_shared"):
+        shared, d_normed = [sh_own[k].reshape(tok, width) for k in range(2)]
+        for s in range(1, nc):
+            shared_copies[s - 1].wait_recv()
+            shared = shared + rs_shared[s - 1, 0].reshape(tok, width).astype(F32)
+            d_normed = d_normed + rs_shared[s - 1, 1].reshape(tok, width).astype(F32)
+    with jax.named_scope("c_wait_returns"):
+        for copy in returns:
+            copy.wait_recv()
+    with jax.named_scope("c_combine"):
+        attended = att_own[...].reshape(tok, width)
+        inverse = inverse_rms(attended)
+        results = join(rb[:, 0], (num_slots, width))
+        d_rows = join(rb[:, 1], (num_slots, width))
+        routed = [mm(dispatch[k], results) for k in range(2)]
+        mixture = gates[0] * routed[0] + gates[1] * routed[1]
+        out_ref[...] = (
+            (live * (attended + mixture + shared)).astype(BF).reshape(out_ref.shape)
+        )
+        d_gates = [jnp.sum(routed[k] * up_f, axis=1, keepdims=True) for k in range(2)]
+        mean_gate = gates[0] * d_gates[0] + gates[1] * d_gates[1]
+        d_logits = hots[0] * (gates[0] * (d_gates[0] - mean_gate)) + hots[1] * (
+            gates[1] * (d_gates[1] - mean_gate)
+        )
+        d_normed = d_normed + mm(anyone, d_rows) + split_dot(mm_nt, d_logits, tail)
+        d_attended = upstream + norm_back(attended, inverse, d_normed * ffn_gain)
+        d_att_b = d_attended.astype(BF)
+        d_context = mm_nt(d_att_b, wo_all[...]).astype(BF)
+        for i in range(nc):
+            dctx_send[i] = d_context[:, i * head_width : (i + 1) * head_width].reshape(
+                num_seqs, shard_len, head_width
+            )
+        for q in range(num_seqs):
+            dctx_all[q, c] = dctx_send[c, q]
+        dctx_copies = [
+            mail.push(dctx_send.at[wrap(c + s, nc)], dctx_all.at[:, c], in_plane[s - 1])
+            for s in range(1, nc)
+        ]
+        gin_ref[...] = d_attended.reshape(gin_ref.shape)
+
+    mail.settle(spread_wo + passed_wo)
+    gwo_at = wo_buf
+    with jax.named_scope("c_reduce"):
+        def two_cores(copy, own, inbox):
+            copy.wait_recv()
+            inbox[...] = (own.astype(F32) + inbox[...].astype(F32)).astype(BF)
+
+        def four_planes(copy, buffer, inbox):
+            copy.wait_recv()
+            for i in range(nc):
+                inbox[i] = (buffer[i, :, f].astype(F32) + inbox[i].astype(F32)).astype(BF)
+
+        for i in range(nc):
+            mine = jnp.concatenate([ctx_all[i, q, c] for q in range(num_seqs)], axis=0)
+            gwo_at[i] = mm_tn(mine, d_att_b).reshape(gwo_at.shape[1:]).astype(BF)
+        sibling_wo = mail.push(gwo_at.at[:, :, 1 - f], sib_wo, sibling)
+        d_router = split_dot(mm_tn, normed, d_logits, left_wide=False)
+        d_gain = jnp.sum(d_normed * attended * inverse, axis=0, keepdims=True)
+        turned = jnp.transpose(jnp.broadcast_to(d_gain, (128, width)), (1, 0))
+        extra_lane = lax.broadcasted_iota(jnp.int32, (width, 128), 1)
+        extras = jnp.where(extra_lane == SMALL + num_experts + 1, turned, d_router)
+        four_planes(sibling_gu, ggu, sib_gu)
+        two_cores(sibling_sd, gsd[:, f], sib_sd)
+        gu_copies = [
+            mail.push(sib_gu.at[:, wrap(z + s, nz)], zi_gu.at[s - 1], in_column[s - 1])
+            for s in range(1, nz)
+        ]
+        sd_copies = [
+            mail.push(sib_sd.at[wrap(z + s, nz)], zi_sd.at[s - 1], in_column[s - 1])
+            for s in range(1, nz)
+        ]
+        four_planes(sibling_wo, gwo_at, sib_wo)
+        wo_copies = [
+            mail.push(sib_wo.at[:, wrap(z + s, nz)], zi_wo.at[s - 1], in_column[s - 1])
+            for s in range(1, nz)
+        ]
+
+    with jax.named_scope("c_wait_dctx"):
+        for copy in dctx_copies:
+            copy.wait_recv()
+    grad_qkv = jnp.zeros((width, 3 * head_width), F32)
+    parting = []
+    for q in range(num_seqs):
+        with jax.named_scope("c_attention"):
+            d_context = dctx_all[q].reshape(full_len, head_width)
+            allowed = allowed_keys(len_ref[q], half_len, full_len)
+            merged = qkv_ref[q]
+            d_query, d_key, d_value = [], [], []
+            for h in range(heads_here):
+                query = merged[:, h * HS : (h + 1) * HS]
+                key = merged[:, head_width + h * HS : head_width + (h + 1) * HS]
+                value = merged[:, 2 * head_width + h * HS : 2 * head_width + (h + 1) * HS]
+                d_head = d_context[:, h * HS : (h + 1) * HS]
+                probs = head_probs(query, key, allowed)
+                d_probs = mm_nt(d_head, value)
+                delta = jnp.sum(probs * d_probs, axis=1, keepdims=True)
+                d_scores = (probs * (d_probs - delta)).astype(BF)
+                d_query.append(mm(d_scores, key) * (HS**-0.5))
+                d_key.append(mm_tn(d_scores, query) * (HS**-0.5))
+                d_value.append(mm_tn(probs.astype(BF), d_head))
+            both = jnp.concatenate(d_query + d_key, axis=1)
+            both = both * cosines - swap_halves(both) * sines
+            d_merged = jnp.concatenate([both] + d_value, axis=1).astype(BF)
+            product = mm_nt(d_merged, w_ref[:, : 3 * head_width]).reshape(nc, shard_len, width)
+            part_own[q] = product
+            part[q] = product.astype(BF)
+            parting.append(
+                [
+                    mail.push(part.at[q, wrap(c + s, nc)], rs_in.at[s - 1, q], in_plane[s - 1])
+                    for s in range(1, nc)
+                ]
+            )
+            grad_qkv = grad_qkv + mm_tn(normed_ref[q], d_merged)
+    mail.settle(spread_wq + passed_wq)
+    gq = wq_buf
+    with jax.named_scope("c_reduce_q"):
+        last = jnp.concatenate([grad_qkv[:, tail_at:], extras[:, 3 * head_width - tail_at :]], axis=1)
+        gq[...] = (
+            jnp.concatenate([grad_qkv[:, :tail_at], last], axis=1).reshape(gq.shape).astype(BF)
+        )
+        sibling_q = mail.push(gq.at[:, :, 1 - f], sib_q, sibling)
+        four_planes(sibling_q, gq, sib_q)
+        q_copies = [
+            mail.push(sib_q.at[:, wrap(z + s, nz)], zi_q.at[s - 1], in_column[s - 1])
+            for s in range(1, nz)
+        ]
+
+    def column_sum(own, copies, inbox):
+        total = own.astype(F32)
+        for s in range(1, nz):
+            copies[s - 1].wait_recv()
+            total = total + inbox[s - 1].astype(F32)
+        return total
+
+    def hand_out(box, final):
+        final[c] = box[c]
+        return [
+            mail.push(box.at[wrap(c + s, nc)], final.at[c], in_plane[s - 1])
+            for s in range(1, nc)
+        ]
+
+    with jax.named_scope("c_column_gu"):
+        pb_gu[...] = column_sum(sib_gu[:, z], gu_copies, zi_gu).astype(BF)
+        final_gu = hand_out(pb_gu, fgu_ref)
+    with jax.named_scope("c_column_sd"):
+        fsd_ref[...] = column_sum(sib_sd[z], sd_copies, zi_sd)
+    with jax.named_scope("c_column_wo"):
+        pb_wo[...] = column_sum(sib_wo[:, z], wo_copies, zi_wo).astype(BF)
+        final_wo = hand_out(pb_wo, in_wo)
+    with jax.named_scope("c_column_q"):
+        pb_q[...] = column_sum(sib_q[:, z], q_copies, zi_q).astype(BF)
+        final_q = hand_out(pb_q, fq_ref)
+    with jax.named_scope("c_grad_in"):
+        for q in range(num_seqs):
+            d_normed = part_own[q, c]
+            for s in range(1, nc):
+                parting[q][s - 1].wait_recv()
+                d_normed = d_normed + rs_in[s - 1, q].astype(F32)
+            rows = hid_ref[q].astype(F32)
+            gin_ref[q] = gin_ref[q] + norm_back(rows, inverse_rms(rows), d_normed * attn_gain)
+    with jax.named_scope("c_final"):
+        for copy in final_wo:
+            copy.wait_recv()
+        fwo_ref[...] = jnp.sum(in_wo[...].astype(F32), axis=0)
+        for copy in final_gu + final_q:
+            copy.wait_recv()
+    with jax.named_scope("c_wait_home"):
+        for copy in home_own:
+            copy.wait()
+        for copy in home_in:
+            copy.wait_recv()
+        for arrives in range(nc):
+
+            @pl.when((arrives != c) | (to_core != f))
+            def _(arrives=arrives):
+                home_out(0, arrives).wait_recv()
+
+        for j in range(nc):
+
+            @pl.when(f * nc + j == block)
+            def _(j=j):
+                home_out_own(j).wait()
+
+            @pl.when(f * nc + j != block)
+            def _(j=j):
+                home_out(j, c).wait_send()
+
+        @pl.when(to_core != f)
+        def _():
+            out_copy(0, sibling, slot, out_lands).wait_send()
+
+        for s in range(1, nc):
+            out_copy(s, (wrap(c + s, nc), z, to_core), slot, out_lands).wait_send()
+        mail.finish()
+
+
+def finish_kernel(
+    nc, fq_ref, fgu_ref, wqkv_ref, ga_ref, ein_ref, eout_ref, out_in, gin_in, fsd_in, fwo_in,
+    gq_ref, gr_ref, gains_ref, ggu_ref, oin_ref, oout_ref, out_ref, gin_ref, fsd_ref, fwo_ref,
+):
+    oin_ref[...] = ein_ref[...].astype(F32)
+    oout_ref[...] = eout_ref[...].astype(F32)
+
+    @pl.when(pl.program_id(0) == 0)
+    def _():
+        out_ref[...] = out_in[...]
+        gin_ref[...] = gin_in[...]
+        fsd_ref[...] = fsd_in[...]
+        fwo_ref[...] = fwo_in[...]
+        rows_w = wqkv_ref.shape[0]
+        head_width = wqkv_ref.shape[1] // 3 // nc
+        grads = jnp.concatenate(
+            [
+                fq_ref[i, :, side * head_width : (side + 1) * head_width].astype(F32)
+                for side in range(3)
+                for i in range(nc)
+            ],
+            axis=1,
+        )
+        gq_ref[...] = grads
+        own_units = fgu_ref.shape[2] // 2
+        ggu_ref[...] = jnp.concatenate(
+            [
+                fgu_ref[i, :, side * own_units : (side + 1) * own_units].astype(F32)
+                for side in range(2)
+                for i in range(nc)
+            ],
+            axis=1,
+        )
+        extras = jnp.sum(fq_ref[:, :, 3 * head_width - SMALL :].astype(F32), axis=0)
+        num_experts = gr_ref.shape[1]
+        gr_ref[...] = extras[:, SMALL : SMALL + num_experts]
+        first = jnp.sum(wqkv_ref[...].astype(F32) * grads, axis=1, keepdims=True)
+        lane = lax.broadcasted_iota(jnp.int32, (rows_w, 128), 1)
+        both = jnp.where(lane == SMALL + num_experts, first, extras)
+        turned = jnp.transpose(
+            jnp.concatenate([both, jnp.zeros((128 - rows_w, 128), F32)], axis=0), (1, 0)
+        )
+        gain = ga_ref[...].astype(F32)
+        at = SMALL + num_experts
+        gains_ref[0:1, :] = turned[at : at + 1, :rows_w] / gain
+        gains_ref[1:2, :] = turned[at + 1 : at + 2, :rows_w]
+
+
+def vmem(*shape, dtype=jnp.bfloat16):
+    return pltpu.VMEM(shape, dtype)
+
+
+def fast_device(
+    hidden_in, seq_lengths, expert_ids, route_rank, gain_attn, w_qkv, w_out, w_router, gain_ffn,
+    w_gate_up, w_shared_down, w_experts_in, w_experts_out, grad_output,
+):
+    nc, nz = lax.axis_size("ctx"), lax.axis_size("exp")
+    num_seqs, two_ends, half_len, width = hidden_in.shape
+    shard_len = 2 * half_len
+    full_len = nc * shard_len
+    tok = num_seqs * shard_len
+    rows_w = w_qkv.shape[0]
+    head_width = w_qkv.shape[1] // 3 // nc
+    num_experts = w_router.shape[1]
+    down_rows = w_shared_down.shape[0]
+    own_units = w_gate_up.shape[1] // 2 // nc
+    half_units = w_experts_in.shape[2] // 4
+    hbm, vm, sm = pl.ANY, pltpu.VMEM, pltpu.SMEM
+    dma = pltpu.SemaphoreType.DMA
+
+    small = jnp.concatenate([w_router, gain_attn[:, None], gain_ffn[:, None]], axis=1)
+    small = jnp.pad(small, ((0, 0), (0, SMALL - small.shape[1])))
+    every = jnp.arange(full_len, dtype=jnp.int32)
+    inside = every % shard_len
+    low = every // shard_len * half_len + inside % half_len
+    cosines, sines = rope_tables(jnp.where(inside >= half_len, full_len - 1 - low, low))
+    turns = jnp.concatenate([cosines] * 4 + [sines] * 4, axis=1)
+
+    seq_shape = (num_seqs, shard_len, width)
+    group_shape = (num_seqs, nc, shard_len, width)
+    blocks = (nc, nz, 2, rows_w)
+    half_blocks = (nc, nz, rows_w)
+    wide_cols = 3 * head_width + SMALL
+    num_slots = num_experts * ROWS
+    row_box = (num_experts, 2, ROWS, width)
+    plane_tok = nc * tok
+    outs = [
+        (seq_shape, BF),
+        (seq_shape, F32),
+        ((nc, rows_w, wide_cols), BF),
+        ((nc, rows_w, 2 * own_units), BF),
+        ((down_rows, width), F32),
+        ((rows_w, width), F32),
+        (w_experts_in.shape, BF),
+        (w_experts_out.shape, BF),
+    ]
+    out, gin, fq, fgu, fsd, fwo, ein, eout = pl.pallas_call(
+        functools.partial(block_kernel, nc, nz),
+        out_shape=[jax.ShapeDtypeStruct(shape, dtype) for shape, dtype in outs],
+        in_specs=[
+            pl.BlockSpec(memory_space=space) for space in [sm] + [vm] * 9 + [hbm, hbm, vm]
+        ],
+        out_specs=[pl.BlockSpec(memory_space=space) for space in [vm] * 6 + [hbm, hbm]],
+        scratch_shapes=[
+            vmem(*group_shape),
+            vmem(*seq_shape),
+            vmem(*group_shape),
+            vmem(nc, rows_w, wide_cols),
+            vmem(nc, rows_w, wide_cols),
+            vmem(*blocks, wide_cols),
+            vmem(width, wide_cols),
+            vmem(nc, rows_w, 2 * own_units),
+            vmem(*blocks, 2 * own_units),
+            vmem(width, 2 * own_units),
+            vmem(nc, rows_w, width),
+            vmem(*blocks, width),
+            vmem(width, width),
+            vmem(own_units, width),
+            vmem(width, 2 * half_units),
+            vmem(half_units, width),
+            vmem(num_seqs, full_len, width),
+            vmem(num_seqs, full_len, 3 * head_width),
+            vmem(nc, num_seqs, nc, shard_len, head_width),
+            vmem(*seq_shape, dtype=F32),
+            vmem(*group_shape),
+            vmem(*row_box),
+            vmem(2, nz, nc, 2, ROWS, width),
+            vmem(2 * num_slots, width),
+            vmem(2 * num_slots, width),
+            vmem(plane_tok, width, dtype=F32),
+            vmem(plane_tok, width, dtype=F32),
+            vmem(2, *seq_shape, dtype=F32),
+            vmem(plane_tok, own_units),
+            vmem(plane_tok, 2 * own_units),
+            vmem(2, *group_shape),
+            vmem(nc - 1, 2, *seq_shape),
+            vmem(2 * num_slots, half_units),
+            vmem(2 * num_slots, 2 * half_units),
+            vmem(*row_box),
+            vmem(*row_box),
+            vmem(*row_box),
+            vmem(nz, 2, down_rows, width),
+            vmem(*seq_shape),
+            vmem(nc, num_seqs, shard_len, head_width),
+            vmem(num_seqs, nc, shard_len, head_width),
+            vmem(*group_shape),
+            vmem(*group_shape, dtype=F32),
+            vmem(nc - 1, *seq_shape),
+            vmem(*half_blocks, 2 * own_units),
+            vmem(nz - 1, nc, rows_w, 2 * own_units),
+            vmem(nc, rows_w, 2 * own_units),
+            vmem(*half_blocks, wide_cols),
+            vmem(nz - 1, nc, rows_w, wide_cols),
+            vmem(nc, rows_w, wide_cols),
+            vmem(nz, down_rows, width),
+            vmem(nz - 1, down_rows, width),
+            vmem(*half_blocks, width),
+            vmem(nz - 1, nc, rows_w, width),
+            vmem(nc, rows_w, width),
+            vmem(nc, rows_w, width),
+            dma((200,)),
+            dma((200,)),
+            dma((nc,)),
+            dma((nc,)),
+            dma((nc,)),
+            dma((nc,)),
+            dma((6,)),
+        ],
+        compiler_params=pltpu.CompilerParams(
+            collective_id=0, has_side_effects=True, vmem_limit_bytes=VMEM_BYTES
+        ),
+        cost_estimate=pl.CostEstimate(
+            flops=16_000_000_000, bytes_accessed=30_000_000, transcendentals=0
+        ),
+        name="block_forward_backward",
+    )(
+        seq_lengths,
+        hidden_in.reshape(seq_shape),
+        grad_output.reshape(seq_shape),
+        expert_ids.reshape(tok, 2),
+        route_rank.reshape(1, tok),
+        w_qkv, small, w_gate_up, w_out, w_shared_down, w_experts_in, w_experts_out, turns,
+    )
+
+    def whole(shape):
+        return pl.BlockSpec(shape, lambda e: (0,) * len(shape))
+
+    def one(shape):
+        return pl.BlockSpec((1,) + shape[1:], lambda e: (e, 0, 0))
+
+    ins = [fq, fgu, w_qkv, gain_attn.reshape(1, rows_w), ein, eout, out, gin, fsd, fwo]
+    results = [
+        (w_qkv.shape, F32),
+        (w_router.shape, F32),
+        ((2, rows_w), F32),
+        (w_gate_up.shape, F32),
+        (ein.shape, F32),
+        (eout.shape, F32),
+        (seq_shape, BF),
+        (seq_shape, F32),
+        (fsd.shape, F32),
+        (fwo.shape, F32),
+    ]
+    grad_qkv, grad_router, gains, grad_gu, grad_in, grad_out, out, gin, fsd, fwo = pl.pallas_call(
+        functools.partial(finish_kernel, nc),
+        grid=(ein.shape[0],),
+        out_shape=[jax.ShapeDtypeStruct(shape, dtype) for shape, dtype in results],
+        in_specs=[one(x.shape) if i in (4, 5) else whole(x.shape) for i, x in enumerate(ins)],
+        out_specs=[
+            one(shape) if i in (4, 5) else whole(shape) for i, (shape, _) in enumerate(results)
+        ],
+        compiler_params=pltpu.CompilerParams(vmem_limit_bytes=VMEM_BYTES),
+        name="widen_gradients",
+    )(*ins)
+    return (
+        out.reshape(hidden_in.shape),
+        gin.reshape(hidden_in.shape),
+        gains[0],
+        grad_qkv,
+        fwo,
+        grad_router,
+        gains[1],
+        grad_gu,
+        fsd,
+        grad_in,
+        grad_out,
+    )
+
+
+def fits(mesh, hidden_in, w_qkv, w_router, w_gate_up, w_experts_in):
+    nc, nz, nf = mesh.shape["ctx"], mesh.shape["exp"], mesh.shape["fsdp"]
+    heads = w_qkv.shape[1] // 3 // HS
+    return (
+        nf == 2
+        and nc == 4
+        and nz == 4
+        and heads == 12
+        and w_router.shape[1] == nc * nz
+        and w_qkv.shape[0] == 768
+        and hidden_in.shape[2] == 32 * nc
+        and hidden_in.shape[0] == 2 * nz * nf
+        and hidden_in.shape[3] == 768
+        and w_gate_up.shape[1] == w_experts_in.shape[2] == 4096
+        and CAP <= ROWS
+    )
+
+
 def solution(mesh):
+    def whole(*args):
+        chosen = fast_device if fits(mesh, args[0], args[5], args[7], args[9], args[11]) else per_device
+        return placed(mesh, chosen)(*args)
+
+    return whole
+
+
+def placed(mesh, chosen):
     return jax.shard_map(
-        per_device,
+        chosen,
         mesh=mesh,
         in_specs=(
             P(("exp", "fsdp"), None, "ctx", None),

time: 1260 us -> 245 us (0.19); the launches traced: 1240 us -> 242 us
  waiting for transfers between devices: 635 us -> 0 us
  Pallas kernels: 0 us -> 233 us
  matrix products: 189 us -> 0 us
  blocking collectives: 189 us -> 0 us
  local copies, waits for them, and re-layouts: 106 us -> 7.3 us
  other arithmetic: 67.8 us -> 1.22 us
  starting transfers between devices: 26.3 us -> 0 us
  between operations: 15.4 us -> 0.68 us
  loops' own time: 13.9 us -> 0 us
    reduce_scatter x6 -> x0, waiting for transfers between devices: 449 us -> none  [the longest x1 162 us: per_device(): lax.psum_scatter(d_shared_in, ('ctx', 'exp', 'fsdp'), scatter_dimension=0...]
    pallas_call x0 -> x2, Pallas kernels: none -> 233 us  [the longest x1 225 us: fast_device(): pl.pallas_call(functools.partial(block_kernel, nc, nz), out_shape=[jax.Sh...]
    dot_general x62 -> x0, matrix products: 189 us -> none  [the longest x6 20 us: first_t(): lax.dot_general(left_side, right_side, (((0,), (0,)), ((), ())), precisio...]
    all_gather x6 -> x0, waiting for transfers between devices: 182 us -> none  [the longest x1 58.9 us: per_device(): lax.all_gather(w_experts_out, ('ctx', 'fsdp'), axis=1, tiled=True)]
    all_gather x7 -> x0, blocking collectives: 103 us -> none  [the longest x1 37.3 us: per_device(): lax.all_gather(w_router, ('ctx', 'exp', 'fsdp'), axis=0, tiled=True)]
    unnamed x2 -> x0, blocking collectives: 86.2 us -> none
    dynamic_slice x44 -> x0, local copies, waits for them, and re-layouts: 39.4 us -> none  [the longest x20 19.6 us: per_device(): lax.scan(lse_step, (jnp.full(stat_shape, masked_out, jnp.float32), jnp.ze...]
    all_to_all x4 -> x0, starting transfers between devices: 24.8 us -> none  [the longest x1 10.2 us: per_device(): lax.all_to_all(send_rows, 'exp', split_axis=0, concat_axis=0, tiled=True)]
  transfers between devices with their start and end apart: 16 -> 0, of which waited for: 8 -> 0; matrix products, arithmetic and copies ran while one was open for 29% -> 0% of each run, Pallas kernels for 0% -> 0%
where the time goes in v2:
time: 245 us; the launch traced here: 242 us
  Pallas kernels  233 us (95%)
  local copies, waits for them, and re-layouts  7.3 us (3%)
    pallas_call x1, Pallas kernels, fast_device(): pl.pallas_call(functools.partial(block_kernel, nc, nz), out_shape=[jax.Sh...  225 us
    pallas_call x1, Pallas kernels, fast_device(): pl.pallas_call(functools.partial(finish_kernel, nc), grid=(ein.shape[0],)...  7.73 us

profile of v2, /device:TPU:31, one launch (start us, length us, event | category | flops | bytes accessed | tf_op | source)
XLA Modules:
  0.0 242.0 jit_solution(10912591442651823575)
XLA Ops:
  0.7 0.8 copy.31
  1.4 0.7 copy.33
  2.2 0.7 copy.32
  2.9 0.7 fusion.4.small_ref
  3.6 1.4 copy.30
  5.0 0.5 multiply_sine_fusion
  5.6 1.0 concatenate.7.turn_ref
  6.5 225.1 %block_forward_backward.1 = (bf16[2,64,768]{2,1,0:T(8,128)(2,1)}, f32[2,64,768]{2,1,0:T(8,128)}, bf16[4,24,640]{2,1,0:T(8,128)(2,1)}, bf16[4,24,1024]{2,1,0:T(8,...) custom-call(s32[2]{0:T(128)} %len_ref.1, ...), custom_call_target="tpu_custom_call" | custom-call | flops 16000000000 | bytes 30000000 | tf_op jit(solution)/shard_map/block_forward_backward/pallas_call | solution.py:1293
  231.6 7.7 %widen_gradients.1 = (f32[24,2304]{1,0:T(8,128)}, f32[24,16]{1,0:T(8,128)}, f32[2,24]{1,0:T(2,128)}, f32[24,4096]{1,0:T(8,128)}, f32[4,96,4096]{2,1,0:T(8,128)},...) custom-call(bf16[4,24,640]{2,1,0:T(8,128)(2,1)} %get-tuple-element.2, ...), custom_call_target="tpu_custom_call" | custom-call | tf_op jit(solution)/shard_map/widen_gradients/pallas_call | solution.py:1400
  239.3 1.3 slice_bitcast_fusion
  240.6 1.4 copy.35
  (2 shorter events, 0.0 us)

commit v3 on v2

--- a/solution.py
+++ b/solution.py
@@ -1,4 +1,5 @@
 import functools
+import math
 
 import jax
 import jax.numpy as jnp
@@ -413,9 +414,13 @@
 F32 = jnp.float32
 BF = jnp.bfloat16
 MESH = pl.DeviceIdType.MESH
-ROWS = 24
+BOX = 40
 SMALL = 64
 VMEM_BYTES = 63 * 1024 * 1024
+PUMPS = (2, 10, 8)
+POSTS = 64
+HOME = 512
+WIDEN = 1
 
 
 def place():
@@ -454,30 +459,60 @@
     pl.semaphore_wait(pltpu.get_barrier_semaphore(), len(peers))
 
 
-class Courier:
-    def __init__(self, send, recv):
-        self.send, self.recv, self.count, self.sent = send, recv, 0, []
-
-    def push(self, src, dst, device):
-        index = self.count
-        self.count += 1
-        copy = pltpu.make_async_remote_copy(
+class Post:
+    def __init__(self, send, recv, like, device):
+        self.send, self.recv, self.like, self.device = send, recv, like, device
+
+    def add(self, src, dst, device):
+        pltpu.make_async_remote_copy(
             src_ref=src,
             dst_ref=dst,
-            send_sem=self.send.at[index],
-            recv_sem=self.recv.at[index],
+            send_sem=self.send,
+            recv_sem=self.recv,
             device_id=device,
             device_id_type=MESH,
-        )
-        copy.start()
-        self.sent.append(copy)
-        return copy
-
-    def settle(self, copies):
-        for copy in copies:
-            copy.wait_send()
-        done = {id(copy) for copy in copies}
-        self.sent = [copy for copy in self.sent if id(copy) not in done]
+        ).start()
+
+    def all_of_it(self, like=None):
+        like = self.like if like is None else like
+        return pltpu.make_async_remote_copy(
+            src_ref=like,
+            dst_ref=like,
+            send_sem=self.send,
+            recv_sem=self.recv,
+            device_id=self.device,
+            device_id_type=MESH,
+        )
+
+    def wait_recv(self, like=None):
+        self.all_of_it(like).wait_recv()
+
+    def wait_send(self, like=None):
+        self.all_of_it(like).wait_send()
+
+
+class Courier:
+    def __init__(self, send, recv, device):
+        self.send, self.recv, self.device, self.count, self.sent = send, recv, device, 0, []
+
+    def open(self, like, keep=True):
+        post = Post(self.send.at[self.count], self.recv.at[self.count], like, self.device)
+        self.count += 1
+        if keep:
+            self.sent.append(post)
+        return post
+
+    def post(self, like, moves):
+        post = self.open(like)
+        for src, dst, device in moves:
+            post.add(src, dst, device)
+        return post
+
+    def settle(self, posts):
+        for post in posts:
+            post.wait_send()
+        done = {id(post) for post in posts}
+        self.sent = [post for post in self.sent if id(post) not in done]
 
     def finish(self):
         self.settle(list(self.sent))
@@ -543,52 +578,58 @@
     return blocks.astype(F32).reshape(shape).astype(BF)
 
 
-def ffn_pass(rows_ref, grads_ref, in_ref, out_ref, hidden_ref, dm_ref, result, back, units, step):
-    result[...] = jnp.zeros(result.shape, F32)
-    back[...] = jnp.zeros(back.shape, F32)
-
-    def body(j, carry):
-        low = pl.multiple_of(j * step, step)
-        gate_at, up_at = pl.ds(low, step), pl.ds(pl.multiple_of(units + low, step), step)
-        rows, grads = rows_ref[...], grads_ref[...]
-        gate, up = mm(rows, in_ref[:, gate_at]), mm(rows, in_ref[:, up_at])
-        down = out_ref[gate_at, :]
-        d_hidden = mm_nt(grads, down)
-        share = 1.0 / (1.0 + jnp.exp(-gate))
-        lit = gate * share
-        hidden = (lit * up).astype(BF)
-        d_gate = (d_hidden * up * (share * (1.0 + gate * (1.0 - share)))).astype(BF)
-        d_up = (d_hidden * lit).astype(BF)
-        hidden_ref[:, gate_at] = hidden
-        dm_ref[:, gate_at] = d_gate
-        dm_ref[:, up_at] = d_up
-        result[...] += mm(hidden, down)
-        back[...] += mm_nt(d_gate, in_ref[:, gate_at]) + mm_nt(d_up, in_ref[:, up_at])
-        return carry
-
-    lax.fori_loop(0, units // step, body, 0)
+def ffn_block(j, rows, grads, in_ref, out_ref, hidden_ref, dm_ref, result, back, units, step):
+    low = pl.multiple_of(j * step, step) if not isinstance(j, int) else j * step
+    high = pl.multiple_of(units + low, step) if not isinstance(j, int) else units + low
+    gate_at, up_at = pl.ds(low, step), pl.ds(high, step)
+    gate, up = mm(rows, in_ref[:, gate_at]), mm(rows, in_ref[:, up_at])
+    down = out_ref[gate_at, :]
+    d_hidden = mm_nt(grads, down)
+    share = 1.0 / (1.0 + jnp.exp(-gate))
+    lit = gate * share
+    hidden = (lit * up).astype(BF)
+    d_gate = (d_hidden * up * (share * (1.0 + gate * (1.0 - share)))).astype(BF)
+    d_up = (d_hidden * lit).astype(BF)
+    hidden_ref[:, gate_at] = hidden
+    dm_ref[:, gate_at] = d_gate
+    dm_ref[:, up_at] = d_up
+    result[...] += mm(hidden, down)
+    back[...] += mm_nt(d_gate, in_ref[:, gate_at]) + mm_nt(d_up, in_ref[:, up_at])
+
+
+def box_rows(kept_rows, boxes, shift):
+    shape = (boxes * kept_rows, boxes * BOX)
+    row = lax.broadcasted_iota(jnp.int32, shape, 0)
+    column = lax.broadcasted_iota(jnp.int32, shape, 1)
+    box = jnp.floor((column.astype(F32) + 0.5) * (1.0 / BOX)).astype(jnp.int32)
+    at = column - box * BOX - shift
+    return ((at >= 0) & (at < kept_rows) & (row == box * kept_rows + at)).astype(BF)
 
 
 def block_kernel(
     nc, nz,
-    len_ref, hid_ref, go_ref, ids_ref, rank_ref, wqkv_ref, small_ref, gu_ref, wo_ref, sd_ref,
-    win_ref, wout_ref, turn_ref,
+    len_ref, hid_ref, go_ref, ids_ref, rank_ref, wqkv_ref, router_ref, ga_ref, gf_ref, gu_ref,
+    wo_ref, sd_ref, win_ref, wout_ref,
     out_ref, gin_ref, fq_ref, fgu_ref, fsd_ref, fwo_ref, ein_ref, eout_ref,
-    hid_all, up_own, up_all, wq_own, wq_st, wq_buf, w_ref, gu_st, gu_buf, gu_all, wo_st, wo_buf,
+    turn_ref, hid_all, up_own, up_all, wq_own, wq_st, wq_buf, w_ref, gu_st, gu_buf, gu_all, wo_st, wo_buf,
     wo_all, sd_all, wie, woe, normed_ref, qkv_ref, ctx_all, att_own, nt_all,
-    sb, ar, xs, ds, acc_a, acc_b, sh_own, sh_hidden, sh_dm, sh_send, rs_shared,
-    ex_hidden, ex_dm, pin, fb, rb, gsd, da_own, dctx_send, dctx_all, part, part_own, rs_in,
+    sb, ar, xs, ds, acc_a, acc_b, sh_own, sh_hidden, sh_dm, sh_send, sh_in, sh_mid, sh_end,
+    ex_hidden, ex_dm, pin, fb, rb, gsd, da_own, dctx_send, dctx_all, part, part_own, rs_in, rs_mid, rs_end,
     sib_gu, zi_gu, pb_gu, sib_q, zi_q, pb_q, sib_sd, zi_sd, sib_wo, zi_wo, pb_wo, in_wo,
-    send, recv, esend, erecv, gsend, grecv, lsem,
+    send, recv, lsem,
 ):
     c, z, f = place()
+    near_x, near_y = c + 1 - 2 * wrap(c, 2), wrap(c + 2, nc)
+    far = wrap(near_x + 2, nc)
+    to_x, to_y = (near_x, z, f), (near_y, z, f)
     in_plane = [(wrap(c + s, nc), z, f) for s in range(1, nc)]
     in_column = [(c, wrap(z + s, nz), f) for s in range(1, nz)]
     sibling = (c, z, 1 - f)
     across = [(wrap(c + s, nc), z, 1 - f) for s in range(1, nc)]
     ring = [(dz, dc) for dz in range(nz) for dc in range(nc) if dz or dc]
     everyone = [(wrap(c + dc, nc), wrap(z + dz, nz), f) for dz, dc in ring]
-    greet(everyone + [sibling] + across)
+    with jax.named_scope("s_greet"):
+        greet(everyone + [sibling] + across)
 
     num_seqs, shard_len, width = hid_ref.shape
     full_len = nc * shard_len
@@ -602,87 +643,122 @@
     own_units = units // nc
     down_rows = sd_ref.shape[0]
     num_experts = nz * nc
-    num_slots = num_experts * ROWS
+    num_slots = num_experts * CAP
+    box_slots = num_experts * BOX
     block_rows = nz * 2 * rows_w
-    mail = Courier(send, recv)
-
+    mail = Courier(send, recv, sibling)
+
+    small = jnp.concatenate(
+        [
+            router_ref[...].astype(F32),
+            ga_ref[...].astype(F32),
+            gf_ref[...].astype(F32),
+            jnp.zeros((128 - num_experts - 2, rows_w), F32),
+        ],
+        axis=0,
+    )
+    small = jnp.concatenate([small, jnp.zeros((128, 128 - rows_w), F32)], axis=1)
+    small = jnp.transpose(small, (1, 0))[:rows_w, :SMALL].astype(BF)
     for owner in range(nc):
         wq_own[owner] = jnp.concatenate(
             [
                 wqkv_ref[:, side * width + owner * head_width : side * width + (owner + 1) * head_width]
                 for side in range(3)
             ]
-            + [small_ref[...]],
+            + [small],
             axis=1,
         )
-    met(everyone + [sibling] + across)
-
-    staged_wq = [
-        mail.push(wq_own.at[wrap(c + s, nc)], wq_st.at[c], in_plane[s - 1]) for s in range(1, nc)
-    ]
+    with jax.named_scope("s_met"):
+        met(everyone + [sibling] + across)
+
+    others = pl.ds(0, nc - 1)
+    staged_wq = mail.post(
+        wq_st.at[others],
+        [(wq_own.at[wrap(c + s, nc)], wq_st.at[c], in_plane[s - 1]) for s in range(1, nc)],
+    )
     arriving = [
-        [mail.push(hid_ref.at[q], hid_all.at[q, c], peer) for peer in in_plane]
+        mail.post(
+            hid_all.at[q, pl.ds(0, 2)],
+            [(hid_ref.at[q], hid_all.at[q, c], peer) for peer in (to_x, to_y)],
+        )
         for q in range(num_seqs)
     ]
-    staged_wo = [mail.push(wo_ref, wo_st.at[c], peer) for peer in in_plane]
-    staged_gu = []
+    staged_wo = mail.post(wo_st.at[others], [(wo_ref, wo_st.at[c], peer) for peer in in_plane])
+    staged_gu = mail.open(gu_st.at[others])
     for s in range(1, nc):
         owner = wrap(c + s, nc)
         for side in range(2):
             at = pl.ds(pl.multiple_of(side * units + owner * own_units, own_units), own_units)
-            staged_gu.append(
-                mail.push(
-                    gu_ref.at[:, at],
-                    gu_st.at[c, :, pl.ds(side * own_units, own_units)],
-                    in_plane[s - 1],
-                )
+            staged_gu.add(
+                gu_ref.at[:, at],
+                gu_st.at[c, :, pl.ds(side * own_units, own_units)],
+                in_plane[s - 1],
             )
 
     block = 2 * c + f
     shard_rows = win_ref.shape[1]
     half_units = units // 2
+    step = 256
+    steps = half_units // step
     lands = pl.ds(pl.multiple_of(block * shard_rows, shard_rows), shard_rows)
-    expert_in, own_in = [], []
-    for s in range(nc):
-        owner = wrap(c + s, nc)
-        for g in range(2):
-            core = f if g == 0 else 1 - f
-            for side in range(2):
-                from_lane = pl.multiple_of(side * units + core * half_units, half_units)
-                src = win_ref.at[owner, :, pl.ds(from_lane, half_units)]
-                dst = wie.at[lands, pl.ds(side * half_units, half_units)]
-                if s == 0 and g == 0:
-                    own_in.append(pltpu.make_async_copy(src, dst, lsem.at[side]))
-                    own_in[-1].start()
-                else:
-                    expert_in.append(mail.push(src, dst, (owner, z, core)))
     out_rows = wout_ref.shape[1]
     to_core = block // nc
     slot = wrap(block, nc)
     out_lands = pl.ds(pl.multiple_of(slot * out_rows, out_rows), out_rows)
-
-    def out_copy(s, device, to_slot, lands_at):
-        return pltpu.make_async_remote_copy(
-            src_ref=wout_ref.at[wrap(c + s, nc)],
-            dst_ref=woe.at[lands_at],
-            send_sem=esend.at[s],
-            recv_sem=erecv.at[to_slot],
-            device_id=device,
-            device_id_type=MESH,
-        )
-
-    for s in range(1, nc):
-        out_copy(s, (wrap(c + s, nc), z, to_core), slot, out_lands).start()
-    own_out = pltpu.make_async_copy(wout_ref.at[c], woe.at[out_lands], lsem.at[2])
-
-    @pl.when(to_core == f)
-    def _():
-        own_out.start()
-
-    @pl.when(to_core != f)
-    def _():
-        out_copy(0, sibling, slot, out_lands).start()
-
+    remote_rows = (2 * nc - 1) * shard_rows
+    expert_in = [
+        mail.open(wie.at[pl.ds(0, remote_rows), pl.ds(0, 2 * step)]) for _ in range(steps)
+    ]
+    expert_out = mail.open(woe, keep=False)
+    remote_out = woe.at[pl.ds(0, (nc - 1) * out_rows)]
+    own_out = pltpu.make_async_copy(wout_ref.at[c], woe.at[out_lands], lsem.at[0])
+
+    def send_out(s):
+        owner = wrap(c + s, nc)
+        expert_out.add(wout_ref.at[owner], woe.at[out_lands], (owner, z, to_core))
+
+    def send_out_own():
+        @pl.when(to_core == f)
+        def _():
+            own_out.start()
+
+        @pl.when(to_core != f)
+        def _():
+            expert_out.add(wout_ref.at[c], woe.at[out_lands], sibling)
+
+    def own_in(j):
+        like = wie.at[pl.ds(0, shard_rows), pl.ds(0, 2 * step)]
+        return pltpu.make_async_copy(like, like, lsem.at[1 + j])
+
+    def send_in(j, s, g, side):
+        owner = wrap(c + s, nc)
+        core = f if g == 0 else 1 - f
+        from_lane = pl.multiple_of(side * units + core * half_units + j * step, step)
+        src = win_ref.at[owner, :, pl.ds(from_lane, step)]
+        dst = wie.at[lands, pl.ds(side * half_units + j * step, step)]
+        if s == 0 and g == 0:
+            pltpu.make_async_copy(src, dst, lsem.at[1 + j]).start()
+        else:
+            expert_in[j].add(src, dst, (owner, z, core))
+
+    bulk = [functools.partial(send_out, s) for s in range(1, nc)] + [send_out_own]
+    for j in range(steps):
+        for s in range(1, nc + 1):
+            for g in range(2):
+                for side in range(2):
+                    bulk.append(functools.partial(send_in, j, s % nc, g, side))
+
+    def pump(queue, count):
+        for _ in range(min(count, len(queue))):
+            queue.pop(0)()
+
+    with jax.named_scope("s_turns"):
+        row = lax.broadcasted_iota(jnp.int32, (full_len, 128), 0)
+        lane = lax.broadcasted_iota(jnp.int32, (full_len, 128), 1) & (HS // 2 - 1)
+        frequency = jnp.exp(lane.astype(F32) * (-2.0 * math.log(10000.0) / HS))
+        angles = position_of(row, half_len, full_len).astype(F32) * frequency
+        turn_ref[:, :128] = jnp.cos(angles)
+        turn_ref[:, 128:] = jnp.sin(angles)
     row_at = lax.broadcasted_iota(jnp.int32, (tok, 1), 0)
     inside = row_at & (shard_len - 1)
     low = c * half_len + (inside & (half_len - 1))
@@ -692,52 +768,75 @@
         lengths = jnp.where(row_at // shard_len == q, len_ref[q], lengths)
     live = (places < lengths).astype(F32)
     lane = lax.broadcasted_iota(jnp.int32, (tok, 128), 1).astype(F32)
-    picked = ids_ref[...].astype(F32)
-    hots = [(lane == SMALL + picked[:, k : k + 1]).astype(F32) for k in range(2)]
+    picked = []
+    for k in range(2):
+        ids = jnp.concatenate(
+            [ids_ref[q, e, k : k + 1, :] for q in range(num_seqs) for e in range(2)], axis=1
+        ).astype(F32)
+        picked.append(jnp.transpose(jnp.broadcast_to(ids, (tok, tok)), (1, 0)))
+    hots = [(lane == SMALL + picked[k]).astype(F32) for k in range(2)]
     rank_row = jnp.broadcast_to(rank_ref[...].astype(F32), (tok, tok))
     earlier = (rank_row < jnp.transpose(rank_row, (1, 0))).astype(BF)
     position = mm(earlier, ((hots[0] + hots[1]) * live).astype(BF))
-    slot_lane = lax.broadcasted_iota(jnp.int32, (tok, num_slots), 1).astype(F32)
-    dispatch = []
+    slot_lane = lax.broadcasted_iota(jnp.int32, (tok, box_slots), 1).astype(F32)
+    dispatch, dispatch_d = [], []
     for k in range(2):
         at = jnp.sum(hots[k] * position, axis=1, keepdims=True)
-        slot_at = jnp.where((live > 0) & (at < CAP), picked[:, k : k + 1] * ROWS + at, -1.0)
+        slot_at = jnp.where((live > 0) & (at < CAP), picked[k][:, :1] * BOX + at, -BOX)
         dispatch.append((slot_lane == slot_at).astype(BF))
+        dispatch_d.append((slot_lane == slot_at + CAP).astype(BF))
     anyone = dispatch[0] + dispatch[1]
+    anyone_d = dispatch_d[0] + dispatch_d[1]
     upstream = go_ref[...].reshape(tok, width).astype(F32) * live
     up_b = upstream.astype(BF)
     up_f = up_b.astype(F32)
     up_own[...] = up_b.reshape(num_seqs, shard_len, width)
-    up_copies = [mail.push(up_own, up_all.at[:, c], peer) for peer in in_plane]
     for q in range(num_seqs):
         hid_all[q, c] = hid_ref[q]
         up_all[q, c] = up_own[q]
 
-    own_down = pl.ds(pl.multiple_of((z * 2 + f) * down_rows, down_rows), down_rows)
-    sd_all[own_down] = sd_ref[...]
+    def pass_on(post, buffer, q, at):
+        post.wait_recv()
+        origin, peer = (near_x, to_y) if q == 0 else (near_y, to_x)
+        block_at = at(buffer, q, origin)
+        return mail.post(block_at, [(block_at, block_at, peer)])
+
+    def by_seq(buffer, q, chip):
+        return buffer.at[q, chip]
+
+    def by_chip(buffer, q, chip):
+        return buffer.at[chip, q]
+
+    sd_all[z, f] = sd_ref[...]
+    planes = pl.ds(0, nz - 1)
 
     def spread(stage, staged, buffer):
-        for copy in staged:
-            copy.wait_recv()
-        copies = [mail.push(stage, buffer.at[:, z, f], peer) for peer in in_column]
-        copies.append(mail.push(stage, buffer.at[:, z, f], sibling))
+        staged.wait_recv()
+        post = mail.post(
+            buffer.at[:, planes, 0],
+            [(stage, buffer.at[:, z, f], peer) for peer in in_column],
+        )
         for i in range(nc):
             buffer[i, z, f] = stage[i]
-        return copies
-
-    def forward(copies, buffer):
-        passed = []
-        for s in range(1, nz):
-            origin = wrap(z + nz - s, nz)
-            copies[s - 1].wait_recv()
-            passed.append(
-                mail.push(buffer.at[:, origin, f], buffer.at[:, origin, f], sibling)
-            )
-        return passed
+        return post
+
+    def forward(post, buffer):
+        post.wait_recv()
+        both = buffer.at[:, :, f]
+        return mail.post(both, [(both, both, sibling)])
 
     with jax.named_scope("a_stage_wq"):
         wq_st[c] = wq_own[c]
         spread_wq = spread(wq_st, staged_wq, wq_buf)
+    with jax.named_scope("a_pass_hidden"):
+        passing = [pass_on(arriving[q], hid_all, q, by_seq) for q in range(num_seqs)]
+    up_copies = [
+        mail.post(
+            up_all.at[q, pl.ds(0, 2)],
+            [(up_own.at[q], up_all.at[q, c], peer) for peer in (to_x, to_y)],
+        )
+        for q in range(num_seqs)
+    ]
     with jax.named_scope("a_stage_wo"):
         wo_st[c] = wo_ref[...]
         spread_wo = spread(wo_st, staged_wo, wo_buf)
@@ -746,12 +845,12 @@
             at = pl.ds(pl.multiple_of(side * units + c * own_units, own_units), own_units)
             gu_st[c, :, side * own_units : (side + 1) * own_units] = gu_ref[:, at]
         spread_gu = spread(gu_st, staged_gu, gu_buf)
-    spread_sd = [mail.push(sd_ref, sd_all.at[own_down], peer) for peer in in_column]
-    spread_sd.append(mail.push(sd_ref, sd_all.at[own_down], sibling))
+    spread_sd = mail.post(
+        sd_all.at[planes, 0], [(sd_ref, sd_all.at[z, f], peer) for peer in in_column]
+    )
     with jax.named_scope("a_forward_wq"):
         passed_wq = forward(spread_wq, wq_buf)
-        for copy in passed_wq + spread_wq[-1:]:
-            copy.wait_recv()
+        passed_wq.wait_recv()
         for i in range(nc):
             w_ref[i * block_rows : (i + 1) * block_rows, :] = join(
                 wq_buf[i], (block_rows, wide_cols)
@@ -764,8 +863,7 @@
     ctx_copies = []
     for q in range(num_seqs):
         with jax.named_scope("a_wait_hidden"):
-            for copy in arriving[q]:
-                copy.wait_recv()
+            passing[q].wait_recv()
         with jax.named_scope("a_attention"):
             rows = hid_all[q].reshape(full_len, width).astype(F32)
             normed = (rows * inverse_rms(rows) * attn_gain).astype(BF)
@@ -788,12 +886,19 @@
             context = jnp.concatenate(heads, axis=1).astype(BF)
             ctx_all[c, q] = context.reshape(nc, shard_len, head_width)
         ctx_copies.append(
-            [mail.push(ctx_all.at[c, q], ctx_all.at[c, q], peer) for peer in in_plane]
-        )
+            mail.post(
+                ctx_all.at[pl.ds(0, 2), q],
+                [(ctx_all.at[c, q], ctx_all.at[c, q], peer) for peer in (to_x, to_y)],
+            )
+        )
+    with jax.named_scope("a_pass_upstream"):
+        up_passing = [pass_on(up_copies[q], up_all, q, by_seq) for q in range(num_seqs)]
+    with jax.named_scope("a_pass_context"):
+        ctx_passing = [pass_on(ctx_copies[q], ctx_all, q, by_chip) for q in range(num_seqs)]
+    pump(bulk, PUMPS[0])
     with jax.named_scope("a_forward_wo"):
         passed_wo = forward(spread_wo, wo_buf)
-        for copy in passed_wo + spread_wo[-1:]:
-            copy.wait_recv()
+        passed_wo.wait_recv()
         for i in range(nc):
             wo_all[i * block_rows : (i + 1) * block_rows, :] = join(
                 wo_buf[i], (block_rows, width)
@@ -801,8 +906,7 @@
     ffn_gain = column_row(w_ref[:, tail_at:], SMALL + num_experts + 1)
     for q in range(num_seqs):
         with jax.named_scope("a_wait_context"):
-            for copy in ctx_copies[q]:
-                copy.wait_recv()
+            ctx_passing[q].wait_recv()
         with jax.named_scope("a_project"):
             total = hid_all[q].reshape(full_len, width).astype(F32)
             for i in range(nc):
@@ -814,7 +918,7 @@
             nt_all[q] = (
                 (total * inverse_rms(total) * ffn_gain).astype(BF).reshape(nc, shard_len, width)
             )
-    by_block = acc_a.reshape(num_seqs, nc, shard_len, width)
+    by_block = acc_a.at[pl.ds(0, nc * tok)].reshape(num_seqs, nc, shard_len, width)
     for q in range(num_seqs):
         att_own[q] = by_block[q, c]
 
@@ -827,103 +931,171 @@
         raised = [jnp.exp(value - top) for value in chosen]
         gates = [value / (raised[0] + raised[1]) for value in raised]
         weighted = [(gates[k] * up_f).astype(BF) for k in range(2)]
-        rows_out = mm_tn(anyone, normed)
-        grads_out = mm_tn(dispatch[0], weighted[0]) + mm_tn(dispatch[1], weighted[1])
-        sb[:, 0] = rows_out.reshape(num_experts, ROWS, width).astype(BF)
-        sb[:, 1] = grads_out.reshape(num_experts, ROWS, width).astype(BF)
-        row_copies = [
-            mail.push(sb.at[to[1] * nc + to[0]], ar.at[f, z, c], to) for to in everyone
-        ]
+        boxes = mm_tn(anyone, normed)
+        boxes = boxes + mm_tn(dispatch_d[0], weighted[0]) + mm_tn(dispatch_d[1], weighted[1])
+        sb[...] = boxes.reshape(num_experts, BOX, width).astype(BF)
+        row_copies = []
+        for dz in range(nz):
+            post = mail.open(ar.at[f, 0] if dz else ar.at[f, 0, others])
+            for dc in range(nc):
+                if dz or dc:
+                    to = (wrap(c + dc, nc), wrap(z + dz, nz), f)
+                    post.add(sb.at[to[1] * nc + to[0]], ar.at[f, z, c], to)
+            row_copies.append(post)
         ar[f, z, c] = sb[z * nc + c]
-        forwards = [mail.push(sb.at[z * nc + c], ar.at[f, z, c], sibling)]
+    pump(bulk, len(bulk))
 
     with jax.named_scope("b_forward_gu"):
         passed_gu = forward(spread_gu, gu_buf)
-        passed_sd = []
-        for s in range(1, nz):
-            origin = wrap(z + nz - s, nz)
-            spread_sd[s - 1].wait_recv()
-            at = pl.ds(pl.multiple_of((origin * 2 + f) * down_rows, down_rows), down_rows)
-            passed_sd.append(mail.push(sd_all.at[at], sd_all.at[at], sibling))
-        for copy in passed_gu + spread_gu[-1:] + passed_sd + spread_sd[-1:]:
-            copy.wait_recv()
+        spread_sd.wait_recv()
+        passed_sd = mail.post(sd_all.at[:, f], [(sd_all.at[:, f], sd_all.at[:, f], sibling)])
+        passed_gu.wait_recv()
+        passed_sd.wait_recv()
         for i in range(nc):
             gu_all[i * block_rows : (i + 1) * block_rows, :] = join(
                 gu_buf[i], (block_rows, 2 * own_units)
             )
     with jax.named_scope("b_wait_upstream"):
-        for copy in up_copies:
-            copy.wait_recv()
+        for post in up_passing:
+            post.wait_recv()
     plane_tok = nc * tok
     shared_rows = nt_all.reshape(plane_tok, width)
     shared_grads = up_all.reshape(plane_tok, width)
+    shared_down = sd_all.reshape(own_units, width)
     with jax.named_scope("b_shared"):
         first = pl.ds(0, plane_tok)
-        ffn_pass(
-            shared_rows, shared_grads, gu_all, sd_all, sh_hidden, sh_dm,
-            acc_a.at[first], acc_b.at[first], own_units, 256,
-        )
+        acc_a[...] = jnp.zeros(acc_a.shape, F32)
+        acc_b[...] = jnp.zeros(acc_b.shape, F32)
+
+        def shared_block(j, carry):
+            ffn_block(
+                j, shared_rows[...], shared_grads[...], gu_all, shared_down, sh_hidden, sh_dm,
+                acc_a.at[first], acc_b.at[first], own_units, 256,
+            )
+            return carry
+
+        lax.fori_loop(0, own_units // 256, shared_block, 0)
         for k, acc in enumerate((acc_a, acc_b)):
-            cut = acc.reshape(num_seqs, nc, shard_len, width)
+            cut = acc.at[first].reshape(num_seqs, nc, shard_len, width)
             for q in range(num_seqs):
-                sh_own[k, q] = cut[q, c]
+                sh_own[k, q, 0] = cut[q, c]
+                sh_own[k, q, 1] = cut[q, near_y if q == 0 else near_x]
             sh_send[k] = cut[...].astype(BF)
-    shared_copies = [
-        mail.push(sh_send.at[:, :, wrap(c + s, nc)], rs_shared.at[s - 1], in_plane[s - 1])
-        for s in range(1, nc)
-    ]
+
+    def first_leg(inbox, box, lead):
+        post = mail.open(inbox)
+        for q in range(num_seqs):
+            peer = to_x if q == 0 else to_y
+            for at, chip in enumerate((near_x if q == 0 else near_y, far)):
+                post.add(box.at[lead + (q, chip)], inbox.at[lead + (q, at)], peer)
+        return post
+
+    shared_first = first_leg(sh_in, sh_send, (slice(None),))
+
+    mail.settle([spread_gu, passed_gu])
+    ggu = gu_buf
+    with jax.named_scope("b_shared_grads"):
+
+        def gate_up_grads(j, carry):
+            at = pl.ds(pl.multiple_of(j * 256, 256), 256)
+            piece = mm_tn(shared_rows[...], sh_dm[:, at])
+            ggu[:, :, :, :, at] = piece.reshape(ggu.shape[:4] + (256,)).astype(BF)
+            return carry
+
+        lax.fori_loop(0, 2 * own_units // 256, gate_up_grads, 0)
+        gsd[...] = mm_tn(sh_hidden[...], shared_grads[...]).reshape(gsd.shape).astype(BF)
+        sibling_gu = mail.post(sib_gu, [(ggu.at[:, :, 1 - f], sib_gu, sibling)])
+        sibling_sd = mail.post(sib_sd, [(gsd.at[:, 1 - f], sib_sd, sibling)])
+
+    with jax.named_scope("b_reduce_shared"):
+        def two_cores(copy, own, inbox):
+            copy.wait_recv()
+            inbox[...] = (own.astype(F32) + inbox[...].astype(F32)).astype(BF)
+
+        def four_planes(copy, buffer, inbox):
+            copy.wait_recv()
+            for i in range(nc):
+                inbox[i] = (buffer[i, :, f].astype(F32) + inbox[i].astype(F32)).astype(BF)
+
+        four_planes(sibling_gu, ggu, sib_gu)
+        two_cores(sibling_sd, gsd[:, f], sib_sd)
+        gu_copies = mail.post(
+            zi_gu,
+            [
+                (sib_gu.at[:, wrap(z + s, nz)], zi_gu.at[s - 1], in_column[s - 1])
+                for s in range(1, nz)
+            ],
+        )
+        sd_copies = mail.post(
+            zi_sd,
+            [(sib_sd.at[wrap(z + s, nz)], zi_sd.at[s - 1], in_column[s - 1]) for s in range(1, nz)],
+        )
 
     with jax.named_scope("b_forward_rows"):
-        for copy, (dz, dc) in zip(row_copies, ring):
-            copy.wait_recv()
-            oz, oc = wrap(z + nz - dz, nz), wrap(c + nc - dc, nc)
-            forwards.append(mail.push(ar.at[f, oz, oc], ar.at[f, oz, oc], sibling))
-        for copy in forwards:
-            copy.wait_recv()
+        forwards = mail.open(ar.at[f])
+        for dz in range(nz):
+            row_copies[dz].wait_recv()
+            origin = wrap(z + nz - dz, nz)
+            forwards.add(ar.at[f, origin], ar.at[f, origin], sibling)
+        forwards.wait_recv()
+        keep_x, keep_d = (box_rows(CAP, num_experts, shift) for shift in (0, CAP))
         for core in range(2):
             at = slice(core * num_slots, (core + 1) * num_slots)
-            xs[at] = join(ar[core, :, :, 0], (num_slots, width))
-            ds[at] = join(ar[core, :, :, 1], (num_slots, width))
-    with jax.named_scope("b_wait_experts"):
-        for copy in own_in:
-            copy.wait()
-        for copy in expert_in:
-            copy.wait_recv()
-        for at in range(nc):
-
-            @pl.when(f * nc + at != block)
-            def _(at=at):
-                out_copy(0, sibling, at, pl.ds(at * out_rows, out_rows)).wait_recv()
-
+            boxes = join(ar[core], (box_slots, width))
+            xs[at] = mm(keep_x, boxes).astype(BF)
+            ds[at] = mm(keep_d, boxes).astype(BF)
+    with jax.named_scope("b_wait_down"):
         @pl.when(to_core == f)
         def _():
+            expert_out.wait_recv(remote_out)
             own_out.wait()
 
-    mail.settle(row_copies + forwards[:1])
+        @pl.when(to_core != f)
+        def _():
+            expert_out.wait_recv()
+
+    acc_a[...] = jnp.zeros(acc_a.shape, F32)
+    acc_b[...] = jnp.zeros(acc_b.shape, F32)
+    for j in range(steps):
+        with jax.named_scope("b_wait_experts"):
+            own_in(j).wait()
+            expert_in[j].wait_recv()
+        with jax.named_scope("b_experts"):
+            ffn_block(
+                j, xs[...], ds[...], wie, woe, ex_hidden, ex_dm, acc_a, acc_b, half_units, step
+            )
+    mail.settle(row_copies)
     pr = sb
-    acc = [ref.at[pl.ds(0, num_slots)] for ref in (acc_a, acc_b)]
-    for turn in range(2):
-        core = 1 - f if turn == 0 else f
-        at = pl.ds(pl.multiple_of(core * num_slots, num_slots), num_slots)
-        with jax.named_scope("b_experts"):
-            ffn_pass(
-                xs.at[at], ds.at[at], wie, woe, ex_hidden.at[at], ex_dm.at[at],
-                acc[0], acc[1], half_units, 256,
-            )
-        if turn == 0:
-            for k in range(2):
-                pr[:, k] = acc[k][...].reshape(num_experts, ROWS, width).astype(BF)
-            swap = mail.push(pr, pin, sibling)
     with jax.named_scope("b_sibling_sum"):
+
+        def boxed(core):
+            at = pl.ds(pl.multiple_of(core * num_slots, num_slots), num_slots)
+            return (
+                mm_tn(keep_x, acc_a[at].astype(BF)) + mm_tn(keep_d, acc_b[at].astype(BF))
+            ).reshape(num_experts, BOX, width)
+
+        pr[...] = boxed(1 - f).astype(BF)
+        swap = mail.post(pin, [(pr, pin, sibling)])
+        ours = boxed(f)
         swap.wait_recv()
+        fb[...] = (ours + pin[...].astype(F32)).astype(BF)
+        returns = mail.post(
+            rb.at[pl.ds(0, num_experts - 1)],
+            [(fb.at[to[1] * nc + to[0]], rb.at[z * nc + c], to) for to in everyone],
+        )
+        rb[z * nc + c] = fb[z * nc + c]
+    with jax.named_scope("b_second_leg"):
+        shared_first.wait_recv()
         for k in range(2):
-            fb[:, k] = (
-                acc[k][...].reshape(num_experts, ROWS, width) + pin[:, k].astype(F32)
-            ).astype(BF)
-        returns = [
-            mail.push(fb.at[to[1] * nc + to[0]], rb.at[z * nc + c], to) for to in everyone
-        ]
-        rb[z * nc + c] = fb[z * nc + c]
+            for q in range(num_seqs):
+                sh_mid[k, q] = (sh_own[k, q, 1] + sh_in[k, q, 1].astype(F32)).astype(BF)
+        shared_second = mail.post(
+            sh_end,
+            [
+                (sh_mid.at[:, q], sh_end.at[:, q], to_y if q == 0 else to_x)
+                for q in range(num_seqs)
+            ],
+        )
 
     gwi, gwo = wie, woe
 
@@ -932,86 +1104,82 @@
         gwi[:, at] = mm_tn(xs[...], ex_dm[:, at]).astype(BF)
         return carry
 
-    home_in, home_own = [], []
-    for side in range(2):
-        steps = half_units // 256
-        with jax.named_scope("b_gwi"):
-            lax.fori_loop(side * steps, (side + 1) * steps, expert_grads, 0)
-        for s in range(nc):
-            owner = wrap(c + s, nc)
-            for g in range(2):
-                core = f if g == 0 else 1 - f
-                from_rows = pl.ds(
-                    pl.multiple_of((2 * owner + core) * shard_rows, shard_rows), shard_rows
-                )
-                to_lane = pl.multiple_of(side * units + f * half_units, half_units)
-                src = gwi.at[from_rows, pl.ds(side * half_units, half_units)]
-                dst = ein_ref.at[c, :, pl.ds(to_lane, half_units)]
-                if s == 0 and g == 0:
-                    home_own.append(pltpu.make_async_copy(src, dst, lsem.at[3 + side]))
-                    home_own[-1].start()
-                else:
-                    home_in.append(mail.push(src, dst, (owner, z, core)))
-
-    def home_out(j, arrives):
-        to_block = f * nc + j
-        return pltpu.make_async_remote_copy(
-            src_ref=gwo.at[pl.ds(j * out_rows, out_rows)],
-            dst_ref=eout_ref.at[arrives],
-            send_sem=gsend.at[j],
-            recv_sem=grecv.at[arrives],
-            device_id=(to_block // 2, z, wrap(to_block, 2)),
-            device_id_type=MESH,
-        )
+    home = []
+    home_in = mail.open(gwi.at[pl.ds(0, remote_rows)])
+    home_out = mail.open(gwo, keep=False)
+    remote_home = gwo.at[pl.ds(0, (nc - 1) * out_rows)]
+    home_in_own = pltpu.make_async_copy(
+        gwi.at[pl.ds(0, shard_rows)], gwi.at[pl.ds(0, shard_rows)], lsem.at[1]
+    )
+
+    def send_home_in(j, s, g, side):
+        owner = wrap(c + s, nc)
+        core = f if g == 0 else 1 - f
+        from_rows = pl.ds(
+            pl.multiple_of((2 * owner + core) * shard_rows, shard_rows), shard_rows
+        )
+        to_lane = pl.multiple_of(side * units + f * half_units + j * HOME, HOME)
+        src = gwi.at[from_rows, pl.ds(side * half_units + j * HOME, HOME)]
+        dst = ein_ref.at[c, :, pl.ds(to_lane, HOME)]
+        if s == 0 and g == 0:
+            pltpu.make_async_copy(src, dst, lsem.at[1]).start()
+        else:
+            home_in.add(src, dst, (owner, z, core))
 
     def home_out_own(j):
         return pltpu.make_async_copy(
-            gwo.at[pl.ds(j * out_rows, out_rows)], eout_ref.at[c], lsem.at[5]
-        )
-
+            gwo.at[pl.ds(j * out_rows, out_rows)], eout_ref.at[c], lsem.at[0]
+        )
+
+    def send_home_out(j):
+        to_block = f * nc + j
+
+        @pl.when(to_block == block)
+        def _():
+            home_out_own(j).start()
+
+        @pl.when(to_block != block)
+        def _():
+            home_out.add(
+                gwo.at[pl.ds(j * out_rows, out_rows)],
+                eout_ref.at[c],
+                (to_block // 2, z, wrap(to_block, 2)),
+            )
+
+    for side in range(2):
+        for j in range(half_units // HOME):
+            for s in range(1, nc + 1):
+                for g in range(2):
+                    home.append(functools.partial(send_home_in, j, s % nc, g, side))
+    for j in range(nc):
+        home.append(functools.partial(send_home_out, j))
+    with jax.named_scope("b_gwi"):
+        lax.fori_loop(0, 2 * half_units // 256, expert_grads, 0)
+    pump(home, PUMPS[1])
     with jax.named_scope("b_gwo"):
         for j in range(nc):
             gwo[j * out_rows : (j + 1) * out_rows, :] = mm_tn(
                 ex_hidden[:, j * out_rows : (j + 1) * out_rows], ds[...]
             ).astype(BF)
 
-            @pl.when(f * nc + j == block)
-            def _(j=j):
-                home_out_own(j).start()
-
-            @pl.when(f * nc + j != block)
-            def _(j=j):
-                home_out(j, c).start()
-
-    mail.settle(spread_gu + passed_gu)
-    ggu = gu_buf
-    with jax.named_scope("b_shared_grads"):
-
-        def gate_up_grads(j, carry):
-            at = pl.ds(pl.multiple_of(j * 256, 256), 256)
-            piece = mm_tn(shared_rows[...], sh_dm[:, at])
-            ggu[:, :, :, :, at] = piece.reshape(ggu.shape[:4] + (256,)).astype(BF)
-            return carry
-
-        lax.fori_loop(0, 2 * own_units // 256, gate_up_grads, 0)
-        gsd[...] = mm_tn(sh_hidden[...], shared_grads[...]).reshape(gsd.shape).astype(BF)
-        sibling_gu = mail.push(ggu.at[:, :, 1 - f], sib_gu, sibling)
-        sibling_sd = mail.push(gsd.at[:, 1 - f], sib_sd, sibling)
-
     with jax.named_scope("c_wait_shared"):
-        shared, d_normed = [sh_own[k].reshape(tok, width) for k in range(2)]
-        for s in range(1, nc):
-            shared_copies[s - 1].wait_recv()
-            shared = shared + rs_shared[s - 1, 0].reshape(tok, width).astype(F32)
-            d_normed = d_normed + rs_shared[s - 1, 1].reshape(tok, width).astype(F32)
+        shared_second.wait_recv()
+        shared, d_normed = [
+            jnp.concatenate(
+                [
+                    sh_own[k, q, 0] + sh_in[k, q, 0].astype(F32) + sh_end[k, q].astype(F32)
+                    for q in range(num_seqs)
+                ],
+                axis=0,
+            )
+            for k in range(2)
+        ]
     with jax.named_scope("c_wait_returns"):
-        for copy in returns:
-            copy.wait_recv()
+        returns.wait_recv()
     with jax.named_scope("c_combine"):
         attended = att_own[...].reshape(tok, width)
         inverse = inverse_rms(attended)
-        results = join(rb[:, 0], (num_slots, width))
-        d_rows = join(rb[:, 1], (num_slots, width))
+        results = join(rb[...], (box_slots, width))
         routed = [mm(dispatch[k], results) for k in range(2)]
         mixture = gates[0] * routed[0] + gates[1] * routed[1]
         out_ref[...] = (
@@ -1022,7 +1190,7 @@
         d_logits = hots[0] * (gates[0] * (d_gates[0] - mean_gate)) + hots[1] * (
             gates[1] * (d_gates[1] - mean_gate)
         )
-        d_normed = d_normed + mm(anyone, d_rows) + split_dot(mm_nt, d_logits, tail)
+        d_normed = d_normed + mm(anyone_d, results) + split_dot(mm_nt, d_logits, tail)
         d_attended = upstream + norm_back(attended, inverse, d_normed * ffn_gain)
         d_att_b = d_attended.astype(BF)
         d_context = mm_nt(d_att_b, wo_all[...]).astype(BF)
@@ -1032,54 +1200,41 @@
             )
         for q in range(num_seqs):
             dctx_all[q, c] = dctx_send[c, q]
-        dctx_copies = [
-            mail.push(dctx_send.at[wrap(c + s, nc)], dctx_all.at[:, c], in_plane[s - 1])
-            for s in range(1, nc)
-        ]
+        dctx_copies = mail.post(
+            dctx_all.at[:, others],
+            [
+                (dctx_send.at[wrap(c + s, nc)], dctx_all.at[:, c], in_plane[s - 1])
+                for s in range(1, nc)
+            ],
+        )
         gin_ref[...] = d_attended.reshape(gin_ref.shape)
-
-    mail.settle(spread_wo + passed_wo)
+    pump(home, PUMPS[2])
+
+    mail.settle([spread_wo, passed_wo])
     gwo_at = wo_buf
     with jax.named_scope("c_reduce"):
-        def two_cores(copy, own, inbox):
-            copy.wait_recv()
-            inbox[...] = (own.astype(F32) + inbox[...].astype(F32)).astype(BF)
-
-        def four_planes(copy, buffer, inbox):
-            copy.wait_recv()
-            for i in range(nc):
-                inbox[i] = (buffer[i, :, f].astype(F32) + inbox[i].astype(F32)).astype(BF)
-
         for i in range(nc):
             mine = jnp.concatenate([ctx_all[i, q, c] for q in range(num_seqs)], axis=0)
             gwo_at[i] = mm_tn(mine, d_att_b).reshape(gwo_at.shape[1:]).astype(BF)
-        sibling_wo = mail.push(gwo_at.at[:, :, 1 - f], sib_wo, sibling)
+        sibling_wo = mail.post(sib_wo, [(gwo_at.at[:, :, 1 - f], sib_wo, sibling)])
         d_router = split_dot(mm_tn, normed, d_logits, left_wide=False)
         d_gain = jnp.sum(d_normed * attended * inverse, axis=0, keepdims=True)
         turned = jnp.transpose(jnp.broadcast_to(d_gain, (128, width)), (1, 0))
         extra_lane = lax.broadcasted_iota(jnp.int32, (width, 128), 1)
         extras = jnp.where(extra_lane == SMALL + num_experts + 1, turned, d_router)
-        four_planes(sibling_gu, ggu, sib_gu)
-        two_cores(sibling_sd, gsd[:, f], sib_sd)
-        gu_copies = [
-            mail.push(sib_gu.at[:, wrap(z + s, nz)], zi_gu.at[s - 1], in_column[s - 1])
-            for s in range(1, nz)
-        ]
-        sd_copies = [
-            mail.push(sib_sd.at[wrap(z + s, nz)], zi_sd.at[s - 1], in_column[s - 1])
-            for s in range(1, nz)
-        ]
         four_planes(sibling_wo, gwo_at, sib_wo)
-        wo_copies = [
-            mail.push(sib_wo.at[:, wrap(z + s, nz)], zi_wo.at[s - 1], in_column[s - 1])
-            for s in range(1, nz)
-        ]
+        wo_copies = mail.post(
+            zi_wo,
+            [
+                (sib_wo.at[:, wrap(z + s, nz)], zi_wo.at[s - 1], in_column[s - 1])
+                for s in range(1, nz)
+            ],
+        )
 
     with jax.named_scope("c_wait_dctx"):
-        for copy in dctx_copies:
-            copy.wait_recv()
+        dctx_copies.wait_recv()
     grad_qkv = jnp.zeros((width, 3 * head_width), F32)
-    parting = []
+    rs_first = mail.open(rs_in)
     for q in range(num_seqs):
         with jax.named_scope("c_attention"):
             d_context = dctx_all[q].reshape(full_len, head_width)
@@ -1104,40 +1259,49 @@
             product = mm_nt(d_merged, w_ref[:, : 3 * head_width]).reshape(nc, shard_len, width)
             part_own[q] = product
             part[q] = product.astype(BF)
-            parting.append(
-                [
-                    mail.push(part.at[q, wrap(c + s, nc)], rs_in.at[s - 1, q], in_plane[s - 1])
-                    for s in range(1, nc)
-                ]
-            )
+            for at, chip in enumerate((near_x if q == 0 else near_y, far)):
+                rs_first.add(part.at[q, chip], rs_in.at[q, at], to_x if q == 0 else to_y)
             grad_qkv = grad_qkv + mm_tn(normed_ref[q], d_merged)
-    mail.settle(spread_wq + passed_wq)
+    pump(home, len(home))
+    mail.settle([spread_wq, passed_wq])
     gq = wq_buf
     with jax.named_scope("c_reduce_q"):
         last = jnp.concatenate([grad_qkv[:, tail_at:], extras[:, 3 * head_width - tail_at :]], axis=1)
         gq[...] = (
             jnp.concatenate([grad_qkv[:, :tail_at], last], axis=1).reshape(gq.shape).astype(BF)
         )
-        sibling_q = mail.push(gq.at[:, :, 1 - f], sib_q, sibling)
+        sibling_q = mail.post(sib_q, [(gq.at[:, :, 1 - f], sib_q, sibling)])
         four_planes(sibling_q, gq, sib_q)
-        q_copies = [
-            mail.push(sib_q.at[:, wrap(z + s, nz)], zi_q.at[s - 1], in_column[s - 1])
-            for s in range(1, nz)
-        ]
+        q_copies = mail.post(
+            zi_q,
+            [
+                (sib_q.at[:, wrap(z + s, nz)], zi_q.at[s - 1], in_column[s - 1])
+                for s in range(1, nz)
+            ],
+        )
+    with jax.named_scope("c_second_leg"):
+        rs_first.wait_recv()
+        for q in range(num_seqs):
+            relay = part_own[q, near_y if q == 0 else near_x]
+            rs_mid[q] = (relay + rs_in[q, 1].astype(F32)).astype(BF)
+        rs_second = mail.post(
+            rs_end,
+            [(rs_mid.at[q], rs_end.at[q], to_y if q == 0 else to_x) for q in range(num_seqs)],
+        )
 
     def column_sum(own, copies, inbox):
+        copies.wait_recv()
         total = own.astype(F32)
         for s in range(1, nz):
-            copies[s - 1].wait_recv()
             total = total + inbox[s - 1].astype(F32)
         return total
 
     def hand_out(box, final):
         final[c] = box[c]
-        return [
-            mail.push(box.at[wrap(c + s, nc)], final.at[c], in_plane[s - 1])
-            for s in range(1, nc)
-        ]
+        return mail.post(
+            final.at[others],
+            [(box.at[wrap(c + s, nc)], final.at[c], in_plane[s - 1]) for s in range(1, nc)],
+        )
 
     with jax.named_scope("c_column_gu"):
         pb_gu[...] = column_sum(sib_gu[:, z], gu_copies, zi_gu).astype(BF)
@@ -1151,57 +1315,46 @@
         pb_q[...] = column_sum(sib_q[:, z], q_copies, zi_q).astype(BF)
         final_q = hand_out(pb_q, fq_ref)
     with jax.named_scope("c_grad_in"):
+        rs_second.wait_recv()
         for q in range(num_seqs):
-            d_normed = part_own[q, c]
-            for s in range(1, nc):
-                parting[q][s - 1].wait_recv()
-                d_normed = d_normed + rs_in[s - 1, q].astype(F32)
+            d_normed = part_own[q, c] + rs_in[q, 0].astype(F32) + rs_end[q].astype(F32)
             rows = hid_ref[q].astype(F32)
             gin_ref[q] = gin_ref[q] + norm_back(rows, inverse_rms(rows), d_normed * attn_gain)
     with jax.named_scope("c_final"):
-        for copy in final_wo:
-            copy.wait_recv()
+        final_wo.wait_recv()
         fwo_ref[...] = jnp.sum(in_wo[...].astype(F32), axis=0)
-        for copy in final_gu + final_q:
-            copy.wait_recv()
+        final_gu.wait_recv()
+        final_q.wait_recv()
     with jax.named_scope("c_wait_home"):
-        for copy in home_own:
-            copy.wait()
-        for copy in home_in:
-            copy.wait_recv()
-        for arrives in range(nc):
-
-            @pl.when((arrives != c) | (to_core != f))
-            def _(arrives=arrives):
-                home_out(0, arrives).wait_recv()
-
-        for j in range(nc):
-
-            @pl.when(f * nc + j == block)
-            def _(j=j):
-                home_out_own(j).wait()
-
-            @pl.when(f * nc + j != block)
-            def _(j=j):
-                home_out(j, c).wait_send()
+        home_in_own.wait()
+        home_in.wait_recv()
+
+        @pl.when(to_core == f)
+        def _():
+            home_out_own(0).wait()
+            home_out.wait_recv(remote_home)
+            home_out.wait_send(remote_home)
+            expert_out.wait_send(remote_out)
 
         @pl.when(to_core != f)
         def _():
-            out_copy(0, sibling, slot, out_lands).wait_send()
-
-        for s in range(1, nc):
-            out_copy(s, (wrap(c + s, nc), z, to_core), slot, out_lands).wait_send()
+            home_out.wait_recv()
+            home_out.wait_send()
+            expert_out.wait_send()
+
+    assert mail.count <= POSTS, mail.count
+    with jax.named_scope("z_finish"):
         mail.finish()
 
 
 def finish_kernel(
     nc, fq_ref, fgu_ref, wqkv_ref, ga_ref, ein_ref, eout_ref, out_in, gin_in, fsd_in, fwo_in,
-    gq_ref, gr_ref, gains_ref, ggu_ref, oin_ref, oout_ref, out_ref, gin_ref, fsd_ref, fwo_ref,
+    gq_ref, gr_ref, gga_ref, ggf_ref, ggu_ref, oin_ref, oout_ref, out_ref, gin_ref, fsd_ref, fwo_ref,
 ):
     oin_ref[...] = ein_ref[...].astype(F32)
     oout_ref[...] = eout_ref[...].astype(F32)
 
-    @pl.when(pl.program_id(0) == 0)
+    @pl.when((pl.program_id(0) == 0) & (pl.program_id(1) == 0))
     def _():
         out_ref[...] = out_in[...]
         gin_ref[...] = gin_in[...]
@@ -1228,18 +1381,17 @@
             axis=1,
         )
         extras = jnp.sum(fq_ref[:, :, 3 * head_width - SMALL :].astype(F32), axis=0)
-        num_experts = gr_ref.shape[1]
-        gr_ref[...] = extras[:, SMALL : SMALL + num_experts]
+        num_experts = gr_ref.shape[0]
         first = jnp.sum(wqkv_ref[...].astype(F32) * grads, axis=1, keepdims=True)
         lane = lax.broadcasted_iota(jnp.int32, (rows_w, 128), 1)
         both = jnp.where(lane == SMALL + num_experts, first, extras)
         turned = jnp.transpose(
             jnp.concatenate([both, jnp.zeros((128 - rows_w, 128), F32)], axis=0), (1, 0)
         )
-        gain = ga_ref[...].astype(F32)
+        gr_ref[...] = turned[SMALL : SMALL + num_experts, :rows_w]
         at = SMALL + num_experts
-        gains_ref[0:1, :] = turned[at : at + 1, :rows_w] / gain
-        gains_ref[1:2, :] = turned[at + 1 : at + 2, :rows_w]
+        gga_ref[...] = turned[at : at + 1, :rows_w] / ga_ref[...].astype(F32)
+        ggf_ref[...] = turned[at + 1 : at + 2, :rows_w]
 
 
 def vmem(*shape, dtype=jnp.bfloat16):
@@ -1264,21 +1416,13 @@
     hbm, vm, sm = pl.ANY, pltpu.VMEM, pltpu.SMEM
     dma = pltpu.SemaphoreType.DMA
 
-    small = jnp.concatenate([w_router, gain_attn[:, None], gain_ffn[:, None]], axis=1)
-    small = jnp.pad(small, ((0, 0), (0, SMALL - small.shape[1])))
-    every = jnp.arange(full_len, dtype=jnp.int32)
-    inside = every % shard_len
-    low = every // shard_len * half_len + inside % half_len
-    cosines, sines = rope_tables(jnp.where(inside >= half_len, full_len - 1 - low, low))
-    turns = jnp.concatenate([cosines] * 4 + [sines] * 4, axis=1)
-
     seq_shape = (num_seqs, shard_len, width)
     group_shape = (num_seqs, nc, shard_len, width)
     blocks = (nc, nz, 2, rows_w)
     half_blocks = (nc, nz, rows_w)
     wide_cols = 3 * head_width + SMALL
-    num_slots = num_experts * ROWS
-    row_box = (num_experts, 2, ROWS, width)
+    num_slots = num_experts * CAP
+    row_box = (num_experts, BOX, width)
     plane_tok = nc * tok
     outs = [
         (seq_shape, BF),
@@ -1294,10 +1438,11 @@
         functools.partial(block_kernel, nc, nz),
         out_shape=[jax.ShapeDtypeStruct(shape, dtype) for shape, dtype in outs],
         in_specs=[
-            pl.BlockSpec(memory_space=space) for space in [sm] + [vm] * 9 + [hbm, hbm, vm]
+            pl.BlockSpec(memory_space=space) for space in [sm] + [vm] * 11 + [hbm, hbm]
         ],
         out_specs=[pl.BlockSpec(memory_space=space) for space in [vm] * 6 + [hbm, hbm]],
         scratch_shapes=[
+            vmem(full_len, 256, dtype=F32),
             vmem(*group_shape),
             vmem(*seq_shape),
             vmem(*group_shape),
@@ -1311,7 +1456,7 @@
             vmem(nc, rows_w, width),
             vmem(*blocks, width),
             vmem(width, width),
-            vmem(own_units, width),
+            vmem(nz, 2, down_rows, width),
             vmem(width, 2 * half_units),
             vmem(half_units, width),
             vmem(num_seqs, full_len, width),
@@ -1320,16 +1465,18 @@
             vmem(*seq_shape, dtype=F32),
             vmem(*group_shape),
             vmem(*row_box),
-            vmem(2, nz, nc, 2, ROWS, width),
+            vmem(2, nz, nc, BOX, width),
             vmem(2 * num_slots, width),
             vmem(2 * num_slots, width),
-            vmem(plane_tok, width, dtype=F32),
-            vmem(plane_tok, width, dtype=F32),
-            vmem(2, *seq_shape, dtype=F32),
+            vmem(2 * num_slots, width, dtype=F32),
+            vmem(2 * num_slots, width, dtype=F32),
+            vmem(2, num_seqs, 2, shard_len, width, dtype=F32),
             vmem(plane_tok, own_units),
             vmem(plane_tok, 2 * own_units),
             vmem(2, *group_shape),
-            vmem(nc - 1, 2, *seq_shape),
+            vmem(2, num_seqs, 2, shard_len, width),
+            vmem(2, *seq_shape),
+            vmem(2, *seq_shape),
             vmem(2 * num_slots, half_units),
             vmem(2 * num_slots, 2 * half_units),
             vmem(*row_box),
@@ -1341,7 +1488,9 @@
             vmem(num_seqs, nc, shard_len, head_width),
             vmem(*group_shape),
             vmem(*group_shape, dtype=F32),
-            vmem(nc - 1, *seq_shape),
+            vmem(num_seqs, 2, shard_len, width),
+            vmem(*seq_shape),
+            vmem(*seq_shape),
             vmem(*half_blocks, 2 * own_units),
             vmem(nz - 1, nc, rows_w, 2 * own_units),
             vmem(nc, rows_w, 2 * own_units),
@@ -1354,13 +1503,9 @@
             vmem(nz - 1, nc, rows_w, width),
             vmem(nc, rows_w, width),
             vmem(nc, rows_w, width),
-            dma((200,)),
-            dma((200,)),
-            dma((nc,)),
-            dma((nc,)),
-            dma((nc,)),
-            dma((nc,)),
-            dma((6,)),
+            dma((POSTS,)),
+            dma((POSTS,)),
+            dma((1 + half_units // 256,)),
         ],
         compiler_params=pltpu.CompilerParams(
             collective_id=0, has_side_effects=True, vmem_limit_bytes=VMEM_BYTES
@@ -1373,22 +1518,24 @@
         seq_lengths,
         hidden_in.reshape(seq_shape),
         grad_output.reshape(seq_shape),
-        expert_ids.reshape(tok, 2),
+        expert_ids.transpose(0, 1, 3, 2),
         route_rank.reshape(1, tok),
-        w_qkv, small, w_gate_up, w_out, w_shared_down, w_experts_in, w_experts_out, turns,
+        w_qkv, w_router.T, gain_attn.reshape(1, rows_w), gain_ffn.reshape(1, rows_w),
+        w_gate_up, w_out, w_shared_down, w_experts_in, w_experts_out,
     )
 
     def whole(shape):
-        return pl.BlockSpec(shape, lambda e: (0,) * len(shape))
+        return pl.BlockSpec(shape, lambda e, j: (0,) * len(shape))
 
     def one(shape):
-        return pl.BlockSpec((1,) + shape[1:], lambda e: (e, 0, 0))
+        return pl.BlockSpec((1, shape[1], shape[2] // WIDEN), lambda e, j: (e, 0, j))
 
     ins = [fq, fgu, w_qkv, gain_attn.reshape(1, rows_w), ein, eout, out, gin, fsd, fwo]
     results = [
         (w_qkv.shape, F32),
-        (w_router.shape, F32),
-        ((2, rows_w), F32),
+        (w_router.shape[::-1], F32),
+        ((1, rows_w), F32),
+        ((1, rows_w), F32),
         (w_gate_up.shape, F32),
         (ein.shape, F32),
         (eout.shape, F32),
@@ -1397,13 +1544,13 @@
         (fsd.shape, F32),
         (fwo.shape, F32),
     ]
-    grad_qkv, grad_router, gains, grad_gu, grad_in, grad_out, out, gin, fsd, fwo = pl.pallas_call(
+    grad_qkv, grad_router, grad_ga, grad_gf, grad_gu, grad_in, grad_out, out, gin, fsd, fwo = pl.pallas_call(
         functools.partial(finish_kernel, nc),
-        grid=(ein.shape[0],),
+        grid=(ein.shape[0], WIDEN),
         out_shape=[jax.ShapeDtypeStruct(shape, dtype) for shape, dtype in results],
         in_specs=[one(x.shape) if i in (4, 5) else whole(x.shape) for i, x in enumerate(ins)],
         out_specs=[
-            one(shape) if i in (4, 5) else whole(shape) for i, (shape, _) in enumerate(results)
+            one(shape) if i in (5, 6) else whole(shape) for i, (shape, _) in enumerate(results)
         ],
         compiler_params=pltpu.CompilerParams(vmem_limit_bytes=VMEM_BYTES),
         name="widen_gradients",
@@ -1411,11 +1558,11 @@
     return (
         out.reshape(hidden_in.shape),
         gin.reshape(hidden_in.shape),
-        gains[0],
+        grad_ga.reshape(rows_w),
         grad_qkv,
         fwo,
-        grad_router,
-        gains[1],
+        grad_router.T,
+        grad_gf.reshape(rows_w),
         grad_gu,
         fsd,
         grad_in,
@@ -1437,7 +1584,7 @@
         and hidden_in.shape[0] == 2 * nz * nf
         and hidden_in.shape[3] == 768
         and w_gate_up.shape[1] == w_experts_in.shape[2] == 4096
-        and CAP <= ROWS
+        and 2 * CAP <= BOX
     )
 
 

time: 245 us -> 213 us (0.87); the launches traced: 242 us -> 213 us
  Pallas kernels: 233 us -> 212 us
  local copies, waits for them, and re-layouts: 7.3 us -> 0 us
    pallas_call x1, Pallas kernels: 225 us -> 204 us  [fast_device(): pl.pallas_call(functools.partial(block_kernel, nc, nz), out_shape=[jax.Sh...]
    unnamed x3 -> x0, local copies, waits for them, and re-layouts: 3.56 us -> none
where the time goes in v3:
time: 213 us
  Pallas kernels  212 us (100%)
    pallas_call x1, Pallas kernels, fast_device(): pl.pallas_call(functools.partial(block_kernel, nc, nz), out_shape=[jax.Sh...  204 us
    pallas_call x1, Pallas kernels, fast_device(): pl.pallas_call(functools.partial(finish_kernel, nc), grid=(ein.shape[0],...  7.73 us

profile of v3, /device:TPU:31, one launch (start us, length us, event | category | flops | bytes accessed | tf_op | source)
XLA Modules:
  0.0 212.6 jit_solution(17258830978886614003)
XLA Ops:
  0.6 204.0 %block_forward_backward.1 = (bf16[2,64,768]{2,1,0:T(8,128)(2,1)}, f32[2,64,768]{2,1,0:T(8,128)}, bf16[4,24,640]{2,1,0:T(8,128)(2,1)}, bf16[4,24,1024]{2,1,0:T(8,...) custom-call(s32[2]{0:T(128)} %len_ref.1, ...), custom_call_target="tpu_custom_call" | custom-call | flops 16000000000 | bytes 30000000 | tf_op jit(solution)/shard_map/block_forward_backward/pallas_call | solution.py:1437
  204.7 7.7 %widen_gradients.1 = (f32[24,2304]{1,0:T(8,128)}, f32[16,24]{1,0:T(8,128)}, f32[1,24]{1,0:T(1,128)}, f32[1,24]{1,0:T(1,128)}, f32[24,4096]{1,0:T(8,128)}, /*inde...) custom-call(bf16[4,24,640]{2,1,0:T(8,128)(2,1)} %get-tuple-element.3, ...), custom_call_target="tpu_custom_call" | custom-call | tf_op jit(solution)/shard_map/widen_gradients/pallas_call | solution.py:1547

commit v4 on v3

--- a/solution.py
+++ b/solution.py
@@ -417,7 +417,7 @@
 BOX = 40
 SMALL = 64
 VMEM_BYTES = 63 * 1024 * 1024
-PUMPS = (2, 10, 8)
+PUMPS = (2, 10, 8, 1)
 POSTS = 64
 HOME = 512
 WIDEN = 1
@@ -837,17 +837,11 @@
         )
         for q in range(num_seqs)
     ]
-    with jax.named_scope("a_stage_wo"):
-        wo_st[c] = wo_ref[...]
-        spread_wo = spread(wo_st, staged_wo, wo_buf)
-    with jax.named_scope("a_stage_gu"):
-        for side in range(2):
-            at = pl.ds(pl.multiple_of(side * units + c * own_units, own_units), own_units)
-            gu_st[c, :, side * own_units : (side + 1) * own_units] = gu_ref[:, at]
-        spread_gu = spread(gu_st, staged_gu, gu_buf)
-    spread_sd = mail.post(
-        sd_all.at[planes, 0], [(sd_ref, sd_all.at[z, f], peer) for peer in in_column]
-    )
+    pump(bulk, PUMPS[3])
+    wo_st[c] = wo_ref[...]
+    for side in range(2):
+        at = pl.ds(pl.multiple_of(side * units + c * own_units, own_units), own_units)
+        gu_st[c, :, side * own_units : (side + 1) * own_units] = gu_ref[:, at]
     with jax.named_scope("a_forward_wq"):
         passed_wq = forward(spread_wq, wq_buf)
         passed_wq.wait_recv()
@@ -891,6 +885,7 @@
                 [(ctx_all.at[c, q], ctx_all.at[c, q], peer) for peer in (to_x, to_y)],
             )
         )
+    spread_wo = spread(wo_st, staged_wo, wo_buf)
     with jax.named_scope("a_pass_upstream"):
         up_passing = [pass_on(up_copies[q], up_all, q, by_seq) for q in range(num_seqs)]
     with jax.named_scope("a_pass_context"):
@@ -898,6 +893,10 @@
     pump(bulk, PUMPS[0])
     with jax.named_scope("a_forward_wo"):
         passed_wo = forward(spread_wo, wo_buf)
+        spread_gu = spread(gu_st, staged_gu, gu_buf)
+        spread_sd = mail.post(
+            sd_all.at[planes, 0], [(sd_ref, sd_all.at[z, f], peer) for peer in in_column]
+        )
         passed_wo.wait_recv()
         for i in range(nc):
             wo_all[i * block_rows : (i + 1) * block_rows, :] = join(
@@ -1262,7 +1261,7 @@
             for at, chip in enumerate((near_x if q == 0 else near_y, far)):
                 rs_first.add(part.at[q, chip], rs_in.at[q, at], to_x if q == 0 else to_y)
             grad_qkv = grad_qkv + mm_tn(normed_ref[q], d_merged)
-    pump(home, len(home))
+    pump(home, len(home) - 2)
     mail.settle([spread_wq, passed_wq])
     gq = wq_buf
     with jax.named_scope("c_reduce_q"):
@@ -1314,6 +1313,7 @@
     with jax.named_scope("c_column_q"):
         pb_q[...] = column_sum(sib_q[:, z], q_copies, zi_q).astype(BF)
         final_q = hand_out(pb_q, fq_ref)
+    pump(home, len(home))
     with jax.named_scope("c_grad_in"):
         rs_second.wait_recv()
         for q in range(num_seqs):

time: 213 us -> 203 us (0.953)
  Pallas kernels: 212 us -> 200 us
    pallas_call x1, Pallas kernels: 204 us -> 192 us  [fast_device(): pl.pallas_call(functools.partial(block_kernel, nc, nz), out_shape=[jax.Sh...]
where the time goes in v4:
time: 203 us; the launch traced here: 201 us
  Pallas kernels  200 us (99%)
    pallas_call x1, Pallas kernels, fast_device(): pl.pallas_call(functools.partial(block_kernel, nc, nz), out_shape=[jax.Sh...  192 us
    pallas_call x1, Pallas kernels, fast_device(): pl.pallas_call(functools.partial(finish_kernel, nc), grid=(ein.shape[0],...  7.73 us

profile of v4, /device:TPU:31, one launch (start us, length us, event | category | flops | bytes accessed | tf_op | source)
XLA Modules:
  0.0 201.0 jit_solution(2902937226858010901)
XLA Ops:
  0.6 192.5 %block_forward_backward.1 = (bf16[2,64,768]{2,1,0:T(8,128)(2,1)}, f32[2,64,768]{2,1,0:T(8,128)}, bf16[4,24,640]{2,1,0:T(8,128)(2,1)}, bf16[4,24,1024]{2,1,0:T(8,...) custom-call(s32[2]{0:T(128)} %len_ref.1, ...), custom_call_target="tpu_custom_call" | custom-call | flops 16000000000 | bytes 30000000 | tf_op jit(solution)/shard_map/block_forward_backward/pallas_call | solution.py:1437
  193.1 7.7 %widen_gradients.1 = (f32[24,2304]{1,0:T(8,128)}, f32[16,24]{1,0:T(8,128)}, f32[1,24]{1,0:T(1,128)}, f32[1,24]{1,0:T(1,128)}, f32[24,4096]{1,0:T(8,128)}, /*inde...) custom-call(bf16[4,24,640]{2,1,0:T(8,128)(2,1)} %get-tuple-element.3, ...), custom_call_target="tpu_custom_call" | custom-call | tf_op jit(solution)/shard_map/widen_gradients/pallas_call | solution.py:1547

commit v5 on v4

--- a/solution.py
+++ b/solution.py
@@ -417,9 +417,10 @@
 BOX = 40
 SMALL = 64
 VMEM_BYTES = 63 * 1024 * 1024
-PUMPS = (2, 10, 8, 1)
+PUMPS = (3, 17, 6, 0, 6, 6)
 POSTS = 64
-HOME = 512
+EARLY = 2
+GATE_UP, DOWN = 1, 2
 WIDEN = 1
 
 
@@ -611,7 +612,7 @@
     len_ref, hid_ref, go_ref, ids_ref, rank_ref, wqkv_ref, router_ref, ga_ref, gf_ref, gu_ref,
     wo_ref, sd_ref, win_ref, wout_ref,
     out_ref, gin_ref, fq_ref, fgu_ref, fsd_ref, fwo_ref, ein_ref, eout_ref,
-    turn_ref, hid_all, up_own, up_all, wq_own, wq_st, wq_buf, w_ref, gu_st, gu_buf, gu_all, wo_st, wo_buf,
+    turn_ref, meta_own, meta_all, picks, hot_x, hot_d, dg_send, dg_in, hid_all, up_own, up_all, wq_own, wq_st, wq_buf, w_ref, gu_st, gu_buf, gu_all, wo_st, wo_buf,
     wo_all, sd_all, wie, woe, normed_ref, qkv_ref, ctx_all, att_own, nt_all,
     sb, ar, xs, ds, acc_a, acc_b, sh_own, sh_hidden, sh_dm, sh_send, sh_in, sh_mid, sh_end,
     ex_hidden, ex_dm, pin, fb, rb, gsd, da_own, dctx_send, dctx_all, part, part_own, rs_in, rs_mid, rs_end,
@@ -624,12 +625,12 @@
     to_x, to_y = (near_x, z, f), (near_y, z, f)
     in_plane = [(wrap(c + s, nc), z, f) for s in range(1, nc)]
     in_column = [(c, wrap(z + s, nz), f) for s in range(1, nz)]
+    steps_up = list(range(1, nz))
     sibling = (c, z, 1 - f)
     across = [(wrap(c + s, nc), z, 1 - f) for s in range(1, nc)]
-    ring = [(dz, dc) for dz in range(nz) for dc in range(nc) if dz or dc]
-    everyone = [(wrap(c + dc, nc), wrap(z + dz, nz), f) for dz, dc in ring]
+    partners = in_plane + in_column + [sibling] + across
     with jax.named_scope("s_greet"):
-        greet(everyone + [sibling] + across)
+        greet(partners)
 
     num_seqs, shard_len, width = hid_ref.shape
     full_len = nc * shard_len
@@ -644,7 +645,7 @@
     down_rows = sd_ref.shape[0]
     num_experts = nz * nc
     num_slots = num_experts * CAP
-    box_slots = num_experts * BOX
+    column_slots = nz * BOX
     block_rows = nz * 2 * rows_w
     mail = Courier(send, recv, sibling)
 
@@ -668,8 +669,18 @@
             + [small],
             axis=1,
         )
+    meta_own[...] = jnp.concatenate(
+        [
+            jnp.concatenate(
+                [ids_ref[q, e, k : k + 1, :] for q in range(num_seqs) for e in range(2)], axis=1
+            )
+            for k in range(2)
+        ]
+        + [rank_ref[...], jnp.zeros((5, tok), jnp.int32)],
+        axis=0,
+    )
     with jax.named_scope("s_met"):
-        met(everyone + [sibling] + across)
+        met(partners)
 
     others = pl.ds(0, nc - 1)
     staged_wq = mail.post(
@@ -683,6 +694,9 @@
         )
         for q in range(num_seqs)
     ]
+    meta_copies = mail.post(
+        meta_all.at[others], [(meta_own, meta_all.at[c], peer) for peer in in_plane]
+    )
     staged_wo = mail.post(wo_st.at[others], [(wo_ref, wo_st.at[c], peer) for peer in in_plane])
     staged_gu = mail.open(gu_st.at[others])
     for s in range(1, nc):
@@ -759,37 +773,53 @@
         angles = position_of(row, half_len, full_len).astype(F32) * frequency
         turn_ref[:, :128] = jnp.cos(angles)
         turn_ref[:, 128:] = jnp.sin(angles)
-    row_at = lax.broadcasted_iota(jnp.int32, (tok, 1), 0)
-    inside = row_at & (shard_len - 1)
-    low = c * half_len + (inside & (half_len - 1))
-    places = jnp.where(inside >= half_len, full_len - 1 - low, low)
-    lengths = jnp.zeros((tok, 1), jnp.int32)
-    for q in range(num_seqs):
-        lengths = jnp.where(row_at // shard_len == q, len_ref[q], lengths)
-    live = (places < lengths).astype(F32)
     lane = lax.broadcasted_iota(jnp.int32, (tok, 128), 1).astype(F32)
-    picked = []
-    for k in range(2):
-        ids = jnp.concatenate(
-            [ids_ref[q, e, k : k + 1, :] for q in range(num_seqs) for e in range(2)], axis=1
-        ).astype(F32)
-        picked.append(jnp.transpose(jnp.broadcast_to(ids, (tok, tok)), (1, 0)))
-    hots = [(lane == SMALL + picked[k]).astype(F32) for k in range(2)]
-    rank_row = jnp.broadcast_to(rank_ref[...].astype(F32), (tok, tok))
-    earlier = (rank_row < jnp.transpose(rank_row, (1, 0))).astype(BF)
-    position = mm(earlier, ((hots[0] + hots[1]) * live).astype(BF))
-    slot_lane = lax.broadcasted_iota(jnp.int32, (tok, box_slots), 1).astype(F32)
-    dispatch, dispatch_d = [], []
-    for k in range(2):
-        at = jnp.sum(hots[k] * position, axis=1, keepdims=True)
-        slot_at = jnp.where((live > 0) & (at < CAP), picked[k][:, :1] * BOX + at, -BOX)
-        dispatch.append((slot_lane == slot_at).astype(BF))
-        dispatch_d.append((slot_lane == slot_at + CAP).astype(BF))
-    anyone = dispatch[0] + dispatch[1]
-    anyone_d = dispatch_d[0] + dispatch_d[1]
+
+    def live_rows(chip):
+        row_at = lax.broadcasted_iota(jnp.int32, (tok, 1), 0)
+        inside = row_at & (shard_len - 1)
+        low = chip * half_len + (inside & (half_len - 1))
+        places = jnp.where(inside >= half_len, full_len - 1 - low, low)
+        lengths = jnp.zeros((tok, 1), jnp.int32)
+        for q in range(num_seqs):
+            lengths = jnp.where(row_at // shard_len == q, len_ref[q], lengths)
+        return (places < lengths).astype(F32)
+
+    def turned(rows):
+        return jnp.transpose(
+            jnp.concatenate([rows, jnp.zeros((128 - rows.shape[0], tok), F32)], axis=0), (1, 0)
+        )
+
+    def hot_lanes(columns):
+        return [(lane == SMALL + columns[:, k : k + 1]).astype(F32) for k in range(2)]
+
+    def gates_of(hots, logits):
+        chosen = [jnp.sum(hot * logits, axis=1, keepdims=True) for hot in hots]
+        top = jnp.maximum(chosen[0], chosen[1])
+        raised = [jnp.exp(value - top) for value in chosen]
+        return [value / (raised[0] + raised[1]) for value in raised]
+
+    def route(chip):
+        rows = meta_all[chip].astype(F32)
+        columns = turned(rows)
+        picks[chip] = columns
+        hots = hot_lanes(columns)
+        rank_row = jnp.broadcast_to(rows[2:3], (tok, tok))
+        earlier = (rank_row < columns[:, 2:3]).astype(BF)
+        live = live_rows(chip)
+        position = mm(earlier, ((hots[0] + hots[1]) * live).astype(BF))
+        slot_lane = lax.broadcasted_iota(jnp.int32, (tok, column_slots), 1).astype(F32)
+        for k in range(2):
+            at = jnp.sum(hots[k] * position, axis=1, keepdims=True)
+            plane = jnp.floor((columns[:, k : k + 1] + 0.5) * (1.0 / nc))
+            here = columns[:, k : k + 1] - plane * nc == c.astype(F32)
+            slot_at = jnp.where((live > 0) & (at < CAP) & here, plane * BOX + at, -BOX)
+            hot_x[chip, k] = (slot_lane == slot_at).astype(BF)
+            hot_d[chip, k] = (slot_lane == slot_at + CAP).astype(BF)
+
+    live = live_rows(c)
     upstream = go_ref[...].reshape(tok, width).astype(F32) * live
     up_b = upstream.astype(BF)
-    up_f = up_b.astype(F32)
     up_own[...] = up_b.reshape(num_seqs, shard_len, width)
     for q in range(num_seqs):
         hid_all[q, c] = hid_ref[q]
@@ -820,8 +850,16 @@
             buffer[i, z, f] = stage[i]
         return post
 
-    def forward(post, buffer):
-        post.wait_recv()
+    def spread_gate_up(side):
+        at = pl.ds(side * own_units, own_units)
+        return mail.post(
+            gu_buf.at[:, planes, 0, :, at],
+            [(gu_st.at[:, :, at], gu_buf.at[:, z, f, :, at], peer) for peer in in_column],
+        )
+
+    def forward(posts, buffer):
+        for post in posts:
+            post.wait_recv()
         both = buffer.at[:, :, f]
         return mail.post(both, [(both, both, sibling)])
 
@@ -838,12 +876,17 @@
         for q in range(num_seqs)
     ]
     pump(bulk, PUMPS[3])
+    with jax.named_scope("a_route"):
+        meta_copies.wait_recv()
+        meta_all[c] = meta_own[...]
+        for chip in range(nc):
+            route(chip)
     wo_st[c] = wo_ref[...]
     for side in range(2):
         at = pl.ds(pl.multiple_of(side * units + c * own_units, own_units), own_units)
         gu_st[c, :, side * own_units : (side + 1) * own_units] = gu_ref[:, at]
     with jax.named_scope("a_forward_wq"):
-        passed_wq = forward(spread_wq, wq_buf)
+        passed_wq = forward([spread_wq], wq_buf)
         passed_wq.wait_recv()
         for i in range(nc):
             w_ref[i * block_rows : (i + 1) * block_rows, :] = join(
@@ -892,11 +935,11 @@
         ctx_passing = [pass_on(ctx_copies[q], ctx_all, q, by_chip) for q in range(num_seqs)]
     pump(bulk, PUMPS[0])
     with jax.named_scope("a_forward_wo"):
-        passed_wo = forward(spread_wo, wo_buf)
-        spread_gu = spread(gu_st, staged_gu, gu_buf)
-        spread_sd = mail.post(
-            sd_all.at[planes, 0], [(sd_ref, sd_all.at[z, f], peer) for peer in in_column]
-        )
+        passed_wo = forward([spread_wo], wo_buf)
+        staged_gu.wait_recv()
+        for i in range(nc):
+            gu_buf[i, z, f] = gu_st[i]
+        spread_gu = [spread_gate_up(0)]
         passed_wo.wait_recv()
         for i in range(nc):
             wo_all[i * block_rows : (i + 1) * block_rows, :] = join(
@@ -921,28 +964,151 @@
     for q in range(num_seqs):
         att_own[q] = by_block[q, c]
 
+    with jax.named_scope("b_wait_upstream"):
+        for post in up_passing:
+            post.wait_recv()
     with jax.named_scope("b_dispatch"):
+        tail = w_ref[:, tail_at:]
+        gates = []
+        for chip in range(nc):
+            normed = jnp.concatenate([nt_all[q, chip] for q in range(num_seqs)], axis=0)
+            gates.append(gates_of(hot_lanes(picks[chip]), mm(normed, tail)))
+            up_f = jnp.concatenate([up_all[q, chip] for q in range(num_seqs)], axis=0).astype(F32)
+            boxes = mm_tn(hot_x[chip, 0] + hot_x[chip, 1], normed)
+            for k in range(2):
+                boxes = boxes + mm_tn(hot_d[chip, k], (gates[chip][k] * up_f).astype(BF))
+            sb[:, chip] = boxes.reshape(nz, BOX, width).astype(BF)
+        row_copies = [
+            mail.post(ar.at[f, 0], [(sb.at[to[1]], ar.at[f, z], to)]) for to in in_column
+        ]
+        ar[f, z] = sb[z]
         normed = jnp.concatenate([nt_all[q, c] for q in range(num_seqs)], axis=0)
-        tail = w_ref[:, tail_at:]
-        logits = mm(normed, tail)
-        chosen = [jnp.sum(hot * logits, axis=1, keepdims=True) for hot in hots]
-        top = jnp.maximum(chosen[0], chosen[1])
-        raised = [jnp.exp(value - top) for value in chosen]
-        gates = [value / (raised[0] + raised[1]) for value in raised]
-        weighted = [(gates[k] * up_f).astype(BF) for k in range(2)]
-        boxes = mm_tn(anyone, normed)
-        boxes = boxes + mm_tn(dispatch_d[0], weighted[0]) + mm_tn(dispatch_d[1], weighted[1])
-        sb[...] = boxes.reshape(num_experts, BOX, width).astype(BF)
-        row_copies = []
-        for dz in range(nz):
-            post = mail.open(ar.at[f, 0] if dz else ar.at[f, 0, others])
-            for dc in range(nc):
-                if dz or dc:
-                    to = (wrap(c + dc, nc), wrap(z + dz, nz), f)
-                    post.add(sb.at[to[1] * nc + to[0]], ar.at[f, z, c], to)
-            row_copies.append(post)
-        ar[f, z, c] = sb[z * nc + c]
     pump(bulk, len(bulk))
+
+    with jax.named_scope("b_forward_rows"):
+        forwards = mail.open(ar.at[f])
+        forwards.add(ar.at[f, z], ar.at[f, z], sibling)
+        for s in range(1, nz):
+            row_copies[s - 1].wait_recv()
+            origin = wrap(z + nz - s, nz)
+            forwards.add(ar.at[f, origin], ar.at[f, origin], sibling)
+        forwards.wait_recv()
+        keep_x, keep_d = (box_rows(CAP, num_experts, shift) for shift in (0, CAP))
+        for core in range(2):
+            at = slice(core * num_slots, (core + 1) * num_slots)
+            boxes = join(ar[core], (num_experts * BOX, width))
+            xs[at] = mm(keep_x, boxes).astype(BF)
+            ds[at] = mm(keep_d, boxes).astype(BF)
+    with jax.named_scope("b_wait_down"):
+        @pl.when(to_core == f)
+        def _():
+            expert_out.wait_recv(remote_out)
+            own_out.wait()
+
+        @pl.when(to_core != f)
+        def _():
+            expert_out.wait_recv()
+
+    gwi, gwo = wie, woe
+
+    def expert_grads(j):
+        for side in range(2):
+            at = pl.ds(side * half_units + j * step, step)
+            gwi[:, at] = mm_tn(xs[...], ex_dm[:, at]).astype(BF)
+        at = pl.ds(j * step, step)
+        gwo[at, :] = mm_tn(ex_hidden[:, at], ds[...]).astype(BF)
+        for s in range(1, nc + 1):
+            for g in range(2):
+                for side in range(2):
+                    home.append(functools.partial(send_home_in, j, s % nc, g, side))
+        home.append(functools.partial(send_home_out, j))
+
+    home = []
+    home_in = mail.open(gwi.at[pl.ds(0, remote_rows)])
+    home_out = mail.open(gwo, keep=False)
+    remote_home = gwo.at[pl.ds(0, (nc - 1) * out_rows)]
+    home_in_own = pltpu.make_async_copy(
+        gwi.at[pl.ds(0, shard_rows)], gwi.at[pl.ds(0, shard_rows)], lsem.at[1]
+    )
+
+    def send_home_in(j, s, g, side):
+        owner = wrap(c + s, nc)
+        core = f if g == 0 else 1 - f
+        from_rows = pl.ds(
+            pl.multiple_of((2 * owner + core) * shard_rows, shard_rows), shard_rows
+        )
+        to_lane = pl.multiple_of(side * units + f * half_units + j * step, step)
+        src = gwi.at[from_rows, pl.ds(side * half_units + j * step, step)]
+        dst = ein_ref.at[c, :, pl.ds(to_lane, step)]
+        if s == 0 and g == 0:
+            pltpu.make_async_copy(src, dst, lsem.at[1]).start()
+        else:
+            home_in.add(src, dst, (owner, z, core))
+
+    def home_out_own(j):
+        return pltpu.make_async_copy(
+            gwo.at[pl.ds(j * out_rows, out_rows)], eout_ref.at[c], lsem.at[0]
+        )
+
+    def send_home_out(j):
+        to_block = f * nc + j
+
+        @pl.when(to_block == block)
+        def _():
+            home_out_own(j).start()
+
+        @pl.when(to_block != block)
+        def _():
+            home_out.add(
+                gwo.at[pl.ds(j * out_rows, out_rows)],
+                eout_ref.at[c],
+                (to_block // 2, z, wrap(to_block, 2)),
+            )
+
+    acc_a[...] = jnp.zeros(acc_a.shape, F32)
+    acc_b[...] = jnp.zeros(acc_b.shape, F32)
+    for j in range(steps):
+        with jax.named_scope("b_wait_experts"):
+            own_in(j).wait()
+            expert_in[j].wait_recv()
+        if j == steps - 1:
+            pump(home, len(home))
+        with jax.named_scope("b_experts"):
+            ffn_block(
+                j, xs[...], ds[...], wie, woe, ex_hidden, ex_dm, acc_a, acc_b, half_units, step
+            )
+        if j < EARLY:
+            with jax.named_scope("b_early_grads"):
+                expert_grads(j)
+        if j == GATE_UP:
+            spread_gu.append(spread_gate_up(1))
+        if j == DOWN:
+            spread_sd = mail.post(
+                sd_all.at[planes, 0], [(sd_ref, sd_all.at[z, f], peer) for peer in in_column]
+            )
+    mail.settle(row_copies)
+    pr = sb
+    with jax.named_scope("b_sibling_sum"):
+
+        def boxed(core):
+            at = pl.ds(pl.multiple_of(core * num_slots, num_slots), num_slots)
+            return (
+                mm_tn(keep_x, acc_a[at].astype(BF)) + mm_tn(keep_d, acc_b[at].astype(BF))
+            ).reshape(nz, nc, BOX, width)
+
+        pr[...] = boxed(1 - f).astype(BF)
+        swap = mail.post(pin, [(pr, pin, sibling)])
+        ours = boxed(f)
+        swap.wait_recv()
+        fb[...] = (ours + pin[...].astype(F32)).astype(BF)
+        returns = mail.post(
+            rb.at[planes], [(fb.at[to[1]], rb.at[z], to) for to in in_column]
+        )
+        rb[z] = fb[z]
+    with jax.named_scope("b_expert_grads"):
+        for j in range(EARLY, steps):
+            expert_grads(j)
+    pump(home, PUMPS[1])
 
     with jax.named_scope("b_forward_gu"):
         passed_gu = forward(spread_gu, gu_buf)
@@ -954,9 +1120,6 @@
             gu_all[i * block_rows : (i + 1) * block_rows, :] = join(
                 gu_buf[i], (block_rows, 2 * own_units)
             )
-    with jax.named_scope("b_wait_upstream"):
-        for post in up_passing:
-            post.wait_recv()
     plane_tok = nc * tok
     shared_rows = nt_all.reshape(plane_tok, width)
     shared_grads = up_all.reshape(plane_tok, width)
@@ -974,12 +1137,45 @@
             return carry
 
         lax.fori_loop(0, own_units // 256, shared_block, 0)
-        for k, acc in enumerate((acc_a, acc_b)):
-            cut = acc.at[first].reshape(num_seqs, nc, shard_len, width)
+    mail.settle(spread_gu + [passed_gu])
+    ggu = gu_buf
+    with jax.named_scope("b_shared_grads"):
+
+        def gate_up_grads(j, carry):
+            at = pl.ds(pl.multiple_of(j * 256, 256), 256)
+            piece = mm_tn(shared_rows[...], sh_dm[:, at])
+            ggu[:, :, :, :, at] = piece.reshape(ggu.shape[:4] + (256,)).astype(BF)
+            return carry
+
+        lax.fori_loop(0, 2 * own_units // 256, gate_up_grads, 0)
+        gsd[...] = mm_tn(sh_hidden[...], shared_grads[...]).reshape(gsd.shape).astype(BF)
+        sibling_gu = mail.post(sib_gu, [(ggu.at[:, :, 1 - f], sib_gu, sibling)])
+        sibling_sd = mail.post(sib_sd, [(gsd.at[:, 1 - f], sib_sd, sibling)])
+
+    with jax.named_scope("c_wait_returns"):
+        returns.wait_recv()
+    with jax.named_scope("c_column_mixture"):
+        cuts = [
+            acc.at[first].reshape(num_seqs, nc, shard_len, width) for acc in (acc_a, acc_b)
+        ]
+        for chip in range(nc):
+            results = join(rb[:, chip], (column_slots, width))
+            up_f = jnp.concatenate([up_all[q, chip] for q in range(num_seqs)], axis=0).astype(F32)
+            routed = [mm(hot_x[chip, k], results) for k in range(2)]
+            mixture = gates[chip][0] * routed[0] + gates[chip][1] * routed[1]
+            d_rows = mm(hot_d[chip, 0] + hot_d[chip, 1], results)
             for q in range(num_seqs):
-                sh_own[k, q, 0] = cut[q, c]
-                sh_own[k, q, 1] = cut[q, near_y if q == 0 else near_x]
-            sh_send[k] = cut[...].astype(BF)
+                at = slice(q * shard_len, (q + 1) * shard_len)
+                cuts[0][q, chip] = cuts[0][q, chip] + mixture[at]
+                cuts[1][q, chip] = cuts[1][q, chip] + d_rows[at]
+            d_gates = [jnp.sum(routed[k] * up_f, axis=1, keepdims=True) for k in range(2)]
+            spread_out = jnp.where(lane == 0, d_gates[0], jnp.where(lane == 1, d_gates[1], 0.0))
+            dg_send[chip] = jnp.transpose(spread_out, (1, 0))[:8]
+        for k in range(2):
+            for q in range(num_seqs):
+                sh_own[k, q, 0] = cuts[k][q, c]
+                sh_own[k, q, 1] = cuts[k][q, near_y if q == 0 else near_x]
+            sh_send[k] = cuts[k][...].astype(BF)
 
     def first_leg(inbox, box, lead):
         post = mail.open(inbox)
@@ -990,21 +1186,12 @@
         return post
 
     shared_first = first_leg(sh_in, sh_send, (slice(None),))
-
-    mail.settle([spread_gu, passed_gu])
-    ggu = gu_buf
-    with jax.named_scope("b_shared_grads"):
-
-        def gate_up_grads(j, carry):
-            at = pl.ds(pl.multiple_of(j * 256, 256), 256)
-            piece = mm_tn(shared_rows[...], sh_dm[:, at])
-            ggu[:, :, :, :, at] = piece.reshape(ggu.shape[:4] + (256,)).astype(BF)
-            return carry
-
-        lax.fori_loop(0, 2 * own_units // 256, gate_up_grads, 0)
-        gsd[...] = mm_tn(sh_hidden[...], shared_grads[...]).reshape(gsd.shape).astype(BF)
-        sibling_gu = mail.post(sib_gu, [(ggu.at[:, :, 1 - f], sib_gu, sibling)])
-        sibling_sd = mail.post(sib_sd, [(gsd.at[:, 1 - f], sib_sd, sibling)])
+    dg_copies = mail.post(
+        dg_in.at[others],
+        [(dg_send.at[wrap(c + s, nc)], dg_in.at[c], in_plane[s - 1]) for s in range(1, nc)],
+    )
+    dg_in[c] = dg_send[c]
+    pump(home, PUMPS[4])
 
     with jax.named_scope("b_reduce_shared"):
         def two_cores(copy, own, inbox):
@@ -1021,69 +1208,16 @@
         gu_copies = mail.post(
             zi_gu,
             [
-                (sib_gu.at[:, wrap(z + s, nz)], zi_gu.at[s - 1], in_column[s - 1])
-                for s in range(1, nz)
+                (sib_gu.at[:, to[1]], zi_gu.at[up - 1], to)
+                for to, up in zip(in_column, steps_up)
             ],
         )
         sd_copies = mail.post(
             zi_sd,
-            [(sib_sd.at[wrap(z + s, nz)], zi_sd.at[s - 1], in_column[s - 1]) for s in range(1, nz)],
-        )
-
-    with jax.named_scope("b_forward_rows"):
-        forwards = mail.open(ar.at[f])
-        for dz in range(nz):
-            row_copies[dz].wait_recv()
-            origin = wrap(z + nz - dz, nz)
-            forwards.add(ar.at[f, origin], ar.at[f, origin], sibling)
-        forwards.wait_recv()
-        keep_x, keep_d = (box_rows(CAP, num_experts, shift) for shift in (0, CAP))
-        for core in range(2):
-            at = slice(core * num_slots, (core + 1) * num_slots)
-            boxes = join(ar[core], (box_slots, width))
-            xs[at] = mm(keep_x, boxes).astype(BF)
-            ds[at] = mm(keep_d, boxes).astype(BF)
-    with jax.named_scope("b_wait_down"):
-        @pl.when(to_core == f)
-        def _():
-            expert_out.wait_recv(remote_out)
-            own_out.wait()
-
-        @pl.when(to_core != f)
-        def _():
-            expert_out.wait_recv()
-
-    acc_a[...] = jnp.zeros(acc_a.shape, F32)
-    acc_b[...] = jnp.zeros(acc_b.shape, F32)
-    for j in range(steps):
-        with jax.named_scope("b_wait_experts"):
-            own_in(j).wait()
-            expert_in[j].wait_recv()
-        with jax.named_scope("b_experts"):
-            ffn_block(
-                j, xs[...], ds[...], wie, woe, ex_hidden, ex_dm, acc_a, acc_b, half_units, step
-            )
-    mail.settle(row_copies)
-    pr = sb
-    with jax.named_scope("b_sibling_sum"):
-
-        def boxed(core):
-            at = pl.ds(pl.multiple_of(core * num_slots, num_slots), num_slots)
-            return (
-                mm_tn(keep_x, acc_a[at].astype(BF)) + mm_tn(keep_d, acc_b[at].astype(BF))
-            ).reshape(num_experts, BOX, width)
-
-        pr[...] = boxed(1 - f).astype(BF)
-        swap = mail.post(pin, [(pr, pin, sibling)])
-        ours = boxed(f)
-        swap.wait_recv()
-        fb[...] = (ours + pin[...].astype(F32)).astype(BF)
-        returns = mail.post(
-            rb.at[pl.ds(0, num_experts - 1)],
-            [(fb.at[to[1] * nc + to[0]], rb.at[z * nc + c], to) for to in everyone],
-        )
-        rb[z * nc + c] = fb[z * nc + c]
-    with jax.named_scope("b_second_leg"):
+            [(sib_sd.at[to[1]], zi_sd.at[up - 1], to) for to, up in zip(in_column, steps_up)],
+        )
+
+    with jax.named_scope("c_second_sum"):
         shared_first.wait_recv()
         for k in range(2):
             for q in range(num_seqs):
@@ -1096,74 +1230,11 @@
             ],
         )
 
-    gwi, gwo = wie, woe
-
-    def expert_grads(j, carry):
-        at = pl.ds(pl.multiple_of(j * 256, 256), 256)
-        gwi[:, at] = mm_tn(xs[...], ex_dm[:, at]).astype(BF)
-        return carry
-
-    home = []
-    home_in = mail.open(gwi.at[pl.ds(0, remote_rows)])
-    home_out = mail.open(gwo, keep=False)
-    remote_home = gwo.at[pl.ds(0, (nc - 1) * out_rows)]
-    home_in_own = pltpu.make_async_copy(
-        gwi.at[pl.ds(0, shard_rows)], gwi.at[pl.ds(0, shard_rows)], lsem.at[1]
-    )
-
-    def send_home_in(j, s, g, side):
-        owner = wrap(c + s, nc)
-        core = f if g == 0 else 1 - f
-        from_rows = pl.ds(
-            pl.multiple_of((2 * owner + core) * shard_rows, shard_rows), shard_rows
-        )
-        to_lane = pl.multiple_of(side * units + f * half_units + j * HOME, HOME)
-        src = gwi.at[from_rows, pl.ds(side * half_units + j * HOME, HOME)]
-        dst = ein_ref.at[c, :, pl.ds(to_lane, HOME)]
-        if s == 0 and g == 0:
-            pltpu.make_async_copy(src, dst, lsem.at[1]).start()
-        else:
-            home_in.add(src, dst, (owner, z, core))
-
-    def home_out_own(j):
-        return pltpu.make_async_copy(
-            gwo.at[pl.ds(j * out_rows, out_rows)], eout_ref.at[c], lsem.at[0]
-        )
-
-    def send_home_out(j):
-        to_block = f * nc + j
-
-        @pl.when(to_block == block)
-        def _():
-            home_out_own(j).start()
-
-        @pl.when(to_block != block)
-        def _():
-            home_out.add(
-                gwo.at[pl.ds(j * out_rows, out_rows)],
-                eout_ref.at[c],
-                (to_block // 2, z, wrap(to_block, 2)),
-            )
-
-    for side in range(2):
-        for j in range(half_units // HOME):
-            for s in range(1, nc + 1):
-                for g in range(2):
-                    home.append(functools.partial(send_home_in, j, s % nc, g, side))
-    for j in range(nc):
-        home.append(functools.partial(send_home_out, j))
-    with jax.named_scope("b_gwi"):
-        lax.fori_loop(0, 2 * half_units // 256, expert_grads, 0)
-    pump(home, PUMPS[1])
-    with jax.named_scope("b_gwo"):
-        for j in range(nc):
-            gwo[j * out_rows : (j + 1) * out_rows, :] = mm_tn(
-                ex_hidden[:, j * out_rows : (j + 1) * out_rows], ds[...]
-            ).astype(BF)
-
+    pump(home, PUMPS[5])
     with jax.named_scope("c_wait_shared"):
+        dg_copies.wait_recv()
         shared_second.wait_recv()
-        shared, d_normed = [
+        added, d_normed = [
             jnp.concatenate(
                 [
                     sh_own[k, q, 0] + sh_in[k, q, 0].astype(F32) + sh_end[k, q].astype(F32)
@@ -1173,23 +1244,19 @@
             )
             for k in range(2)
         ]
-    with jax.named_scope("c_wait_returns"):
-        returns.wait_recv()
     with jax.named_scope("c_combine"):
         attended = att_own[...].reshape(tok, width)
         inverse = inverse_rms(attended)
-        results = join(rb[...], (box_slots, width))
-        routed = [mm(dispatch[k], results) for k in range(2)]
-        mixture = gates[0] * routed[0] + gates[1] * routed[1]
-        out_ref[...] = (
-            (live * (attended + mixture + shared)).astype(BF).reshape(out_ref.shape)
-        )
-        d_gates = [jnp.sum(routed[k] * up_f, axis=1, keepdims=True) for k in range(2)]
-        mean_gate = gates[0] * d_gates[0] + gates[1] * d_gates[1]
-        d_logits = hots[0] * (gates[0] * (d_gates[0] - mean_gate)) + hots[1] * (
-            gates[1] * (d_gates[1] - mean_gate)
-        )
-        d_normed = d_normed + mm(anyone_d, results) + split_dot(mm_nt, d_logits, tail)
+        out_ref[...] = (live * (attended + added)).astype(BF).reshape(out_ref.shape)
+        hots = hot_lanes(picks[c])
+        own_gates = gates_of(hots, mm(normed, tail))
+        summed = turned(jnp.sum(dg_in[...], axis=0))
+        d_gates = [summed[:, k : k + 1] for k in range(2)]
+        mean_gate = own_gates[0] * d_gates[0] + own_gates[1] * d_gates[1]
+        d_logits = hots[0] * (own_gates[0] * (d_gates[0] - mean_gate)) + hots[1] * (
+            own_gates[1] * (d_gates[1] - mean_gate)
+        )
+        d_normed = d_normed + split_dot(mm_nt, d_logits, tail)
         d_attended = upstream + norm_back(attended, inverse, d_normed * ffn_gain)
         d_att_b = d_attended.astype(BF)
         d_context = mm_nt(d_att_b, wo_all[...]).astype(BF)
@@ -1261,7 +1328,7 @@
             for at, chip in enumerate((near_x if q == 0 else near_y, far)):
                 rs_first.add(part.at[q, chip], rs_in.at[q, at], to_x if q == 0 else to_y)
             grad_qkv = grad_qkv + mm_tn(normed_ref[q], d_merged)
-    pump(home, len(home) - 2)
+    pump(home, len(home))
     mail.settle([spread_wq, passed_wq])
     gq = wq_buf
     with jax.named_scope("c_reduce_q"):
@@ -1274,8 +1341,8 @@
         q_copies = mail.post(
             zi_q,
             [
-                (sib_q.at[:, wrap(z + s, nz)], zi_q.at[s - 1], in_column[s - 1])
-                for s in range(1, nz)
+                (sib_q.at[:, to[1]], zi_q.at[up - 1], to)
+                for to, up in zip(in_column, steps_up)
             ],
         )
     with jax.named_scope("c_second_leg"):
@@ -1313,7 +1380,6 @@
     with jax.named_scope("c_column_q"):
         pb_q[...] = column_sum(sib_q[:, z], q_copies, zi_q).astype(BF)
         final_q = hand_out(pb_q, fq_ref)
-    pump(home, len(home))
     with jax.named_scope("c_grad_in"):
         rs_second.wait_recv()
         for q in range(num_seqs):
@@ -1422,7 +1488,7 @@
     half_blocks = (nc, nz, rows_w)
     wide_cols = 3 * head_width + SMALL
     num_slots = num_experts * CAP
-    row_box = (num_experts, BOX, width)
+    row_box = (nz, nc, BOX, width)
     plane_tok = nc * tok
     outs = [
         (seq_shape, BF),
@@ -1443,6 +1509,13 @@
         out_specs=[pl.BlockSpec(memory_space=space) for space in [vm] * 6 + [hbm, hbm]],
         scratch_shapes=[
             vmem(full_len, 256, dtype=F32),
+            vmem(8, tok, dtype=jnp.int32),
+            vmem(nc, 8, tok, dtype=jnp.int32),
+            vmem(nc, tok, 128, dtype=F32),
+            vmem(nc, 2, tok, nz * BOX),
+            vmem(nc, 2, tok, nz * BOX),
+            vmem(nc, 8, tok, dtype=F32),
+            vmem(nc, 8, tok, dtype=F32),
             vmem(*group_shape),
             vmem(*seq_shape),
             vmem(*group_shape),

time: 203 us -> 190 us (0.936)
  Pallas kernels: 200 us -> 189 us
    pallas_call x1, Pallas kernels: 192 us -> 181 us  [fast_device(): pl.pallas_call(functools.partial(block_kernel, nc, nz), out_shape=[jax.Sh...]
where the time goes in v5:
time: 190 us
  Pallas kernels  189 us (99%)
    pallas_call x1, Pallas kernels, fast_device(): pl.pallas_call(functools.partial(block_kernel, nc, nz), out_shape=[jax.Sh...  181 us
    pallas_call x1, Pallas kernels, fast_device(): pl.pallas_call(functools.partial(finish_kernel, nc), grid=(ein.shape[0],...  7.73 us

profile of v5, /device:TPU:31, one launch (start us, length us, event | category | flops | bytes accessed | tf_op | source)
XLA Modules:
  0.0 189.9 jit_solution(12913131017186330301)
XLA Ops:
  0.6 181.4 %block_forward_backward.1 = (bf16[2,64,768]{2,1,0:T(8,128)(2,1)}, f32[2,64,768]{2,1,0:T(8,128)}, bf16[4,24,640]{2,1,0:T(8,128)(2,1)}, bf16[4,24,1024]{2,1,0:T(8,...) custom-call(s32[2]{0:T(128)} %len_ref.1, ...), custom_call_target="tpu_custom_call" | custom-call | flops 16000000000 | bytes 30000000 | tf_op jit(solution)/shard_map/block_forward_backward/pallas_call | solution.py:1503
  182.0 7.7 %widen_gradients.1 = (f32[24,2304]{1,0:T(8,128)}, f32[16,24]{1,0:T(8,128)}, f32[1,24]{1,0:T(1,128)}, f32[1,24]{1,0:T(1,128)}, f32[24,4096]{1,0:T(8,128)}, /*inde...) custom-call(bf16[4,24,640]{2,1,0:T(8,128)(2,1)} %get-tuple-element.3, ...), custom_call_target="tpu_custom_call" | custom-call | tf_op jit(solution)/shard_map/widen_gradients/pallas_call | solution.py:1620

commit v6 on v5

--- a/solution.py
+++ b/solution.py
@@ -420,7 +420,7 @@
 PUMPS = (3, 17, 6, 0, 6, 6)
 POSTS = 64
 EARLY = 2
-GATE_UP, DOWN = 1, 2
+LATE = 1
 WIDEN = 1
 
 
@@ -502,6 +502,9 @@
         if keep:
             self.sent.append(post)
         return post
+
+    def at(self, index, like):
+        return Post(self.send.at[index], self.recv.at[index], like, self.device)
 
     def post(self, like, moves):
         post = self.open(like)
@@ -720,6 +723,7 @@
     slot = wrap(block, nc)
     out_lands = pl.ds(pl.multiple_of(slot * out_rows, out_rows), out_rows)
     remote_rows = (2 * nc - 1) * shard_rows
+    first_in = mail.count
     expert_in = [
         mail.open(wie.at[pl.ds(0, remote_rows), pl.ds(0, 2 * step)]) for _ in range(steps)
     ]
@@ -744,12 +748,16 @@
         like = wie.at[pl.ds(0, shard_rows), pl.ds(0, 2 * step)]
         return pltpu.make_async_copy(like, like, lsem.at[1 + j])
 
+    def nth_block(j, chip):
+        return wrap(2 * j + j // 2 + 2 * wrap(chip, 2), steps)
+
     def send_in(j, s, g, side):
         owner = wrap(c + s, nc)
+        at = nth_block(j, owner) * step
         core = f if g == 0 else 1 - f
-        from_lane = pl.multiple_of(side * units + core * half_units + j * step, step)
+        from_lane = pl.multiple_of(side * units + core * half_units + at, step)
         src = win_ref.at[owner, :, pl.ds(from_lane, step)]
-        dst = wie.at[lands, pl.ds(side * half_units + j * step, step)]
+        dst = wie.at[lands, pl.ds(pl.multiple_of(side * half_units + at, step), step)]
         if s == 0 and g == 0:
             pltpu.make_async_copy(src, dst, lsem.at[1 + j]).start()
         else:
@@ -879,8 +887,12 @@
     with jax.named_scope("a_route"):
         meta_copies.wait_recv()
         meta_all[c] = meta_own[...]
-        for chip in range(nc):
+
+        def route_one(chip, carry):
             route(chip)
+            return carry
+
+        lax.fori_loop(0, nc, route_one, 0)
     wo_st[c] = wo_ref[...]
     for side in range(2):
         at = pl.ds(pl.multiple_of(side * units + c * own_units, own_units), own_units)
@@ -969,15 +981,22 @@
             post.wait_recv()
     with jax.named_scope("b_dispatch"):
         tail = w_ref[:, tail_at:]
-        gates = []
-        for chip in range(nc):
+
+        def box_rows_of(chip, carry):
             normed = jnp.concatenate([nt_all[q, chip] for q in range(num_seqs)], axis=0)
-            gates.append(gates_of(hot_lanes(picks[chip]), mm(normed, tail)))
+            columns = picks[chip]
+            gates = gates_of(hot_lanes(columns), mm(normed, tail))
+            picks[chip] = jnp.where(lane == 3, gates[0], jnp.where(lane == 4, gates[1], columns))
             up_f = jnp.concatenate([up_all[q, chip] for q in range(num_seqs)], axis=0).astype(F32)
             boxes = mm_tn(hot_x[chip, 0] + hot_x[chip, 1], normed)
             for k in range(2):
-                boxes = boxes + mm_tn(hot_d[chip, k], (gates[chip][k] * up_f).astype(BF))
-            sb[:, chip] = boxes.reshape(nz, BOX, width).astype(BF)
+                boxes = boxes + mm_tn(hot_d[chip, k], (gates[k] * up_f).astype(BF))
+            boxes = boxes.reshape(nz, BOX, width).astype(BF)
+            for plane in range(nz):
+                sb[plane, chip] = boxes[plane]
+            return carry
+
+        lax.fori_loop(0, nc, box_rows_of, 0)
         row_copies = [
             mail.post(ar.at[f, 0], [(sb.at[to[1]], ar.at[f, z], to)]) for to in in_column
         ]
@@ -1012,16 +1031,21 @@
     gwi, gwo = wie, woe
 
     def expert_grads(j):
+        low = nth_block(j, c) * step
         for side in range(2):
-            at = pl.ds(side * half_units + j * step, step)
+            at = pl.ds(pl.multiple_of(side * half_units + low, step), step)
             gwi[:, at] = mm_tn(xs[...], ex_dm[:, at]).astype(BF)
-        at = pl.ds(j * step, step)
+        at = pl.ds(pl.multiple_of(low, step), step)
         gwo[at, :] = mm_tn(ex_hidden[:, at], ds[...]).astype(BF)
-        for s in range(1, nc + 1):
-            for g in range(2):
-                for side in range(2):
-                    home.append(functools.partial(send_home_in, j, s % nc, g, side))
-        home.append(functools.partial(send_home_out, j))
+
+    def homeward(j):
+        moves = [
+            functools.partial(send_home_in, j, s % nc, g, side)
+            for s in range(1, nc + 1)
+            for g in range(2)
+            for side in range(2)
+        ]
+        return moves + [functools.partial(send_home_out, j)]
 
     home = []
     home_in = mail.open(gwi.at[pl.ds(0, remote_rows)])
@@ -1037,21 +1061,23 @@
         from_rows = pl.ds(
             pl.multiple_of((2 * owner + core) * shard_rows, shard_rows), shard_rows
         )
-        to_lane = pl.multiple_of(side * units + f * half_units + j * step, step)
-        src = gwi.at[from_rows, pl.ds(side * half_units + j * step, step)]
+        low = nth_block(j, c) * step
+        to_lane = pl.multiple_of(side * units + f * half_units + low, step)
+        src = gwi.at[from_rows, pl.ds(pl.multiple_of(side * half_units + low, step), step)]
         dst = ein_ref.at[c, :, pl.ds(to_lane, step)]
         if s == 0 and g == 0:
             pltpu.make_async_copy(src, dst, lsem.at[1]).start()
         else:
             home_in.add(src, dst, (owner, z, core))
 
+    def home_rows(j):
+        return gwo.at[pl.ds(pl.multiple_of(nth_block(j, c) * out_rows, out_rows), out_rows)]
+
     def home_out_own(j):
-        return pltpu.make_async_copy(
-            gwo.at[pl.ds(j * out_rows, out_rows)], eout_ref.at[c], lsem.at[0]
-        )
+        return pltpu.make_async_copy(home_rows(j), eout_ref.at[c], lsem.at[0])
 
     def send_home_out(j):
-        to_block = f * nc + j
+        to_block = f * nc + nth_block(j, c)
 
         @pl.when(to_block == block)
         def _():
@@ -1060,32 +1086,49 @@
         @pl.when(to_block != block)
         def _():
             home_out.add(
-                gwo.at[pl.ds(j * out_rows, out_rows)],
+                home_rows(j),
                 eout_ref.at[c],
                 (to_block // 2, z, wrap(to_block, 2)),
             )
 
     acc_a[...] = jnp.zeros(acc_a.shape, F32)
     acc_b[...] = jnp.zeros(acc_b.shape, F32)
-    for j in range(steps):
+    early = [move for j in range(EARLY) for move in homeward(j)]
+    home = [move for j in range(EARLY, steps) for move in homeward(j)]
+    late_gate_up = mail.open(gu_buf.at[:, planes, 0, :, pl.ds(0, own_units)])
+    spread_sd = mail.open(sd_all.at[planes, 0])
+    spread_gu.append(late_gate_up)
+
+    def expert_block(j, carry):
         with jax.named_scope("b_wait_experts"):
             own_in(j).wait()
-            expert_in[j].wait_recv()
-        if j == steps - 1:
-            pump(home, len(home))
+            mail.at(first_in + j, expert_in[0].like).wait_recv()
+
+        @pl.when(j == steps - 1)
+        def _():
+            pump(early, len(early))
+
         with jax.named_scope("b_experts"):
             ffn_block(
-                j, xs[...], ds[...], wie, woe, ex_hidden, ex_dm, acc_a, acc_b, half_units, step
+                nth_block(j, c), xs[...], ds[...], wie, woe, ex_hidden, ex_dm, acc_a, acc_b,
+                half_units, step,
             )
-        if j < EARLY:
+
+        @pl.when(j < EARLY)
+        def _():
             with jax.named_scope("b_early_grads"):
                 expert_grads(j)
-        if j == GATE_UP:
-            spread_gu.append(spread_gate_up(1))
-        if j == DOWN:
-            spread_sd = mail.post(
-                sd_all.at[planes, 0], [(sd_ref, sd_all.at[z, f], peer) for peer in in_column]
-            )
+
+        @pl.when(j == LATE)
+        def _():
+            at = pl.ds(own_units, own_units)
+            for peer in in_column:
+                late_gate_up.add(gu_st.at[:, :, at], gu_buf.at[:, z, f, :, at], peer)
+                spread_sd.add(sd_ref, sd_all.at[z, f], peer)
+
+        return carry
+
+    lax.fori_loop(0, steps, expert_block, 0)
     mail.settle(row_copies)
     pr = sb
     with jax.named_scope("b_sibling_sum"):
@@ -1106,8 +1149,12 @@
         )
         rb[z] = fb[z]
     with jax.named_scope("b_expert_grads"):
-        for j in range(EARLY, steps):
+
+        def late_grads(j, carry):
             expert_grads(j)
+            return carry
+
+        lax.fori_loop(EARLY, steps, late_grads, 0)
     pump(home, PUMPS[1])
 
     with jax.named_scope("b_forward_gu"):
@@ -1158,11 +1205,16 @@
         cuts = [
             acc.at[first].reshape(num_seqs, nc, shard_len, width) for acc in (acc_a, acc_b)
         ]
-        for chip in range(nc):
-            results = join(rb[:, chip], (column_slots, width))
+
+        def add_results(chip, carry):
+            results = join(
+                jnp.concatenate([rb[plane, chip].astype(F32) for plane in range(nz)], axis=0),
+                (column_slots, width),
+            )
             up_f = jnp.concatenate([up_all[q, chip] for q in range(num_seqs)], axis=0).astype(F32)
+            gates = [picks[chip][:, 3 + k : 4 + k] for k in range(2)]
             routed = [mm(hot_x[chip, k], results) for k in range(2)]
-            mixture = gates[chip][0] * routed[0] + gates[chip][1] * routed[1]
+            mixture = gates[0] * routed[0] + gates[1] * routed[1]
             d_rows = mm(hot_d[chip, 0] + hot_d[chip, 1], results)
             for q in range(num_seqs):
                 at = slice(q * shard_len, (q + 1) * shard_len)
@@ -1171,6 +1223,9 @@
             d_gates = [jnp.sum(routed[k] * up_f, axis=1, keepdims=True) for k in range(2)]
             spread_out = jnp.where(lane == 0, d_gates[0], jnp.where(lane == 1, d_gates[1], 0.0))
             dg_send[chip] = jnp.transpose(spread_out, (1, 0))[:8]
+            return carry
+
+        lax.fori_loop(0, nc, add_results, 0)
         for k in range(2):
             for q in range(num_seqs):
                 sh_own[k, q, 0] = cuts[k][q, c]
@@ -1416,48 +1471,67 @@
 def finish_kernel(
     nc, fq_ref, fgu_ref, wqkv_ref, ga_ref, ein_ref, eout_ref, out_in, gin_in, fsd_in, fwo_in,
     gq_ref, gr_ref, gga_ref, ggf_ref, ggu_ref, oin_ref, oout_ref, out_ref, gin_ref, fsd_ref, fwo_ref,
+    narrow_in, narrow_out, wide_in, wide_out, sems,
 ):
-    oin_ref[...] = ein_ref[...].astype(F32)
-    oout_ref[...] = eout_ref[...].astype(F32)
-
-    @pl.when((pl.program_id(0) == 0) & (pl.program_id(1) == 0))
-    def _():
-        out_ref[...] = out_in[...]
-        gin_ref[...] = gin_in[...]
-        fsd_ref[...] = fsd_in[...]
-        fwo_ref[...] = fwo_in[...]
-        rows_w = wqkv_ref.shape[0]
-        head_width = wqkv_ref.shape[1] // 3 // nc
-        grads = jnp.concatenate(
-            [
-                fq_ref[i, :, side * head_width : (side + 1) * head_width].astype(F32)
-                for side in range(3)
-                for i in range(nc)
-            ],
-            axis=1,
-        )
-        gq_ref[...] = grads
-        own_units = fgu_ref.shape[2] // 2
-        ggu_ref[...] = jnp.concatenate(
-            [
-                fgu_ref[i, :, side * own_units : (side + 1) * own_units].astype(F32)
-                for side in range(2)
-                for i in range(nc)
-            ],
-            axis=1,
-        )
-        extras = jnp.sum(fq_ref[:, :, 3 * head_width - SMALL :].astype(F32), axis=0)
-        num_experts = gr_ref.shape[0]
-        first = jnp.sum(wqkv_ref[...].astype(F32) * grads, axis=1, keepdims=True)
-        lane = lax.broadcasted_iota(jnp.int32, (rows_w, 128), 1)
-        both = jnp.where(lane == SMALL + num_experts, first, extras)
-        turned = jnp.transpose(
-            jnp.concatenate([both, jnp.zeros((128 - rows_w, 128), F32)], axis=0), (1, 0)
-        )
-        gr_ref[...] = turned[SMALL : SMALL + num_experts, :rows_w]
-        at = SMALL + num_experts
-        gga_ref[...] = turned[at : at + 1, :rows_w] / ga_ref[...].astype(F32)
-        ggf_ref[...] = turned[at + 1 : at + 2, :rows_w]
+    pieces = []
+    for e in range(ein_ref.shape[0]):
+        for source, narrow, widened, target in (
+            (ein_ref, narrow_in, wide_in, oin_ref),
+            (eout_ref, narrow_out, wide_out, oout_ref),
+        ):
+            rows = source.shape[1] // WIDEN
+            for k in range(WIDEN):
+                at = (e, pl.ds(k * rows, rows))
+                pieces.append((at, source, narrow, widened, target))
+    arriving = []
+    for i, (at, source, narrow, _, _) in enumerate(pieces):
+        arriving.append(pltpu.make_async_copy(source.at[at], narrow.at[at], sems.at[0, i]))
+        arriving[-1].start()
+    out_ref[...] = out_in[...]
+    gin_ref[...] = gin_in[...]
+    fsd_ref[...] = fsd_in[...]
+    fwo_ref[...] = fwo_in[...]
+    rows_w = wqkv_ref.shape[0]
+    head_width = wqkv_ref.shape[1] // 3 // nc
+    grads = jnp.concatenate(
+        [
+            fq_ref[i, :, side * head_width : (side + 1) * head_width].astype(F32)
+            for side in range(3)
+            for i in range(nc)
+        ],
+        axis=1,
+    )
+    gq_ref[...] = grads
+    own_units = fgu_ref.shape[2] // 2
+    ggu_ref[...] = jnp.concatenate(
+        [
+            fgu_ref[i, :, side * own_units : (side + 1) * own_units].astype(F32)
+            for side in range(2)
+            for i in range(nc)
+        ],
+        axis=1,
+    )
+    extras = jnp.sum(fq_ref[:, :, 3 * head_width - SMALL :].astype(F32), axis=0)
+    num_experts = gr_ref.shape[0]
+    first = jnp.sum(wqkv_ref[...].astype(F32) * grads, axis=1, keepdims=True)
+    lane = lax.broadcasted_iota(jnp.int32, (rows_w, 128), 1)
+    both = jnp.where(lane == SMALL + num_experts, first, extras)
+    turned = jnp.transpose(
+        jnp.concatenate([both, jnp.zeros((128 - rows_w, 128), F32)], axis=0), (1, 0)
+    )
+    gr_ref[...] = turned[SMALL : SMALL + num_experts, :rows_w]
+    at = SMALL + num_experts
+    gga_ref[...] = turned[at : at + 1, :rows_w] / ga_ref[...].astype(F32)
+    ggf_ref[...] = turned[at + 1 : at + 2, :rows_w]
+
+    leaving = []
+    for i, (at, _, narrow, widened, target) in enumerate(pieces):
+        arriving[i].wait()
+        widened[at] = narrow[at].astype(F32)
+        leaving.append(pltpu.make_async_copy(widened.at[at], target.at[at], sems.at[1, i]))
+        leaving[-1].start()
+    for copy in leaving:
+        copy.wait()
 
 
 def vmem(*shape, dtype=jnp.bfloat16):
@@ -1597,12 +1671,6 @@
         w_gate_up, w_out, w_shared_down, w_experts_in, w_experts_out,
     )
 
-    def whole(shape):
-        return pl.BlockSpec(shape, lambda e, j: (0,) * len(shape))
-
-    def one(shape):
-        return pl.BlockSpec((1, shape[1], shape[2] // WIDEN), lambda e, j: (e, 0, j))
-
     ins = [fq, fgu, w_qkv, gain_attn.reshape(1, rows_w), ein, eout, out, gin, fsd, fwo]
     results = [
         (w_qkv.shape, F32),
@@ -1619,11 +1687,17 @@
     ]
     grad_qkv, grad_router, grad_ga, grad_gf, grad_gu, grad_in, grad_out, out, gin, fsd, fwo = pl.pallas_call(
         functools.partial(finish_kernel, nc),
-        grid=(ein.shape[0], WIDEN),
         out_shape=[jax.ShapeDtypeStruct(shape, dtype) for shape, dtype in results],
-        in_specs=[one(x.shape) if i in (4, 5) else whole(x.shape) for i, x in enumerate(ins)],
+        in_specs=[pl.BlockSpec(memory_space=hbm if i in (4, 5) else vm) for i in range(len(ins))],
         out_specs=[
-            one(shape) if i in (5, 6) else whole(shape) for i, (shape, _) in enumerate(results)
+            pl.BlockSpec(memory_space=hbm if i in (5, 6) else vm) for i in range(len(results))
+        ],
+        scratch_shapes=[
+            vmem(*ein.shape),
+            vmem(*eout.shape),
+            vmem(*ein.shape, dtype=F32),
+            vmem(*eout.shape, dtype=F32),
+            dma((2, 2 * ein.shape[0] * WIDEN)),
         ],
         compiler_params=pltpu.CompilerParams(vmem_limit_bytes=VMEM_BYTES),
         name="widen_gradients",

time: 190 us -> 186 us (0.979)
  Pallas kernels: 189 us -> 183 us
    pallas_call x1, Pallas kernels: 181 us -> 176 us  [fast_device(): pl.pallas_call(functools.partial(block_kernel, nc, nz), out_shape=[jax.Sh...]
where the time goes in v6:
time: 186 us; the launch traced here: 184 us
  Pallas kernels  183 us (98%)
    pallas_call x1, Pallas kernels, fast_device(): pl.pallas_call(functools.partial(block_kernel, nc, nz), out_shape=[jax.Sh...  176 us
    pallas_call x1, Pallas kernels, fast_device(): pl.pallas_call(functools.partial(finish_kernel, nc), out_shape=[jax.Shape...  7.42 us

profile of v6, /device:TPU:31, one launch (start us, length us, event | category | flops | bytes accessed | tf_op | source)
XLA Modules:
  0.0 184.1 jit_solution(11407638704550074111)
XLA Ops:
  0.6 175.9 %block_forward_backward.1 = (bf16[2,64,768]{2,1,0:T(8,128)(2,1)}, f32[2,64,768]{2,1,0:T(8,128)}, bf16[4,24,640]{2,1,0:T(8,128)(2,1)}, bf16[4,24,1024]{2,1,0:T(8,...) custom-call(s32[2]{0:T(128)} %len_ref.1, ...), custom_call_target="tpu_custom_call" | custom-call | flops 16000000000 | bytes 30000000 | tf_op jit(solution)/shard_map/block_forward_backward/pallas_call | solution.py:1577
  176.6 7.4 %widen_gradients.1 = (f32[24,2304]{1,0:T(8,128)}, f32[16,24]{1,0:T(8,128)}, f32[1,24]{1,0:T(1,128)}, f32[1,24]{1,0:T(1,128)}, f32[24,4096]{1,0:T(8,128)}, /*inde...) custom-call(bf16[4,24,640]{2,1,0:T(8,128)(2,1)} %get-tuple-element.3, ...), custom_call_target="tpu_custom_call" | custom-call | tf_op jit(solution)/shard_map/widen_gradients/pallas_call | solution.py:1688

commit v7 on v6

--- a/solution.py
+++ b/solution.py
@@ -417,7 +417,7 @@
 BOX = 40
 SMALL = 64
 VMEM_BYTES = 63 * 1024 * 1024
-PUMPS = (3, 17, 6, 0, 6, 6)
+PUMPS = (3, 6, 6, 0, 6, 6)
 POSTS = 64
 EARLY = 2
 LATE = 1
@@ -612,15 +612,17 @@
 
 def block_kernel(
     nc, nz,
-    len_ref, hid_ref, go_ref, ids_ref, rank_ref, wqkv_ref, router_ref, ga_ref, gf_ref, gu_ref,
-    wo_ref, sd_ref, win_ref, wout_ref,
-    out_ref, gin_ref, fq_ref, fgu_ref, fsd_ref, fwo_ref, ein_ref, eout_ref,
+    len_ref, ids_in, rank_in, wqkv_in, router_in, ga_in, gf_in, hid_in, gu_in, wo_in, sd_in, go_in,
+    win_ref, wout_ref,
+    out_to, gin_to, fq_ref, fgu_ref, fsd_to, fwo_to, ein_ref, eout_ref,
+    ids_ref, rank_ref, wqkv_ref, router_ref, ga_ref, gf_ref, hid_ref, gu_ref, wo_ref, sd_ref, go_ref,
+    out_ref, gin_ref, fsd_ref, fwo_ref,
     turn_ref, meta_own, meta_all, picks, hot_x, hot_d, dg_send, dg_in, hid_all, up_own, up_all, wq_own, wq_st, wq_buf, w_ref, gu_st, gu_buf, gu_all, wo_st, wo_buf,
     wo_all, sd_all, wie, woe, normed_ref, qkv_ref, ctx_all, att_own, nt_all,
     sb, ar, xs, ds, acc_a, acc_b, sh_own, sh_hidden, sh_dm, sh_send, sh_in, sh_mid, sh_end,
     ex_hidden, ex_dm, pin, fb, rb, gsd, da_own, dctx_send, dctx_all, part, part_own, rs_in, rs_mid, rs_end,
     sib_gu, zi_gu, pb_gu, sib_q, zi_q, pb_q, sib_sd, zi_sd, sib_wo, zi_wo, pb_wo, in_wo,
-    send, recv, lsem,
+    send, recv, lsem, isem, osem,
 ):
     c, z, f = place()
     near_x, near_y = c + 1 - 2 * wrap(c, 2), wrap(c + 2, nc)
@@ -634,6 +636,24 @@
     partners = in_plane + in_column + [sibling] + across
     with jax.named_scope("s_greet"):
         greet(partners)
+
+    loads = [
+        pltpu.make_async_copy(source, target, isem.at[i])
+        for i, (source, target) in enumerate(
+            (
+                (ids_in, ids_ref), (rank_in, rank_ref), (wqkv_in, wqkv_ref),
+                (router_in, router_ref), (ga_in, ga_ref), (gf_in, gf_ref), (hid_in, hid_ref),
+                (gu_in, gu_ref), (wo_in, wo_ref), (sd_in, sd_ref), (go_in, go_ref),
+            )
+        )
+    ]
+    for load in loads:
+        load.start()
+    stores = []
+
+    def store(source, target):
+        stores.append(pltpu.make_async_copy(source, target, osem.at[len(stores)]))
+        stores[-1].start()
 
     num_seqs, shard_len, width = hid_ref.shape
     full_len = nc * shard_len
@@ -652,6 +672,8 @@
     block_rows = nz * 2 * rows_w
     mail = Courier(send, recv, sibling)
 
+    for load in loads:
+        load.wait()
     small = jnp.concatenate(
         [
             router_ref[...].astype(F32),
@@ -1303,6 +1325,7 @@
         attended = att_own[...].reshape(tok, width)
         inverse = inverse_rms(attended)
         out_ref[...] = (live * (attended + added)).astype(BF).reshape(out_ref.shape)
+        store(out_ref, out_to)
         hots = hot_lanes(picks[c])
         own_gates = gates_of(hots, mm(normed, tail))
         summed = turned(jnp.sum(dg_in[...], axis=0))
@@ -1354,6 +1377,23 @@
 
     with jax.named_scope("c_wait_dctx"):
         dctx_copies.wait_recv()
+    def column_sum(own, copies, inbox):
+        copies.wait_recv()
+        total = own.astype(F32)
+        for s in range(1, nz):
+            total = total + inbox[s - 1].astype(F32)
+        return total
+
+    def hand_out(box, final):
+        store(box.at[c], final.at[c])
+        return mail.post(
+            final.at[others],
+            [(box.at[wrap(c + s, nc)], final.at[c], in_plane[s - 1]) for s in range(1, nc)],
+        )
+
+    with jax.named_scope("c_column_gu"):
+        pb_gu[...] = column_sum(sib_gu[:, z], gu_copies, zi_gu).astype(BF)
+        final_gu = hand_out(pb_gu, fgu_ref)
     grad_qkv = jnp.zeros((width, 3 * head_width), F32)
     rs_first = mail.open(rs_in)
     for q in range(num_seqs):
@@ -1410,28 +1450,16 @@
             [(rs_mid.at[q], rs_end.at[q], to_y if q == 0 else to_x) for q in range(num_seqs)],
         )
 
-    def column_sum(own, copies, inbox):
-        copies.wait_recv()
-        total = own.astype(F32)
-        for s in range(1, nz):
-            total = total + inbox[s - 1].astype(F32)
-        return total
-
-    def hand_out(box, final):
-        final[c] = box[c]
-        return mail.post(
-            final.at[others],
-            [(box.at[wrap(c + s, nc)], final.at[c], in_plane[s - 1]) for s in range(1, nc)],
-        )
-
-    with jax.named_scope("c_column_gu"):
-        pb_gu[...] = column_sum(sib_gu[:, z], gu_copies, zi_gu).astype(BF)
-        final_gu = hand_out(pb_gu, fgu_ref)
     with jax.named_scope("c_column_sd"):
         fsd_ref[...] = column_sum(sib_sd[z], sd_copies, zi_sd)
+        store(fsd_ref, fsd_to)
     with jax.named_scope("c_column_wo"):
         pb_wo[...] = column_sum(sib_wo[:, z], wo_copies, zi_wo).astype(BF)
-        final_wo = hand_out(pb_wo, in_wo)
+        in_wo[c] = pb_wo[c]
+        final_wo = mail.post(
+            in_wo.at[others],
+            [(pb_wo.at[wrap(c + s, nc)], in_wo.at[c], in_plane[s - 1]) for s in range(1, nc)],
+        )
     with jax.named_scope("c_column_q"):
         pb_q[...] = column_sum(sib_q[:, z], q_copies, zi_q).astype(BF)
         final_q = hand_out(pb_q, fq_ref)
@@ -1441,9 +1469,11 @@
             d_normed = part_own[q, c] + rs_in[q, 0].astype(F32) + rs_end[q].astype(F32)
             rows = hid_ref[q].astype(F32)
             gin_ref[q] = gin_ref[q] + norm_back(rows, inverse_rms(rows), d_normed * attn_gain)
+        store(gin_ref, gin_to)
     with jax.named_scope("c_final"):
         final_wo.wait_recv()
         fwo_ref[...] = jnp.sum(in_wo[...].astype(F32), axis=0)
+        store(fwo_ref, fwo_to)
         final_gu.wait_recv()
         final_q.wait_recv()
     with jax.named_scope("c_wait_home"):
@@ -1465,13 +1495,17 @@
 
     assert mail.count <= POSTS, mail.count
     with jax.named_scope("z_finish"):
+        for copy in stores:
+            copy.wait()
         mail.finish()
 
 
 def finish_kernel(
-    nc, fq_ref, fgu_ref, wqkv_ref, ga_ref, ein_ref, eout_ref, out_in, gin_in, fsd_in, fwo_in,
-    gq_ref, gr_ref, gga_ref, ggf_ref, ggu_ref, oin_ref, oout_ref, out_ref, gin_ref, fsd_ref, fwo_ref,
-    narrow_in, narrow_out, wide_in, wide_out, sems,
+    nc, fq_in, fgu_in, wqkv_in, ga_in, ein_ref, eout_ref, out_in, gin_in, fsd_in, fwo_in,
+    gq_to, gr_to, gga_to, ggf_to, ggu_to, oin_ref, oout_ref, out_to, gin_to, fsd_to, fwo_to,
+    narrow_in, narrow_out, wide_in, wide_out,
+    fq_ref, fgu_ref, wqkv_ref, ga_ref, out_ref, gin_ref, fsd_ref, fwo_ref,
+    gq_ref, gr_ref, gga_ref, ggf_ref, ggu_ref, sems, isem, osem,
 ):
     pieces = []
     for e in range(ein_ref.shape[0]):
@@ -1483,14 +1517,45 @@
             for k in range(WIDEN):
                 at = (e, pl.ds(k * rows, rows))
                 pieces.append((at, source, narrow, widened, target))
+    loads = [
+        pltpu.make_async_copy(source, target, isem.at[i])
+        for i, (source, target) in enumerate(
+            (
+                (fq_in, fq_ref), (fgu_in, fgu_ref), (wqkv_in, wqkv_ref), (ga_in, ga_ref),
+                (out_in, out_ref), (gin_in, gin_ref), (fsd_in, fsd_ref), (fwo_in, fwo_ref),
+            )
+        )
+    ]
     arriving = []
     for i, (at, source, narrow, _, _) in enumerate(pieces):
         arriving.append(pltpu.make_async_copy(source.at[at], narrow.at[at], sems.at[0, i]))
         arriving[-1].start()
-    out_ref[...] = out_in[...]
-    gin_ref[...] = gin_in[...]
-    fsd_ref[...] = fsd_in[...]
-    fwo_ref[...] = fwo_in[...]
+        if i == 1:
+            for load in loads:
+                load.start()
+    stores = []
+
+    def store(source, target):
+        stores.append(pltpu.make_async_copy(source, target, osem.at[len(stores)]))
+        stores[-1].start()
+
+    leaving = []
+
+    def widen(i):
+        at, _, narrow, widened, target = pieces[i]
+        arriving[i].wait()
+        widened[at] = narrow[at].astype(F32)
+        leaving.append(pltpu.make_async_copy(widened.at[at], target.at[at], sems.at[1, i]))
+        leaving[-1].start()
+
+    for i in range(len(pieces) // 2):
+        widen(i)
+    for load in loads:
+        load.wait()
+    for source, target in (
+        (out_ref, out_to), (gin_ref, gin_to), (fsd_ref, fsd_to), (fwo_ref, fwo_to)
+    ):
+        store(source, target)
     rows_w = wqkv_ref.shape[0]
     head_width = wqkv_ref.shape[1] // 3 // nc
     grads = jnp.concatenate(
@@ -1524,13 +1589,13 @@
     gga_ref[...] = turned[at : at + 1, :rows_w] / ga_ref[...].astype(F32)
     ggf_ref[...] = turned[at + 1 : at + 2, :rows_w]
 
-    leaving = []
-    for i, (at, _, narrow, widened, target) in enumerate(pieces):
-        arriving[i].wait()
-        widened[at] = narrow[at].astype(F32)
-        leaving.append(pltpu.make_async_copy(widened.at[at], target.at[at], sems.at[1, i]))
-        leaving[-1].start()
-    for copy in leaving:
+    for source, target in (
+        (gq_ref, gq_to), (gr_ref, gr_to), (gga_ref, gga_to), (ggf_ref, ggf_to), (ggu_ref, ggu_to)
+    ):
+        store(source, target)
+    for i in range(len(pieces) // 2, len(pieces)):
+        widen(i)
+    for copy in leaving + stores:
         copy.wait()
 
 
@@ -1574,14 +1639,29 @@
         (w_experts_in.shape, BF),
         (w_experts_out.shape, BF),
     ]
+    small_ins = [
+        expert_ids.transpose(0, 1, 3, 2),
+        route_rank.reshape(1, tok),
+        w_qkv,
+        w_router.T,
+        gain_attn.reshape(1, rows_w),
+        gain_ffn.reshape(1, rows_w),
+        hidden_in.reshape(seq_shape),
+        w_gate_up,
+        w_out,
+        w_shared_down,
+        grad_output.reshape(seq_shape),
+    ]
     out, gin, fq, fgu, fsd, fwo, ein, eout = pl.pallas_call(
         functools.partial(block_kernel, nc, nz),
         out_shape=[jax.ShapeDtypeStruct(shape, dtype) for shape, dtype in outs],
         in_specs=[
-            pl.BlockSpec(memory_space=space) for space in [sm] + [vm] * 11 + [hbm, hbm]
+            pl.BlockSpec(memory_space=space) for space in [sm] + [hbm] * 13
         ],
-        out_specs=[pl.BlockSpec(memory_space=space) for space in [vm] * 6 + [hbm, hbm]],
+        out_specs=[pl.BlockSpec(memory_space=hbm) for _ in outs],
         scratch_shapes=[
+            *[vmem(*x.shape, dtype=x.dtype) for x in small_ins],
+            *[vmem(*outs[i][0], dtype=outs[i][1]) for i in (0, 1, 4, 5)],
             vmem(full_len, 256, dtype=F32),
             vmem(8, tok, dtype=jnp.int32),
             vmem(nc, 8, tok, dtype=jnp.int32),
@@ -1653,6 +1733,8 @@
             dma((POSTS,)),
             dma((POSTS,)),
             dma((1 + half_units // 256,)),
+            dma((len(small_ins),)),
+            dma((6,)),
         ],
         compiler_params=pltpu.CompilerParams(
             collective_id=0, has_side_effects=True, vmem_limit_bytes=VMEM_BYTES
@@ -1662,13 +1744,7 @@
         ),
         name="block_forward_backward",
     )(
-        seq_lengths,
-        hidden_in.reshape(seq_shape),
-        grad_output.reshape(seq_shape),
-        expert_ids.transpose(0, 1, 3, 2),
-        route_rank.reshape(1, tok),
-        w_qkv, w_router.T, gain_attn.reshape(1, rows_w), gain_ffn.reshape(1, rows_w),
-        w_gate_up, w_out, w_shared_down, w_experts_in, w_experts_out,
+        seq_lengths, *small_ins, w_experts_in, w_experts_out
     )
 
     ins = [fq, fgu, w_qkv, gain_attn.reshape(1, rows_w), ein, eout, out, gin, fsd, fwo]
@@ -1688,16 +1764,18 @@
     grad_qkv, grad_router, grad_ga, grad_gf, grad_gu, grad_in, grad_out, out, gin, fsd, fwo = pl.pallas_call(
         functools.partial(finish_kernel, nc),
         out_shape=[jax.ShapeDtypeStruct(shape, dtype) for shape, dtype in results],
-        in_specs=[pl.BlockSpec(memory_space=hbm if i in (4, 5) else vm) for i in range(len(ins))],
-        out_specs=[
-            pl.BlockSpec(memory_space=hbm if i in (5, 6) else vm) for i in range(len(results))
-        ],
+        in_specs=[pl.BlockSpec(memory_space=hbm) for _ in ins],
+        out_specs=[pl.BlockSpec(memory_space=hbm) for _ in results],
         scratch_shapes=[
             vmem(*ein.shape),
             vmem(*eout.shape),
             vmem(*ein.shape, dtype=F32),
             vmem(*eout.shape, dtype=F32),
+            *[vmem(*ins[i].shape, dtype=ins[i].dtype) for i in (0, 1, 2, 3, 6, 7, 8, 9)],
+            *[vmem(*results[i][0], dtype=results[i][1]) for i in range(5)],
             dma((2, 2 * ein.shape[0] * WIDEN)),
+            dma((8,)),
+            dma((9,)),
         ],
         compiler_params=pltpu.CompilerParams(vmem_limit_bytes=VMEM_BYTES),
         name="widen_gradients",

time: 186 us -> 181 us (0.973)
  Pallas kernels: 183 us -> 177 us
    pallas_call x1, Pallas kernels: 176 us -> 171 us  [fast_device(): pl.pallas_call(functools.partial(block_kernel, nc, nz), out_shape=[jax.Sh...]
where the time goes in v7:
time: 181 us; the launch traced here: 178 us
  Pallas kernels  177 us (98%)
    pallas_call x1, Pallas kernels, fast_device(): pl.pallas_call(functools.partial(block_kernel, nc, nz), out_shape=[jax.Sh...  171 us
    pallas_call x1, Pallas kernels, fast_device(): pl.pallas_call(functools.partial(finish_kernel, nc), out_shape=[jax.Shape...  6.28 us

profile of v7, /device:TPU:31, one launch (start us, length us, event | category | flops | bytes accessed | tf_op | source)
XLA Modules:
  0.0 178.3 jit_solution(10759758579142645541)
XLA Ops:
  0.6 171.2 %block_forward_backward.1 = (bf16[2,64,768]{2,1,0:T(8,128)(2,1)}, f32[2,64,768]{2,1,0:T(8,128)}, bf16[4,24,640]{2,1,0:T(8,128)(2,1)}, bf16[4,24,1024]{2,1,0:T(8,...) custom-call(s32[2]{0:T(128)} %len_ref.1, ...), custom_call_target="tpu_custom_call" | custom-call | flops 16000000000 | bytes 30000000 | tf_op jit(solution)/shard_map/block_forward_backward/pallas_call | solution.py:1655
  171.9 6.3 %widen_gradients.1 = (f32[24,2304]{1,0:T(8,128)}, f32[16,24]{1,0:T(8,128)}, f32[1,24]{1,0:T(1,128)}, f32[1,24]{1,0:T(1,128)}, f32[24,4096]{1,0:T(8,128)}, /*inde...) custom-call(bf16[4,24,640]{2,1,0:T(8,128)(2,1)} %get-tuple-element.3, ...), custom_call_target="tpu_custom_call" | custom-call | tf_op jit(solution)/shard_map/widen_gradients/pallas_call | solution.py:1764

commit v8 on v7

--- a/solution.py
+++ b/solution.py
@@ -417,10 +417,10 @@
 BOX = 40
 SMALL = 64
 VMEM_BYTES = 63 * 1024 * 1024
-PUMPS = (3, 6, 6, 0, 6, 6)
+PUMPS = (3, 10, 12, 0, 4, 4)
 POSTS = 64
 EARLY = 2
-LATE = 1
+LATE = 0
 WIDEN = 1
 
 
@@ -618,7 +618,7 @@
     ids_ref, rank_ref, wqkv_ref, router_ref, ga_ref, gf_ref, hid_ref, gu_ref, wo_ref, sd_ref, go_ref,
     out_ref, gin_ref, fsd_ref, fwo_ref,
     turn_ref, meta_own, meta_all, picks, hot_x, hot_d, dg_send, dg_in, hid_all, up_own, up_all, wq_own, wq_st, wq_buf, w_ref, gu_st, gu_buf, gu_all, wo_st, wo_buf,
-    wo_all, sd_all, wie, woe, normed_ref, qkv_ref, ctx_all, att_own, nt_all,
+    wo_all, sd_all, wie, woe, normed_ref, qkv_ref, probs_all, ctx_all, att_own, nt_all,
     sb, ar, xs, ds, acc_a, acc_b, sh_own, sh_hidden, sh_dm, sh_send, sh_in, sh_mid, sh_end,
     ex_hidden, ex_dm, pin, fb, rb, gsd, da_own, dctx_send, dctx_all, part, part_own, rs_in, rs_mid, rs_end,
     sib_gu, zi_gu, pb_gu, sib_q, zi_q, pb_q, sib_sd, zi_sd, sib_wo, zi_wo, pb_wo, in_wo,
@@ -1067,7 +1067,7 @@
             for g in range(2)
             for side in range(2)
         ]
-        return moves + [functools.partial(send_home_out, j)]
+        return moves
 
     home = []
     home_in = mail.open(gwi.at[pl.ds(0, remote_rows)])
@@ -1116,7 +1116,9 @@
     acc_a[...] = jnp.zeros(acc_a.shape, F32)
     acc_b[...] = jnp.zeros(acc_b.shape, F32)
     early = [move for j in range(EARLY) for move in homeward(j)]
+    early += [functools.partial(send_home_out, j) for j in range(EARLY)]
     home = [move for j in range(EARLY, steps) for move in homeward(j)]
+    home += [functools.partial(send_home_out, j) for j in range(EARLY, steps)]
     late_gate_up = mail.open(gu_buf.at[:, planes, 0, :, pl.ds(0, own_units)])
     spread_sd = mail.open(sd_all.at[planes, 0])
     spread_gu.append(late_gate_up)
@@ -1221,6 +1223,19 @@
         sibling_gu = mail.post(sib_gu, [(ggu.at[:, :, 1 - f], sib_gu, sibling)])
         sibling_sd = mail.post(sib_sd, [(gsd.at[:, 1 - f], sib_sd, sibling)])
 
+    with jax.named_scope("c_probs"):
+        def probs_of(q, carry):
+            allowed = allowed_keys(len_ref[q], half_len, full_len)
+            merged = qkv_ref[q]
+            for h in range(heads_here):
+                probs_all[q, h] = head_probs(
+                    merged[:, h * HS : (h + 1) * HS],
+                    merged[:, head_width + h * HS : head_width + (h + 1) * HS],
+                    allowed,
+                )
+            return carry
+
+        lax.fori_loop(0, num_seqs, probs_of, 0)
     with jax.named_scope("c_wait_returns"):
         returns.wait_recv()
     with jax.named_scope("c_column_mixture"):
@@ -1395,11 +1410,10 @@
         pb_gu[...] = column_sum(sib_gu[:, z], gu_copies, zi_gu).astype(BF)
         final_gu = hand_out(pb_gu, fgu_ref)
     grad_qkv = jnp.zeros((width, 3 * head_width), F32)
-    rs_first = mail.open(rs_in)
+    merged_grads = []
     for q in range(num_seqs):
         with jax.named_scope("c_attention"):
             d_context = dctx_all[q].reshape(full_len, head_width)
-            allowed = allowed_keys(len_ref[q], half_len, full_len)
             merged = qkv_ref[q]
             d_query, d_key, d_value = [], [], []
             for h in range(heads_here):
@@ -1407,7 +1421,7 @@
                 key = merged[:, head_width + h * HS : head_width + (h + 1) * HS]
                 value = merged[:, 2 * head_width + h * HS : 2 * head_width + (h + 1) * HS]
                 d_head = d_context[:, h * HS : (h + 1) * HS]
-                probs = head_probs(query, key, allowed)
+                probs = probs_all[q, h]
                 d_probs = mm_nt(d_head, value)
                 delta = jnp.sum(probs * d_probs, axis=1, keepdims=True)
                 d_scores = (probs * (d_probs - delta)).astype(BF)
@@ -1417,13 +1431,8 @@
             both = jnp.concatenate(d_query + d_key, axis=1)
             both = both * cosines - swap_halves(both) * sines
             d_merged = jnp.concatenate([both] + d_value, axis=1).astype(BF)
-            product = mm_nt(d_merged, w_ref[:, : 3 * head_width]).reshape(nc, shard_len, width)
-            part_own[q] = product
-            part[q] = product.astype(BF)
-            for at, chip in enumerate((near_x if q == 0 else near_y, far)):
-                rs_first.add(part.at[q, chip], rs_in.at[q, at], to_x if q == 0 else to_y)
+            merged_grads.append(d_merged)
             grad_qkv = grad_qkv + mm_tn(normed_ref[q], d_merged)
-    pump(home, len(home))
     mail.settle([spread_wq, passed_wq])
     gq = wq_buf
     with jax.named_scope("c_reduce_q"):
@@ -1432,6 +1441,17 @@
             jnp.concatenate([grad_qkv[:, :tail_at], last], axis=1).reshape(gq.shape).astype(BF)
         )
         sibling_q = mail.post(sib_q, [(gq.at[:, :, 1 - f], sib_q, sibling)])
+    with jax.named_scope("c_d_normed"):
+        rs_first = mail.open(rs_in)
+        for q in range(num_seqs):
+            d_merged = merged_grads[q]
+            product = mm_nt(d_merged, w_ref[:, : 3 * head_width]).reshape(nc, shard_len, width)
+            part_own[q] = product
+            part[q] = product.astype(BF)
+            for at, chip in enumerate((near_x if q == 0 else near_y, far)):
+                rs_first.add(part.at[q, chip], rs_in.at[q, at], to_x if q == 0 else to_y)
+    pump(home, len(home))
+    with jax.named_scope("c_reduce_q"):
         four_planes(sibling_q, gq, sib_q)
         q_copies = mail.post(
             zi_q,
@@ -1688,6 +1708,7 @@
             vmem(half_units, width),
             vmem(num_seqs, full_len, width),
             vmem(num_seqs, full_len, 3 * head_width),
+            vmem(num_seqs, head_width // HS, full_len, full_len, dtype=F32),
             vmem(nc, num_seqs, nc, shard_len, head_width),
             vmem(*seq_shape, dtype=F32),
             vmem(*group_shape),

time: 181 us -> 177 us (0.978)
  Pallas kernels: 177 us -> 174 us
    pallas_call x1, Pallas kernels: 171 us -> 168 us  [fast_device(): pl.pallas_call(functools.partial(block_kernel, nc, nz), out_shape=[jax.Sh...]
where the time goes in v8:
time: 177 us; the launch traced here: 175 us
  Pallas kernels  174 us (98%)
    pallas_call x1, Pallas kernels, fast_device(): pl.pallas_call(functools.partial(block_kernel, nc, nz), out_shape=[jax.Sh...  168 us
    pallas_call x1, Pallas kernels, fast_device(): pl.pallas_call(functools.partial(finish_kernel, nc), out_shape=[jax.Shape...  6.28 us

profile of v8, /device:TPU:31, one launch (start us, length us, event | category | flops | bytes accessed | tf_op | source)
XLA Modules:
  0.0 175.2 jit_solution(5605502381806853509)
XLA Ops:
  0.6 168.1 %block_forward_backward.1 = (bf16[2,64,768]{2,1,0:T(8,128)(2,1)}, f32[2,64,768]{2,1,0:T(8,128)}, bf16[4,24,640]{2,1,0:T(8,128)(2,1)}, bf16[4,24,1024]{2,1,0:T(8,...) custom-call(s32[2]{0:T(128)} %len_ref.1, ...), custom_call_target="tpu_custom_call" | custom-call | flops 16000000000 | bytes 30000000 | tf_op jit(solution)/shard_map/block_forward_backward/pallas_call | solution.py:1675
  168.7 6.3 %widen_gradients.1 = (f32[24,2304]{1,0:T(8,128)}, f32[16,24]{1,0:T(8,128)}, f32[1,24]{1,0:T(1,128)}, f32[1,24]{1,0:T(1,128)}, f32[24,4096]{1,0:T(8,128)}, /*inde...) custom-call(bf16[4,24,640]{2,1,0:T(8,128)(2,1)} %get-tuple-element.3, ...), custom_call_target="tpu_custom_call" | custom-call | tf_op jit(solution)/shard_map/widen_gradients/pallas_call | solution.py:1785

commit v9 on v8

--- a/solution.py
+++ b/solution.py
@@ -418,9 +418,10 @@
 SMALL = 64
 VMEM_BYTES = 63 * 1024 * 1024
 PUMPS = (3, 10, 12, 0, 4, 4)
-POSTS = 64
+POSTS = 55
 EARLY = 2
-LATE = 0
+LATE = -1
+SMALL_AT = 1
 WIDEN = 1
 
 
@@ -1123,6 +1124,15 @@
     spread_sd = mail.open(sd_all.at[planes, 0])
     spread_gu.append(late_gate_up)
 
+    def send_late():
+        at = pl.ds(own_units, own_units)
+        for peer in in_column:
+            late_gate_up.add(gu_st.at[:, :, at], gu_buf.at[:, z, f, :, at], peer)
+            spread_sd.add(sd_ref, sd_all.at[z, f], peer)
+
+    if LATE < 0:
+        send_late()
+
     def expert_block(j, carry):
         with jax.named_scope("b_wait_experts"):
             own_in(j).wait()
@@ -1145,10 +1155,7 @@
 
         @pl.when(j == LATE)
         def _():
-            at = pl.ds(own_units, own_units)
-            for peer in in_column:
-                late_gate_up.add(gu_st.at[:, :, at], gu_buf.at[:, z, f, :, at], peer)
-                spread_sd.add(sd_ref, sd_all.at[z, f], peer)
+            send_late()
 
         return carry
 
@@ -1236,6 +1243,18 @@
             return carry
 
         lax.fori_loop(0, num_seqs, probs_of, 0)
+    with jax.named_scope("b_reduce_shared"):
+        def two_cores(copy, own, inbox):
+            copy.wait_recv()
+            inbox[...] = (own.astype(F32) + inbox[...].astype(F32)).astype(BF)
+
+        def four_planes(copy, buffer, inbox):
+            copy.wait_recv()
+            for i in range(nc):
+                inbox[i] = (buffer[i, :, f].astype(F32) + inbox[i].astype(F32)).astype(BF)
+
+        four_planes(sibling_gu, ggu, sib_gu)
+        two_cores(sibling_sd, gsd[:, f], sib_sd)
     with jax.named_scope("c_wait_returns"):
         returns.wait_recv()
     with jax.named_scope("c_column_mixture"):
@@ -1285,18 +1304,7 @@
     dg_in[c] = dg_send[c]
     pump(home, PUMPS[4])
 
-    with jax.named_scope("b_reduce_shared"):
-        def two_cores(copy, own, inbox):
-            copy.wait_recv()
-            inbox[...] = (own.astype(F32) + inbox[...].astype(F32)).astype(BF)
-
-        def four_planes(copy, buffer, inbox):
-            copy.wait_recv()
-            for i in range(nc):
-                inbox[i] = (buffer[i, :, f].astype(F32) + inbox[i].astype(F32)).astype(BF)
-
-        four_planes(sibling_gu, ggu, sib_gu)
-        two_cores(sibling_sd, gsd[:, f], sib_sd)
+    with jax.named_scope("c_reduce_column"):
         gu_copies = mail.post(
             zi_gu,
             [
@@ -1308,7 +1316,6 @@
             zi_sd,
             [(sib_sd.at[to[1]], zi_sd.at[up - 1], to) for to, up in zip(in_column, steps_up)],
         )
-
     with jax.named_scope("c_second_sum"):
         shared_first.wait_recv()
         for k in range(2):
@@ -1550,7 +1557,7 @@
     for i, (at, source, narrow, _, _) in enumerate(pieces):
         arriving.append(pltpu.make_async_copy(source.at[at], narrow.at[at], sems.at[0, i]))
         arriving[-1].start()
-        if i == 1:
+        if i == SMALL_AT:
             for load in loads:
                 load.start()
     stores = []

time: 177 us -> 177 us (level)
  no operation moved by 1% of the time
where the time goes in v9:
time: 177 us; the launch traced here: 175 us
  Pallas kernels  174 us (98%)
    pallas_call x1, Pallas kernels, fast_device(): pl.pallas_call(functools.partial(block_kernel, nc, nz), out_shape=[jax.Sh...  168 us
    pallas_call x1, Pallas kernels, fast_device(): pl.pallas_call(functools.partial(finish_kernel, nc), out_shape=[jax.Shape...  6.28 us

profile of v9, /device:TPU:31, one launch (start us, length us, event | category | flops | bytes accessed | tf_op | source)
XLA Modules:
  0.0 174.7 jit_solution(15766999990544148907)
XLA Ops:
  0.6 167.6 %block_forward_backward.1 = (bf16[2,64,768]{2,1,0:T(8,128)(2,1)}, f32[2,64,768]{2,1,0:T(8,128)}, bf16[4,24,640]{2,1,0:T(8,128)(2,1)}, bf16[4,24,1024]{2,1,0:T(8,...) custom-call(s32[2]{0:T(128)} %len_ref.1, ...), custom_call_target="tpu_custom_call" | custom-call | flops 16000000000 | bytes 30000000 | tf_op jit(solution)/shard_map/block_forward_backward/pallas_call | solution.py:1682
  168.2 6.3 %widen_gradients.1 = (f32[24,2304]{1,0:T(8,128)}, f32[16,24]{1,0:T(8,128)}, f32[1,24]{1,0:T(1,128)}, f32[1,24]{1,0:T(1,128)}, f32[24,4096]{1,0:T(8,128)}, /*inde...) custom-call(bf16[4,24,640]{2,1,0:T(8,128)(2,1)} %get-tuple-element.3, ...), custom_call_target="tpu_custom_call" | custom-call | tf_op jit(solution)/shard_map/widen_gradients/pallas_call | solution.py:1792
